TPU v7x, 32 devices: a whole 2x2x4 slice. The times are simulated.
32 devices in a mesh: dp: 4 (over y, x), col: 8 (over z, core).
Axes of the slice: x: 2, y: 2, z: 4, core: 2. Of those that a mesh axis runs over, the one named last changes fastest.
Arguments:
- inputs: bfloat16 [32, 768, 960], P(('dp', 'col')), may hold values from -6 to 6
- segment_ids: int32 [32, 768], P(('dp', 'col')), may hold values from 0 to 3, never falling along the last dimension, each value on 1 to 384 neighbouring positions
- cotangent: bfloat16 [32, 768, 960], P(('dp', 'col')), may hold values from -6 to 6
- attn_gain: bfloat16 [2, 960], replicated, may hold values from 0.5 to 1.5
- query_weight: bfloat16 [2, 960, 960], P(None, None, 'col'), may hold values from -0.1875 to 0.1875
- key_value_weight: bfloat16 [2, 960, 640], P(None, None, 'col'), may hold values from -0.1875 to 0.1875
- output_weight: bfloat16 [2, 960, 960], P(None, 'col'), may hold values from -0.75 to 0.75
- ffn_gain: bfloat16 [2, 960], replicated, may hold values from 0.5 to 1.5
- gate_weight: bfloat16 [2, 960, 2560], P(None, None, 'col'), may hold values from -0.1875 to 0.1875
- upward_weight: bfloat16 [2, 960, 2560], P(None, None, 'col'), may hold values from -0.1875 to 0.1875
- down_weight: bfloat16 [2, 2560, 960], P(None, 'col'), may hold values from -0.125 to 0.125
Outputs:
- final: bfloat16 [32, 768, 960], P(('dp', 'col'))
- input_grad: float32 [32, 768, 960], P(('dp', 'col'))
- attn_gain_grad: float32 [2, 960], replicated
- query_grad: float32 [2, 960, 960], P(None, None, 'col')
- keyval_grad: float32 [2, 960, 640], P(None, None, 'col')
- output_grad: float32 [2, 960, 960], P(None, 'col')
- ffn_gain_grad: float32 [2, 960], replicated
- gate_grad: float32 [2, 960, 2560], P(None, None, 'col')
- upward_grad: float32 [2, 960, 2560], P(None, None, 'col')
- down_grad: float32 [2, 2560, 960], P(None, 'col')
Inputs may be any that keep to these rules, and one draw needn't show every extreme that they name: `segment_ids`: within each sequence of 768 tokens the segment numbers never fall, and each segment holds at most 384 tokens.
All inputs are finite; a program needn't handle non-finite values.
Results may differ from a plain program's by a relative error of at most 0.025.
Values may be sent and summed in bfloat16 or wider, within the bound.
No kernel may reach another device: no remote copies, remote signals or barrier semaphores. Data moves between devices by JAX's collectives and lax.ppermute only.
A program may use at most 384 MiB of HBM per device.

v0:
```python
import math

import jax
import jax.numpy as jnp
from jax import lax
from jax.sharding import PartitionSpec as P

QUERY_HEADS = 15
KEY_VALUE_HEADS = 5
HEAD_WIDTH = 64


epsilon = 1e-05
theta_base = 10000.0


def rms_norm(value_rows, gain):
    return (
        value_rows
        * lax.rsqrt(jnp.mean(value_rows * value_rows, axis=-1, keepdims=True) + epsilon)
        * gain
    )


def apply_rotary(value_rows, cosine_table, sine_table):
    half = value_rows.shape[-1] // 2
    first = value_rows[..., :half]
    second = value_rows[..., half:]
    return jnp.concatenate(
        [first * cosine_table - second * sine_table, second * cosine_table + first * sine_table],
        axis=-1,
    )


def inverse_rotary(grads, cosine_table, sine_table):
    half = grads.shape[-1] // 2
    first = grads[..., :half]
    second = grads[..., half:]
    return jnp.concatenate(
        [first * cosine_table + second * sine_table, second * cosine_table - first * sine_table],
        axis=-1,
    )


def swiglu(gate, upward):
    return jax.nn.silu(gate) * upward


def tables(segments, head_size):
    sequence_length = segments.shape[0]
    rows = jnp.arange(sequence_length, dtype=jnp.int32)
    before = jnp.sum((segments[None, :] < segments[:, None]).astype(jnp.int32), axis=1)
    places = (rows - before).astype(jnp.float32)
    half = head_size // 2
    freqs = jnp.exp(-math.log(theta_base) * (2.0 * jnp.arange(half, dtype=jnp.float32) / head_size))
    angles = places[:, None] * freqs[None, :]
    permitted_mask = (rows[None, :] <= rows[:, None]) & (segments[None, :] == segments[:, None])
    return (permitted_mask, jnp.cos(angles)[:, None, :], jnp.sin(angles)[:, None, :])


def contract_rows(left, right):
    return lax.dot_general(
        left, right, (((0,), (0,)), ((), ())), preferred_element_type=jnp.float32
    )


def contract_cols(left, right):
    return lax.dot_general(
        left, right, (((1,), (1,)), ((), ())), preferred_element_type=jnp.float32
    )


def scores(query_grouped, keys, permitted_mask):
    raw = jnp.einsum(
        "qkgd,ckd->kgqc", query_grouped, keys, preferred_element_type=jnp.float32
    ) * HEAD_WIDTH ** (-0.5)
    return jnp.where(permitted_mask[None, None], raw, -1e30)


def forward_layer(hidden_in, full, attn_g, ffn_g, permitted_mask, cosine_table, sine_table):
    query_full, keyval_full, output_full, gate_full, upward_full, down_full = full
    sequence_length = hidden_in.shape[0]
    feature_width = KEY_VALUE_HEADS * HEAD_WIDTH
    normed = rms_norm(hidden_in, attn_g).astype(jnp.bfloat16)
    query = jnp.dot(normed, query_full, preferred_element_type=jnp.float32)
    key_value_rows = jnp.dot(normed, keyval_full, preferred_element_type=jnp.float32)
    rotated_queries = apply_rotary(
        query.reshape(sequence_length, QUERY_HEADS, HEAD_WIDTH), cosine_table, sine_table
    ).astype(jnp.bfloat16)
    rotated_keys = apply_rotary(
        key_value_rows[:, :feature_width].reshape(sequence_length, KEY_VALUE_HEADS, HEAD_WIDTH),
        cosine_table,
        sine_table,
    ).astype(jnp.bfloat16)
    value_rows = (
        key_value_rows[:, feature_width:]
        .reshape(sequence_length, KEY_VALUE_HEADS, HEAD_WIDTH)
        .astype(jnp.bfloat16)
    )
    query_grouped = rotated_queries.reshape(
        sequence_length, KEY_VALUE_HEADS, QUERY_HEADS // KEY_VALUE_HEADS, HEAD_WIDTH
    )
    logits = scores(query_grouped, rotated_keys, permitted_mask)
    peak = jnp.max(logits, axis=-1, keepdims=True)
    expo = jnp.exp(logits - peak)
    total = jnp.sum(expo, axis=-1, keepdims=True)
    logsum = peak + jnp.log(total)
    probs = (expo / total).astype(jnp.bfloat16)
    attended_values = jnp.einsum(
        "kgqc,ckd->qkgd", probs, value_rows, preferred_element_type=jnp.float32
    )
    attended_values = attended_values.reshape(sequence_length, QUERY_HEADS * HEAD_WIDTH).astype(
        jnp.bfloat16
    )
    middle = hidden_in + jnp.dot(attended_values, output_full, preferred_element_type=jnp.float32)
    normed2 = rms_norm(middle, ffn_g).astype(jnp.bfloat16)
    gate = jnp.dot(normed2, gate_full, preferred_element_type=jnp.float32)
    upward = jnp.dot(normed2, upward_full, preferred_element_type=jnp.float32)
    active = swiglu(gate, upward).astype(jnp.bfloat16)
    result = middle + jnp.dot(active, down_full, preferred_element_type=jnp.float32)
    kept = (
        hidden_in,
        normed,
        rotated_queries,
        rotated_keys,
        value_rows,
        attended_values,
        logsum,
        middle,
        normed2,
        gate,
        upward,
        active,
    )
    return (result, kept)


def backward_layer(grad_out, kept, full, attn_g, ffn_g, permitted_mask, cosine_table, sine_table):
    (
        hidden_in,
        normed,
        rotated_queries,
        rotated_keys,
        value_rows,
        attended_values,
        logsum,
        middle,
        normed2,
        gate,
        upward,
        active,
    ) = kept
    query_full, keyval_full, output_full, gate_full, upward_full, down_full = full
    sequence_length = hidden_in.shape[0]
    scale = HEAD_WIDTH ** (-0.5)
    grad_low = grad_out.astype(jnp.bfloat16)
    down_grad = contract_rows(active, grad_low)
    grad_active = contract_cols(grad_low, down_full)
    unused, pull = jax.vjp(swiglu, gate, upward)
    grad_gate, grad_upward = pull(grad_active)
    grad_gate = grad_gate.astype(jnp.bfloat16)
    grad_upward = grad_upward.astype(jnp.bfloat16)
    gate_grad = contract_rows(normed2, grad_gate)
    upward_grad = contract_rows(normed2, grad_upward)
    grad_normed2 = contract_cols(grad_gate, gate_full) + contract_cols(grad_upward, upward_full)
    unused, pull = jax.vjp(rms_norm, middle, ffn_g)
    grad_mid_part, ffn_gain_grad = pull(grad_normed2)
    grad_middle = grad_out + grad_mid_part
    grad_mid_low = grad_middle.astype(jnp.bfloat16)
    output_grad = contract_rows(attended_values, grad_mid_low)
    attention_gradient = contract_cols(grad_mid_low, output_full).astype(jnp.bfloat16)
    attention_gradient = attention_gradient.reshape(
        sequence_length, KEY_VALUE_HEADS, QUERY_HEADS // KEY_VALUE_HEADS, HEAD_WIDTH
    )
    query_grouped = rotated_queries.reshape(
        sequence_length, KEY_VALUE_HEADS, QUERY_HEADS // KEY_VALUE_HEADS, HEAD_WIDTH
    )
    logits = scores(query_grouped, rotated_keys, permitted_mask)
    probs = jnp.exp(logits - logsum)
    probs_low = probs.astype(jnp.bfloat16)
    value_gradient = jnp.einsum(
        "kgqc,qkgd->ckd", probs_low, attention_gradient, preferred_element_type=jnp.float32
    )
    grad_probs = jnp.einsum(
        "qkgd,ckd->kgqc", attention_gradient, value_rows, preferred_element_type=jnp.float32
    )
    inner = jnp.sum(probs * grad_probs, axis=-1, keepdims=True)
    grad_logits = (probs * (grad_probs - inner)).astype(jnp.bfloat16)
    grad_qrot = (
        jnp.einsum("kgqc,ckd->qkgd", grad_logits, rotated_keys, preferred_element_type=jnp.float32)
        * scale
    )
    rotated_key_gradient = (
        jnp.einsum("kgqc,qkgd->ckd", grad_logits, query_grouped, preferred_element_type=jnp.float32)
        * scale
    )
    grad_query = (
        inverse_rotary(
            grad_qrot.reshape(sequence_length, QUERY_HEADS, HEAD_WIDTH), cosine_table, sine_table
        )
        .reshape(sequence_length, QUERY_HEADS * HEAD_WIDTH)
        .astype(jnp.bfloat16)
    )
    key_gradient = inverse_rotary(rotated_key_gradient, cosine_table, sine_table).reshape(
        sequence_length, KEY_VALUE_HEADS * HEAD_WIDTH
    )
    grad_keyval = jnp.concatenate(
        [key_gradient, value_gradient.reshape(sequence_length, KEY_VALUE_HEADS * HEAD_WIDTH)],
        axis=1,
    ).astype(jnp.bfloat16)
    query_grad = contract_rows(normed, grad_query)
    keyval_grad = contract_rows(normed, grad_keyval)
    grad_normed = contract_cols(grad_query, query_full) + contract_cols(grad_keyval, keyval_full)
    unused, pull = jax.vjp(rms_norm, hidden_in, attn_g)
    grad_in_part, attn_gain_grad = pull(grad_normed)
    grad_in = grad_middle + grad_in_part
    weight_grads = (query_grad, keyval_grad, output_grad, gate_grad, upward_grad, down_grad)
    return (grad_in, weight_grads, (attn_gain_grad, ffn_gain_grad))


def per_device(
    inputs,
    segment_ids,
    cotangent,
    attn_gain,
    query_weight,
    key_value_weight,
    output_weight,
    ffn_gain,
    gate_weight,
    upward_weight,
    down_weight,
):
    layers = attn_gain.shape[0]
    permitted_mask, cosine_table, sine_table = tables(segment_ids[0], HEAD_WIDTH)
    attn_gains = attn_gain.astype(jnp.float32)
    ffn_gains = ffn_gain.astype(jnp.float32)
    hidden = inputs[0].astype(jnp.float32)
    saved = []
    fulls = []
    for layer in range(layers):
        full = (
            lax.all_gather(query_weight[layer], "col", axis=1, tiled=True),
            lax.all_gather(key_value_weight[layer], "col", axis=1, tiled=True),
            lax.all_gather(output_weight[layer], "col", axis=0, tiled=True),
            lax.all_gather(gate_weight[layer], "col", axis=1, tiled=True),
            lax.all_gather(upward_weight[layer], "col", axis=1, tiled=True),
            lax.all_gather(down_weight[layer], "col", axis=0, tiled=True),
        )
        hidden, kept = forward_layer(
            hidden,
            full,
            attn_gains[layer],
            ffn_gains[layer],
            permitted_mask,
            cosine_table,
            sine_table,
        )
        saved.append(kept)
        fulls.append(full)
    final = hidden.astype(jnp.bfloat16)[None]
    grad = cotangent[0].astype(jnp.float32)
    shard_grads = [None] * layers
    gain_terms = [None] * layers
    for layer in reversed(range(layers)):
        full = (
            lax.all_gather(query_weight[layer], "col", axis=1, tiled=True),
            lax.all_gather(key_value_weight[layer], "col", axis=1, tiled=True),
            lax.all_gather(output_weight[layer], "col", axis=0, tiled=True),
            lax.all_gather(gate_weight[layer], "col", axis=1, tiled=True),
            lax.all_gather(upward_weight[layer], "col", axis=1, tiled=True),
            lax.all_gather(down_weight[layer], "col", axis=0, tiled=True),
        )
        grad, weight_grads, gain_grads = backward_layer(
            grad,
            saved[layer],
            full,
            attn_gains[layer],
            ffn_gains[layer],
            permitted_mask,
            cosine_table,
            sine_table,
        )
        query_grad, keyval_grad, output_grad, gate_grad, upward_grad, down_grad = weight_grads
        shard_grads[layer] = (
            lax.psum_scatter(
                query_grad.astype(jnp.bfloat16), "col", scatter_dimension=1, tiled=True
            ).astype(jnp.float32),
            lax.psum_scatter(
                keyval_grad.astype(jnp.bfloat16), "col", scatter_dimension=1, tiled=True
            ).astype(jnp.float32),
            lax.psum_scatter(
                output_grad.astype(jnp.bfloat16), "col", scatter_dimension=0, tiled=True
            ).astype(jnp.float32),
            lax.psum_scatter(
                gate_grad.astype(jnp.bfloat16), "col", scatter_dimension=1, tiled=True
            ).astype(jnp.float32),
            lax.psum_scatter(
                upward_grad.astype(jnp.bfloat16), "col", scatter_dimension=1, tiled=True
            ).astype(jnp.float32),
            lax.psum_scatter(
                down_grad.astype(jnp.bfloat16), "col", scatter_dimension=0, tiled=True
            ).astype(jnp.float32),
        )
        gain_terms[layer] = gain_grads
    stacked = tuple(
        (jnp.stack([shard_grads[layer][index] for layer in range(layers)]) for index in range(6))
    )
    summed = (
        lax.psum(stacked[0].astype(jnp.bfloat16), "dp").astype(jnp.float32),
        lax.psum(stacked[1].astype(jnp.bfloat16), "dp").astype(jnp.float32),
        lax.psum(stacked[2].astype(jnp.bfloat16), "dp").astype(jnp.float32),
        lax.psum(stacked[3].astype(jnp.bfloat16), "dp").astype(jnp.float32),
        lax.psum(stacked[4].astype(jnp.bfloat16), "dp").astype(jnp.float32),
        lax.psum(stacked[5].astype(jnp.bfloat16), "dp").astype(jnp.float32),
    )
    attn_terms = jnp.stack([gain_terms[layer][0] for layer in range(layers)])
    ffn_terms = jnp.stack([gain_terms[layer][1] for layer in range(layers)])
    attn_total, ffn_total = lax.psum((attn_terms, ffn_terms), ("dp", "col"))
    return (
        final,
        grad[None],
        attn_total,
        summed[0],
        summed[1],
        summed[2],
        ffn_total,
        summed[3],
        summed[4],
        summed[5],
    )


def solution(mesh):
    placed = (
        P(("dp", "col"), None, None),
        P(("dp", "col"), None),
        P(("dp", "col"), None, None),
        P(),
        P(None, None, "col"),
        P(None, None, "col"),
        P(None, "col", None),
        P(),
        P(None, None, "col"),
        P(None, None, "col"),
        P(None, "col", None),
    )
    return jax.shard_map(
        per_device,
        mesh=mesh,
        in_specs=placed,
        out_specs=(
            P(("dp", "col"), None, None),
            P(("dp", "col"), None, None),
            P(),
            P(None, None, "col"),
            P(None, None, "col"),
            P(None, "col", None),
            P(),
            P(None, None, "col"),
            P(None, None, "col"),
            P(None, "col", None),
        ),
        check_vma=False,
    )
```

profile of v0, /device:TPU:0, one launch (start us, length us, event | category | flops | bytes accessed | tf_op | source)
XLA Modules:
  0.0 1521.6 jit_solution(7364833467687791327)
XLA Ops:
  38.8 43.6 %all-gather.27.cloned.1.call-done = bf16[1,960,960]{1,0,2:T(2,128)(2,1)} async-done(((bf16[1,960,120]{1,0,2:T(2,128)(2,1)}), bf16[1,960,960]{1,0,2:T(2,128)(2,1)}) %all-gather.27.cloned.1.call-update) | async-done | bytes 1843216 | tf_op jit(solution)/shard_map/all_gather | solution.py:243
  118.7 17.6 %fusion.102 = bf16[5,64,3,768]{3,1,2,0:T(8,128)(2,1)} fusion(bf16[768,5,64,1]{0,2,3,1:T(8,128)(2,1)S(1)} %bitcast.379, f32[5,3,768]{2,1,0:T(4,128)S(1)} %fusion.6, f32[5,3,768]{2,1,0:T(4,128)S(1)} %get-tuple-element.65, f32[5,768,768,3]{2,1,3,0:T(8,128)} %get-tuple-element.66, pred[768,768]{0,1:T(8,128)(4,1)S(1)} %fusion.70), kind=kOutput, calls=%fused_computation.142 | convolution fusion | flops 1177436160 | bytes 38037504 | tf_op jit(solution)/shard_map/kgqc,ckd->qkgd/dot_general | solution.py:109
  168.4 46.4 %all-gather.31.cloned.1.call-done = bf16[1,960,2560]{1,2,0:T(8,128)(2,1)} async-done(((bf16[1,960,320]{1,2,0:T(8,128)(2,1)}), bf16[1,960,2560]{1,2,0:T(8,128)(2,1)}) %all-gather.31.cloned.1.call-update) | async-done | bytes 4915216 | tf_op jit(solution)/shard_map/all_gather | solution.py:246
  223.8 47.9 %all-gather.33.cloned.1.call-done = bf16[1,960,2560]{1,2,0:T(8,128)(2,1)} async-done(((bf16[1,960,320]{1,2,0:T(8,128)(2,1)}), bf16[1,960,2560]{1,2,0:T(8,128)(2,1)}) %all-gather.33.cloned.1.call-update) | async-done | bytes 4915216 | tf_op jit(solution)/shard_map/all_gather | solution.py:247
  283.5 45.3 %all-gather.35.cloned.1.call-done = bf16[1,2560,960]{2,1,0:T(8,128)(2,1)} async-done(((bf16[1,320,960]{2,1,0:T(8,128)(2,1)}), bf16[1,2560,960]{2,1,0:T(8,128)(2,1)}) %all-gather.35.cloned.1.call-update) | async-done | bytes 4915216 | tf_op jit(solution)/shard_map/all_gather | solution.py:248
  391.3 17.1 %fusion.101 = bf16[5,64,3,768]{3,1,2,0:T(8,128)(2,1)} fusion(bf16[768,5,64,1]{0,2,3,1:T(8,128)(2,1)S(1)} %bitcast.381, f32[5,3,768]{2,1,0:T(4,128)S(1)} %fusion.7, f32[5,3,768]{2,1,0:T(4,128)S(1)} %get-tuple-element.73, f32[5,768,768,3]{2,1,3,0:T(8,128)} %get-tuple-element.74, pred[768,768]{0,1:T(8,128)(4,1)S(1)} %fusion.70), kind=kOutput, calls=%fused_computation.141 | convolution fusion | flops 1177436160 | bytes 38037504 | tf_op jit(solution)/shard_map/kgqc,ckd->qkgd/dot_general | solution.py:109
  414.3 24.7 %all-gather.47.cloned.1.call-done = bf16[1,2560,960]{2,1,0:T(8,128)(2,1)} async-done(((bf16[1,320,960]{2,1,0:T(8,128)(2,1)}), bf16[1,2560,960]{2,1,0:T(8,128)(2,1)}) %all-gather.47.cloned.1.call-update) | async-done | bytes 4915216 | tf_op jit(solution)/shard_map/all_gather | solution.py:248
  448.0 48.0 %all-gather.45.cloned.1.call-done = bf16[1,960,2560]{1,2,0:T(8,128)(2,1)} async-done(((bf16[1,960,320]{1,2,0:T(8,128)(2,1)}), bf16[1,960,2560]{1,2,0:T(8,128)(2,1)}) %all-gather.45.cloned.1.call-update) | async-done | bytes 4915216 | tf_op jit(solution)/shard_map/all_gather | solution.py:247
  505.2 47.7 %all-gather.43.cloned.1.call-done = bf16[1,960,2560]{1,2,0:T(8,128)(2,1)} async-done(((bf16[1,960,320]{1,2,0:T(8,128)(2,1)}), bf16[1,960,2560]{1,2,0:T(8,128)(2,1)}) %all-gather.43.cloned.1.call-update) | async-done | bytes 4915216 | tf_op jit(solution)/shard_map/all_gather | solution.py:246
  603.4 28.3 %fusion.3 = (f32[5,3,768]{2,1,0:T(4,128)S(1)}, f32[5,768,768,3]{2,1,3,0:T(8,128)}) fusion(f32[5,3,768]{2,1,0:T(4,128)S(1)} %copy-done.54, f32[5,768,768,3]{2,1,3,0:T(8,128)} %get-tuple-element.74, pred[768,768]{0,1:T(8,128)(4,1)S(1)} %fusion.70, bf16[768,5,64,1]{0,2,3,1:T(8,128)(2,1)S(1)} %bitcast.382, bf16[768,5,3,64]{0,3,2,1:T(8,128)(2,1)S(1)} %bitcast.389), kind=kOutput, calls=%fused_computation.7 | convolution fusion | flops 1176687360 | bytes 73426944 | tf_op jit(solution)/shard_map/qkgd,ckd->kgqc/dot_general | solution.py:184
  631.7 30.2 %fusion.5 = bf16[5,3,768,768]{2,3,1,0:T(8,128)(2,1)} fusion(f32[5,768,768,3]{2,1,3,0:T(8,128)} %get-tuple-element.79, f32[5,3,768]{2,1,0:T(4,128)S(1)} %get-tuple-element.78, f32[5,3,768]{2,1,0:T(4,128)S(1)} %copy-done.54, f32[5,768,768,3]{2,1,3,0:T(8,128)} %get-tuple-element.74, pred[768,768]{0,1:T(8,128)(4,1)S(1)} %fusion.70), kind=kLoop, calls=%fused_computation.9 | loop fusion | flops 53084160 | bytes 89155584 | tf_op jit(solution)/shard_map/convert_element_type | solution.py:188
  737.7 29.5 %fusion = (f32[5,3,768]{2,1,0:T(4,128)S(1)}, f32[5,768,768,3]{2,1,3,0:T(8,128)}) fusion(f32[5,3,768]{2,1,0:T(4,128)S(1)} %copy-done.53, f32[5,768,768,3]{2,1,3,0:T(8,128)} %get-tuple-element.66, pred[768,768]{0,1:T(8,128)(4,1)S(1)} %fusion.70, bf16[768,5,64,1]{0,2,3,1:T(8,128)(2,1)S(1)} %bitcast.380, bf16[768,5,3,64]{0,3,2,1:T(8,128)(2,1)} %bitcast.386), kind=kOutput, calls=%fused_computation.2 | convolution fusion | flops 1176687360 | bytes 73426944 | tf_op jit(solution)/shard_map/qkgd,ckd->kgqc/dot_general | solution.py:184
  767.2 29.9 %fusion.2 = bf16[5,3,768,768]{2,3,1,0:T(8,128)(2,1)} fusion(f32[5,768,768,3]{2,1,3,0:T(8,128)} %get-tuple-element.83, f32[5,3,768]{2,1,0:T(4,128)S(1)} %get-tuple-element.82, f32[5,3,768]{2,1,0:T(4,128)S(1)} %copy-done.53, f32[5,768,768,3]{2,1,3,0:T(8,128)} %get-tuple-element.66, pred[768,768]{0,1:T(8,128)(4,1)S(1)} %fusion.70), kind=kLoop, calls=%fused_computation.4 | loop fusion | flops 53084160 | bytes 89155584 | tf_op jit(solution)/shard_map/convert_element_type | solution.py:188
  812.1 16.7 %fusion.133 = bf16[5,64,768]{2,1,0:T(8,128)(2,1)} fusion(bf16[768,5,3,64]{0,3,2,1:T(8,128)(2,1)} %bitcast.387, f32[5,3,768]{2,1,0:T(4,128)} %log_add_fusion, f32[5,768,768,3]{2,1,3,0:T(8,128)} %get-tuple-element.66, pred[768,768]{0,1:T(8,128)(4,1)S(1)} %fusion.70), kind=kOutput, calls=%fused_computation.183 | convolution fusion | flops 1168097280 | bytes 37991424 | tf_op jit(solution)/shard_map/kgqc,qkgd->ckd/dot_general | solution.py:181
  939.4 35.4 %reduce-scatter.23.cloned.1.call-done = bf16[120,960]{1,0:T(8,128)(2,1)} async-done(((bf16[960,960]{1,0:T(8,128)(2,1)}), bf16[120,960]{1,0:T(8,128)(2,1)}) %reduce-scatter.23.cloned.1.call-update) | async-done | bytes 230416 | tf_op jit(solution)/shard_map/reduce_scatter | solution.py:292
  974.8 36.8 %reduce-scatter.21.cloned.1.call-done = bf16[120,960]{1,0:T(8,128)(2,1)} async-done(((bf16[960,960]{1,0:T(8,128)(2,1)}), bf16[120,960]{1,0:T(8,128)(2,1)}) %reduce-scatter.21.cloned.1.call-update) | async-done | bytes 230416 | tf_op jit(solution)/shard_map/reduce_scatter | solution.py:292
  1014.4 57.9 %reduce-scatter.35.cloned.1.call-done = bf16[320,960]{1,0:T(8,128)(2,1)} async-done(((bf16[2560,960]{1,0:T(8,128)(2,1)}), bf16[320,960]{1,0:T(8,128)(2,1)}) %reduce-scatter.35.cloned.1.call-update) | async-done | bytes 614416 | tf_op jit(solution)/shard_map/reduce_scatter | solution.py:301
  1072.2 60.4 %reduce-scatter.33.cloned.1.call-done = bf16[320,960]{1,0:T(8,128)(2,1)} async-done(((bf16[2560,960]{1,0:T(8,128)(2,1)}), bf16[320,960]{1,0:T(8,128)(2,1)}) %reduce-scatter.33.cloned.1.call-update) | async-done | bytes 614416 | tf_op jit(solution)/shard_map/reduce_scatter | solution.py:301
  1135.1 58.2 %reduce-scatter.31.cloned.1.call-done = bf16[960,320]{0,1:T(8,128)(2,1)} async-done(((bf16[960,2560]{0,1:T(8,128)(2,1)}), bf16[960,320]{0,1:T(8,128)(2,1)}) %reduce-scatter.31.cloned.1.call-update) | async-done | bytes 614416 | tf_op jit(solution)/shard_map/reduce_scatter | solution.py:298
  1193.3 60.6 %reduce-scatter.29.cloned.1.call-done = bf16[960,320]{0,1:T(8,128)(2,1)} async-done(((bf16[960,2560]{0,1:T(8,128)(2,1)}), bf16[960,320]{0,1:T(8,128)(2,1)}) %reduce-scatter.29.cloned.1.call-update) | async-done | bytes 614416 | tf_op jit(solution)/shard_map/reduce_scatter | solution.py:298
  1256.3 58.2 %reduce-scatter.27.cloned.1.call-done = bf16[960,320]{0,1:T(8,128)(2,1)} async-done(((bf16[960,2560]{0,1:T(8,128)(2,1)}), bf16[960,320]{0,1:T(8,128)(2,1)}) %reduce-scatter.27.cloned.1.call-update) | async-done | bytes 614416 | tf_op jit(solution)/shard_map/reduce_scatter | solution.py:295
  1314.5 60.5 %reduce-scatter.25.cloned.1.call-done = bf16[960,320]{0,1:T(8,128)(2,1)} async-done(((bf16[960,2560]{0,1:T(8,128)(2,1)}), bf16[960,320]{0,1:T(8,128)(2,1)}) %reduce-scatter.25.cloned.1.call-update) | async-done | bytes 614416 | tf_op jit(solution)/shard_map/reduce_scatter | solution.py:295
  1395.6 38.5 %all-reduce = (f32[2,960]{1,0:T(2,128)}, f32[2,960]{1,0:T(2,128)}) all-reduce(f32[2,960]{1,0:T(2,128)S(1)} %get-tuple-element.85, f32[2,960]{1,0:T(2,128)S(1)} %get-tuple-element.86), channel_id=1, replica_groups=mesh['dp'=4,'col'=8] {'dp','col'}, use_global_device_ids=true, to_apply=%region_17.18 | all-reduce | flops 3840 | bytes 30720 | tf_op jit(solution)/shard_map/psum | solution.py:319
  1447.0 56.2 %all-reduce.4.cloned.1.call-done = (bf16[2,960,120]{2,1,0:T(8,128)(2,1)}, bf16[2,960,80]{1,2,0:T(8,128)(2,1)}, bf16[2,120,960]{2,1,0:T(8,128)(2,1)}, bf16[2,960,...) async-done(((bf16[2,960,120]{2,1,0:T(8,128)(2,1)}, bf16[2,960,80]{1,2,0:T(8,128)(2,1)}, bf16[2,120,960]{2,1,0:T(8,128)(2,1)}, ...) | async-done | bytes 4915216 | tf_op jit(solution)/shard_map/psum | solution.py:310
  (369 shorter events, 510.3 us)
Async XLA Ops:
  9.1 73.2 %all-gather.27.cloned.1.call-start = ((), (), s32[]{:S(2)}) async-start(), calls=%async_computation.23 | async-start | bytes 4423680 | tf_op jit(solution)/shard_map/all_gather | solution.py:243
  11.8 124.6 %all-gather.29.cloned.1.call-start = ((), (), s32[]{:S(2)}) async-start(), calls=%async_computation.24 | async-start | bytes 2211840 | tf_op jit(solution)/shard_map/all_gather | solution.py:245
  12.6 145.2 %all-gather.39.cloned.1.call-start = ((), (), s32[]{:S(2)}) async-start(), calls=%async_computation.29 | async-start | bytes 4423680 | tf_op jit(solution)/shard_map/all_gather | solution.py:243
  14.1 200.7 %all-gather.31.cloned.1.call-start = ((), (), s32[]{:S(2)}) async-start(), calls=%async_computation.25 | async-start | bytes 5898240 | tf_op jit(solution)/shard_map/all_gather | solution.py:246
  15.4 256.4 %all-gather.33.cloned.1.call-start = ((), (), s32[]{:S(2)}) async-start(), calls=%async_computation.26 | async-start | bytes 5898240 | tf_op jit(solution)/shard_map/all_gather | solution.py:247
  16.6 312.2 %all-gather.35.cloned.1.call-start = ((), (), s32[]{:S(2)}) async-start(), calls=%async_computation.27 | async-start | bytes 5898240 | tf_op jit(solution)/shard_map/all_gather | solution.py:248
  19.2 333.4 %all-gather.37.cloned.1.call-start = ((), (), s32[]{:S(2)}) async-start(), calls=%async_computation.28 | async-start | bytes 1474560 | tf_op jit(solution)/shard_map/all_gather | solution.py:244
  20.0 388.4 %all-gather.41.cloned.1.call-start = ((), (), s32[]{:S(2)}) async-start(), calls=%async_computation.30 | async-start | bytes 2211840 | tf_op jit(solution)/shard_map/all_gather | solution.py:245
  20.7 418.2 %all-gather.47.cloned.1.call-start = ((), (), s32[]{:S(2)}) async-start(), calls=%async_computation.33 | async-start | bytes 5898240 | tf_op jit(solution)/shard_map/all_gather | solution.py:248
  21.3 474.7 %all-gather.45.cloned.1.call-start = ((), (), s32[]{:S(2)}) async-start(), calls=%async_computation.32 | async-start | bytes 5898240 | tf_op jit(solution)/shard_map/all_gather | solution.py:247
  22.0 530.9 %all-gather.43.cloned.1.call-start = ((), (), s32[]{:S(2)}) async-start(), calls=%async_computation.31 | async-start | bytes 5898240 | tf_op jit(solution)/shard_map/all_gather | solution.py:246
  22.6 904.5 %reduce-scatter.19.cloned.1.call-start = ((), (), s32[]{:S(2)}) async-start(), calls=%async_computation.13 | async-start | bytes 1474560 | tf_op jit(solution)/shard_map/reduce_scatter | solution.py:289
  730.4 196.8 %reduce-scatter.17.cloned.1.call-start = ((), (), s32[]{:S(2)}) async-start(), calls=%async_computation.12 | async-start | bytes 1474560 | tf_op jit(solution)/shard_map/reduce_scatter | solution.py:289
  832.8 96.0 %reduce-scatter.39.cloned.1.call-start = ((), (), s32[]{:S(2)}) async-start(), calls=%async_computation.35 | async-start | bytes 2211840
  841.6 96.7 %reduce-scatter.37.cloned.1.call-start = ((), (), s32[]{:S(2)}) async-start(), calls=%async_computation.34 | async-start | bytes 2211840
  859.9 115.0 %reduce-scatter.23.cloned.1.call-start = ((), (), s32[]{:S(2)}) async-start(), calls=%async_computation.15 | async-start | bytes 2211840 | tf_op jit(solution)/shard_map/reduce_scatter | solution.py:292
  865.2 146.4 %reduce-scatter.21.cloned.1.call-start = ((), (), s32[]{:S(2)}) async-start(), calls=%async_computation.14 | async-start | bytes 2211840 | tf_op jit(solution)/shard_map/reduce_scatter | solution.py:292
  869.6 202.6 %reduce-scatter.35.cloned.1.call-start = ((), (), s32[]{:S(2)}) async-start(), calls=%async_computation.21 | async-start | bytes 5898240 | tf_op jit(solution)/shard_map/reduce_scatter | solution.py:301
  879.3 253.3 %reduce-scatter.33.cloned.1.call-start = ((), (), s32[]{:S(2)}) async-start(), calls=%async_computation.20 | async-start | bytes 5898240 | tf_op jit(solution)/shard_map/reduce_scatter | solution.py:301
  889.1 304.2 %reduce-scatter.31.cloned.1.call-start = ((), (), s32[]{:S(2)}) async-start(), calls=%async_computation.19 | async-start | bytes 5898240 | tf_op jit(solution)/shard_map/reduce_scatter | solution.py:298
  898.6 355.3 %reduce-scatter.29.cloned.1.call-start = ((), (), s32[]{:S(2)}) async-start(), calls=%async_computation.18 | async-start | bytes 5898240 | tf_op jit(solution)/shard_map/reduce_scatter | solution.py:298
  907.9 406.6 %reduce-scatter.27.cloned.1.call-start = ((), (), s32[]{:S(2)}) async-start(), calls=%async_computation.17 | async-start | bytes 5898240 | tf_op jit(solution)/shard_map/reduce_scatter | solution.py:295
  917.6 457.3 %reduce-scatter.25.cloned.1.call-start = ((), (), s32[]{:S(2)}) async-start(), calls=%async_computation.16 | async-start | bytes 5898240 | tf_op jit(solution)/shard_map/reduce_scatter | solution.py:295
  926.8 576.3 %all-reduce.4.cloned.1.call-start = ((), (), s32[]{:S(2)}) async-start(), calls=%async_computation.36 | async-start | bytes 10485760 | tf_op jit(solution)/shard_map/psum | solution.py:310
  (98 other events, 1911.9 us)
Sparse Core Ops, SparseCore 0:
  9.7 26.1 all-gather.24
  38.1 44.2 all-gather.26
  84.6 26.8 all-gather.28
  113.5 44.2 all-gather.38
  159.9 54.8 all-gather.30
  216.9 54.8 all-gather.32
  273.9 54.8 all-gather.34
  354.3 27.4 all-gather.40
  383.3 55.5 all-gather.46
  441.1 54.8 all-gather.44
  498.1 54.8 all-gather.42
  730.5 32.0 reduce-scatter.18
  832.9 32.0 reduce-scatter.16
  867.8 33.6 reduce-scatter.38
  904.4 33.8 reduce-scatter.36
  941.0 33.7 reduce-scatter.22
  977.7 33.8 reduce-scatter.20
  1013.9 58.2 reduce-scatter.34
  1074.4 58.2 reduce-scatter.32
  1135.0 58.2 reduce-scatter.30
  1195.6 58.2 reduce-scatter.28
  1256.2 58.2 reduce-scatter.26
  1316.7 58.2 reduce-scatter.24
  1380.4 122.7 all-reduce.3
  (1 shorter events, 22.2 us)
where the time goes:
time: 1530 us; the launch traced here: 1520 us
  waiting for transfers between devices  838 us (55%)
  matrix products  435 us (28%)
  other arithmetic  135 us (9%)
  local copies, waits for them, and re-layouts  57.4 us (4%)
  blocking collectives  38.5 us (3%)
  between operations  15.7 us (1%)
    reduce_scatter x2, waiting for transfers between devices, per_device(): lax.psum_scatter(upward_grad.astype(jnp.bfloat16), 'col', scatter_dimensi...  119 us
    reduce_scatter x2, waiting for transfers between devices, per_device(): lax.psum_scatter(gate_grad.astype(jnp.bfloat16), 'col', scatter_dimension...  119 us
    reduce_scatter x2, waiting for transfers between devices, per_device(): lax.psum_scatter(down_grad.astype(jnp.bfloat16), 'col', scatter_dimension...  118 us
    all_gather x2, waiting for transfers between devices, per_device(): lax.all_gather(upward_weight[layer], 'col', axis=1, tiled=True)  95.9 us
    all_gather x2, waiting for transfers between devices, per_device(): lax.all_gather(gate_weight[layer], 'col', axis=1, tiled=True)  94.2 us
    dot_general x12, matrix products, contract_rows(): lax.dot_general(left, right, (((0,), (0,)), ((), ())), preferred_element_...  79.6 us
    dot_general x12, matrix products, contract_cols(): lax.dot_general(left, right, (((1,), (1,)), ((), ())), preferred_element_...  78.9 us
    reduce_scatter x2, waiting for transfers between devices, per_device(): lax.psum_scatter(output_grad.astype(jnp.bfloat16), 'col', scatter_dimensi...  72.2 us
  transfers between devices with their start and end apart: 25, of which 20 were waited for; matrix products, arithmetic and copies ran while one was open for 28% of the time, Pallas kernels for 0%

commit v1 on v0

v1 whole, which is shorter than its diff:
```python
import functools
import math

import jax
import jax.numpy as jnp
from jax import lax
from jax.experimental import pallas as pl
from jax.experimental.pallas import tpu as pltpu
from jax.sharding import PartitionSpec as P

QUERY_HEADS = 15
KEY_VALUE_HEADS = 5
HEAD_WIDTH = 64


epsilon = 1e-05
theta_base = 10000.0


def rms_norm(value_rows, gain):
    return (
        value_rows
        * lax.rsqrt(jnp.mean(value_rows * value_rows, axis=-1, keepdims=True) + epsilon)
        * gain
    )


def tables(segments, head_size):
    sequence_length = segments.shape[0]
    rows = jnp.arange(sequence_length, dtype=jnp.int32)
    before = jnp.sum((segments[None, :] < segments[:, None]).astype(jnp.int32), axis=1)
    places = (rows - before).astype(jnp.float32)
    half = head_size // 2
    freqs = jnp.exp(-math.log(theta_base) * (2.0 * jnp.arange(half, dtype=jnp.float32) / head_size))
    angles = places[:, None] * freqs[None, :]
    cosine, sine = jnp.cos(angles), jnp.sin(angles)
    return (jnp.tile(cosine, (1, 4)), jnp.tile(jnp.concatenate([-sine, sine], axis=1), (1, 2)))


BLOCK = 256
REACH = 384
MEGA = 2**20


def call(body, outs, args, after=(), scratch=(), limit=56, flops=0, nbytes=0, **grid):
    given = len(args)
    late = len(after)

    def run(*refs):
        body(*refs[:given], *refs[given + late :])

    specs = grid.pop("in_specs", None) or [pl.BlockSpec(memory_space=pltpu.VMEM)] * given
    out_specs = grid.pop("out_specs", None) or [pl.BlockSpec(memory_space=pltpu.VMEM)] * len(outs)
    return pl.pallas_call(
        run,
        out_shape=outs,
        in_specs=list(specs) + [pl.BlockSpec(memory_space=pl.ANY)] * late,
        out_specs=out_specs,
        scratch_shapes=list(scratch),
        compiler_params=pltpu.CompilerParams(vmem_limit_bytes=limit * MEGA),
        cost_estimate=pl.CostEstimate(flops=flops, bytes_accessed=nbytes, transcendentals=0),
        **grid,
    )(*args, *after)


def dot(left, right, dims=((1,), (0,))):
    return lax.dot_general(left, right, (dims, ((), ())), preferred_element_type=jnp.float32)


NT = ((1,), (1,))
TN = ((0,), (0,))


def swap_halves(value):
    lane = lax.broadcasted_iota(jnp.int32, value.shape, 1)
    return jnp.where(lane % HEAD_WIDTH < HEAD_WIDTH // 2, pltpu.roll(value, 96, 1), pltpu.roll(value, 32, 1))


def spans(length):
    for start in range(0, length, BLOCK):
        yield start, max(0, start - REACH + 1) // 128 * 128, start + BLOCK


def fill_bias(bias, seg_col, seg_row, length):
    for index, (start, low, high) in enumerate(spans(length)):
        shape = (high - low, BLOCK)
        key = lax.broadcasted_iota(jnp.int32, shape, 0) + low
        query = lax.broadcasted_iota(jnp.int32, shape, 1) + start
        same = seg_col[low:high, :] == seg_row[:, start : start + BLOCK]
        bias[index, : high - low, :] = jnp.where((key <= query) & same, 0.0, -1e30)


def attention_forward(raw, cosine, sine, seg_col, seg_row, after=()):
    length, width = raw.shape
    q_width = QUERY_HEADS * HEAD_WIDTH
    kv_width = KEY_VALUE_HEADS * HEAD_WIDTH
    group = QUERY_HEADS // KEY_VALUE_HEADS
    rotated = q_width + kv_width
    most = max(high - low for _, low, high in spans(length))

    def body(raw, cosine, sine, seg_col, seg_row, qkv, attended, logsum, bias, turned):
        for lane in range(0, rotated, 128):
            value = raw[:, lane : lane + 128]
            qkv[:, lane : lane + 128] = (value * cosine[...] + swap_halves(value) * sine[...]).astype(jnp.bfloat16)
        qkv[:, rotated:] = raw[:, rotated:].astype(jnp.bfloat16)
        fill_bias(bias, seg_col, seg_row, length)
        logsum[...] = jnp.zeros_like(logsum)
        turned[...] = raw[:, rotated:].T.astype(jnp.bfloat16)
        for index, (start, low, high) in enumerate(spans(length)):
            columns = []
            for head in range(QUERY_HEADS):
                kv = head // group
                query = qkv[start : start + BLOCK, head * HEAD_WIDTH : (head + 1) * HEAD_WIDTH] * 0.125
                at = q_width + kv * HEAD_WIDTH
                key = qkv[low:high, at : at + HEAD_WIDTH]
                logits = dot(key, query, NT) + bias[index, : high - low, :]
                peak = jnp.max(logits, axis=0, keepdims=True)
                expo = jnp.exp(logits - peak)
                total = jnp.sum(expo, axis=0, keepdims=True)
                value = turned[kv * HEAD_WIDTH : (kv + 1) * HEAD_WIDTH, low:high]
                columns.append(dot(value, expo.astype(jnp.bfloat16)) / total)
                logsum[head : head + 1, start : start + BLOCK] = peak + jnp.log(total)
            attended[start : start + BLOCK, :] = jnp.concatenate(columns, axis=0).T.astype(jnp.bfloat16)

    return call(
        body,
        [
            jax.ShapeDtypeStruct((length, width), jnp.bfloat16),
            jax.ShapeDtypeStruct((length, q_width), jnp.bfloat16),
            jax.ShapeDtypeStruct((16, length), jnp.float32),
        ],
        [raw, cosine, sine, seg_col, seg_row],
        after,
        [
            pltpu.VMEM((length // BLOCK, most, BLOCK), jnp.float32),
            pltpu.VMEM((kv_width, length), jnp.bfloat16),
        ],
        flops=15 * 10**9,
        nbytes=15 * MEGA,
    )


def attention_backward(qkv, grad, logsum, cosine, sine, seg_col, seg_row, after=()):
    length, width = qkv.shape
    q_width = QUERY_HEADS * HEAD_WIDTH
    kv_width = KEY_VALUE_HEADS * HEAD_WIDTH
    group = QUERY_HEADS // KEY_VALUE_HEADS
    rotated = q_width + kv_width
    most = max(high - low for _, low, high in spans(length))
    scale = 0.125

    def body(qkv, grad, logsum, cosine, sine, seg_col, seg_row, out, bias, turned, key_sum, value_sum, query_sum):
        fill_bias(bias, seg_col, seg_row, length)
        turned[...] = qkv[:, q_width:rotated].astype(jnp.float32).T.astype(jnp.bfloat16) * scale
        key_sum[...] = jnp.zeros_like(key_sum)
        value_sum[...] = jnp.zeros_like(value_sum)
        for index, (start, low, high) in enumerate(spans(length)):
            for head in range(QUERY_HEADS):
                kv = head // group
                lanes = slice(head * HEAD_WIDTH, (head + 1) * HEAD_WIDTH)
                query = qkv[start : start + BLOCK, lanes] * scale
                upstream = grad[start : start + BLOCK, lanes]
                at = q_width + kv * HEAD_WIDTH
                key = qkv[low:high, at : at + HEAD_WIDTH]
                value = qkv[low:high, at + kv_width : at + kv_width + HEAD_WIDTH]
                logits = dot(key, query, NT) + bias[index, : high - low, :]
                probs = jnp.exp(logits - logsum[head : head + 1, start : start + BLOCK])
                grad_probs = dot(value, upstream, NT)
                inner = jnp.sum(probs * grad_probs, axis=0, keepdims=True)
                grad_logits = (probs * (grad_probs - inner)).astype(jnp.bfloat16)
                value_sum[kv, low:high, :] += dot(probs.astype(jnp.bfloat16), upstream)
                key_sum[kv, low:high, :] += dot(grad_logits, query)
                query_sum[lanes, start : start + BLOCK] = dot(
                    turned[kv * HEAD_WIDTH : (kv + 1) * HEAD_WIDTH, low:high], grad_logits
                )
        raw = [query_sum[...].T] + [key_sum[kv] for kv in range(KEY_VALUE_HEADS)]
        raw = jnp.concatenate(raw, axis=1)
        for lane in range(0, rotated, 128):
            value = raw[:, lane : lane + 128]
            out[:, lane : lane + 128] = (value * cosine[...] - swap_halves(value) * sine[...]).astype(jnp.bfloat16)
        out[:, rotated:] = jnp.concatenate([value_sum[kv] for kv in range(KEY_VALUE_HEADS)], axis=1).astype(jnp.bfloat16)

    return call(
        body,
        [jax.ShapeDtypeStruct((length, width), jnp.bfloat16)],
        [qkv, grad, logsum, cosine, sine, seg_col, seg_row],
        after,
        [
            pltpu.VMEM((length // BLOCK, most, BLOCK), jnp.float32),
            pltpu.VMEM((kv_width, length), jnp.bfloat16),
            pltpu.VMEM((KEY_VALUE_HEADS, length, HEAD_WIDTH), jnp.float32),
            pltpu.VMEM((KEY_VALUE_HEADS, length, HEAD_WIDTH), jnp.float32),
            pltpu.VMEM((q_width, length), jnp.float32),
        ],
        flops=30 * 10**9,
        nbytes=20 * MEGA,
    )[0]


TILE = 256


def ffn_forward(middle, normed, here, there, after=()):
    length, width = middle.shape
    units = here[0].shape[0]
    tile = math.gcd(TILE, units)
    steps = units // tile

    def body(middle, normed, gate_a, upward_a, down_a, gate_b, upward_b, down_b, out, gate_one, up_one, gate_two, up_two):
        step = pl.program_id(0)

        @pl.when(step == 0)
        def _():
            out[...] = middle[...]

        def half(gate_w, upward_w, down_w, gate_out, upward_out):
            gate = dot(normed[...], gate_w[...], NT)
            upward = dot(normed[...], upward_w[...], NT)
            gate_out[...] = gate.astype(jnp.bfloat16)
            upward_out[...] = upward.astype(jnp.bfloat16)
            active = (gate * jax.nn.sigmoid(gate) * upward).astype(jnp.bfloat16)
            out[...] += dot(active, down_w[...])

        @pl.when(step < steps)
        def _():
            half(gate_a, upward_a, down_a, gate_one, up_one)

        @pl.when(step >= steps)
        def _():
            half(gate_b, upward_b, down_b, gate_two, up_two)

    whole = pl.BlockSpec((length, width), lambda i: (0, 0))
    weight_a = pl.BlockSpec((tile, width), lambda i: (jnp.minimum(i, steps - 1), 0))
    weight_b = pl.BlockSpec((tile, width), lambda i: (jnp.maximum(i - steps, 0), 0))
    columns_a = pl.BlockSpec((length, tile), lambda i: (0, jnp.minimum(i, steps - 1)))
    columns_b = pl.BlockSpec((length, tile), lambda i: (0, jnp.maximum(i - steps, 0)))
    low = jax.ShapeDtypeStruct((length, units), jnp.bfloat16)
    return call(
        body,
        [jax.ShapeDtypeStruct((length, width), jnp.float32), low, low, low, low],
        [middle, normed, *here, *there],
        after,
        grid=(2 * steps,),
        in_specs=[whole, whole] + [weight_a] * 3 + [weight_b] * 3,
        out_specs=[whole, columns_a, columns_a, columns_b, columns_b],
        flops=11 * 10**9,
        nbytes=20 * MEGA,
    )


def ffn_backward(grad_low, normed, gate, upward, gate_full, upward_full, down_full, earlier=None):
    length, width = normed.shape
    units = gate_full.shape[0]
    tile = math.gcd(TILE, units)

    def body(grad_low, normed, gate, upward, gate_w, upward_w, down_w, *rest):
        *before, gate_grad, upward_grad, down_grad, out = rest

        @pl.when(pl.program_id(0) == 0)
        def _():
            out[...] = before[0][...] if before else jnp.zeros_like(out)

        grad_active = dot(grad_low[...], down_w[...], NT)
        gate_value = gate[...].astype(jnp.float32)
        up_value = upward[...].astype(jnp.float32)
        sigma = jax.nn.sigmoid(gate_value)
        silu = gate_value * sigma
        down_grad[...] = dot((silu * up_value).astype(jnp.bfloat16), grad_low[...], TN).astype(jnp.bfloat16)
        grad_up = (grad_active * silu).astype(jnp.bfloat16)
        grad_gate = (grad_active * up_value * (sigma + silu * (1.0 - sigma))).astype(jnp.bfloat16)
        gate_grad[...] = dot(grad_gate, normed[...], TN).astype(jnp.bfloat16)
        upward_grad[...] = dot(grad_up, normed[...], TN).astype(jnp.bfloat16)
        out[...] += dot(grad_gate, gate_w[...]) + dot(grad_up, upward_w[...])

    whole = pl.BlockSpec((length, width), lambda i: (0, 0))
    weight = pl.BlockSpec((tile, width), lambda i: (i, 0))
    columns = pl.BlockSpec((length, tile), lambda i: (0, i))
    shape = jax.ShapeDtypeStruct((units, width), jnp.bfloat16)
    before = [] if earlier is None else [earlier]
    return call(
        body,
        [shape, shape, shape, jax.ShapeDtypeStruct((length, width), jnp.float32)],
        [grad_low, normed, gate, upward, gate_full, upward_full, down_full, *before],
        grid=(units // tile,),
        in_specs=[whole, whole, columns, columns, weight, weight, weight] + [whole] * len(before),
        out_specs=[weight, weight, weight, whole],
        flops=22 * 10**9,
        nbytes=45 * MEGA,
    )


class Links:
    def __init__(self, dp, col):
        self.dp, self.col, self.line = dp, col, col // 2
        self.rest = [list(range(r, dp, 4)) for r in range(4)]
        self.quarter = lax.axis_index("dp") % 4
        self.core = lax.axis_index("col") % 2
        self.chip = lax.axis_index("col") // 2

    def x(self, value):
        return lax.ppermute(value, "dp", [(i, i ^ 1) for i in range(self.dp)])

    def y(self, value):
        return lax.ppermute(value, "dp", [(i, i ^ 2) for i in range(self.dp)])

    def other_core(self, value):
        return lax.ppermute(value, "col", [(i, i ^ 1) for i in range(self.col)])

    def send(self, value, step):
        return lax.ppermute(value, "col", [(i, (i + 2 * step) % self.col) for i in range(self.col)])

    def sum_all(self, value):
        for axis, size in (("dp", self.dp), ("col", self.col)):
            step = 1
            while step < size:
                value = value + lax.ppermute(value, axis, [(i, i ^ step) for i in range(size)])
                step *= 2
        return value


def add(*terms):
    total = terms[0].astype(jnp.float32)
    for term in terms[1:]:
        total = total + term.astype(jnp.float32)
    return total.astype(jnp.bfloat16)


class Transfer:
    def __init__(self, stages):
        self.stages = stages
        self.result = None
        self.flying = next(stages)

    def advance(self, arrays=None):
        try:
            self.flying = self.stages.send(self.flying if arrays is None else arrays)
        except StopIteration as stop:
            self.flying, self.result = [], stop.value

    def finish(self):
        while self.result is None:
            self.advance()
        return self.result


def advance(value, *transfers):
    flying = [transfer.flying for transfer in transfers]
    value, flying = lax.optimization_barrier((value, flying))
    for transfer, arrays in zip(transfers, flying, strict=True):
        transfer.advance(arrays)
    return value


def gather_stages(links, part):
    far = yield [links.send(part, -step) for step in range(1, links.line)]
    own = jnp.stack([part, *far])
    half = links.line // 2
    from_x, from_y, own_c = yield [links.x(own), links.y(own), links.other_core(own)]
    low, high, x_c, y_c = yield [
        links.y(from_x[:half]),
        links.x(from_y[half:]),
        links.other_core(from_x),
        links.other_core(from_y),
    ]
    low_c, high_c = yield [links.other_core(low), links.other_core(high)]
    return [
        [own, from_x, from_y, jnp.concatenate([low, high])],
        [own_c, x_c, y_c, jnp.concatenate([low_c, high_c])],
    ]


def scatter_stages(links, here, there):
    got = yield [links.other_core(block) for block in there]
    half = links.line // 2
    count = len(here)
    sums = [[add(mine[j], theirs[j]) for j in range(4)] for mine, theirs in zip(here, got, strict=True)]
    got = yield (
        [links.y(s[3][:half]) for s in sums]
        + [links.x(s[3][half:]) for s in sums]
        + [links.x(s[1][half:]) for s in sums]
        + [links.y(s[2][:half]) for s in sums]
    )
    low, high, x_high, y_low = (got[i * count : (i + 1) * count] for i in range(4))
    got = yield (
        [links.x(add(s[1][:half], v)) for s, v in zip(sums, low, strict=True)]
        + [links.y(add(s[2][half:], v)) for s, v in zip(sums, high, strict=True)]
    )
    x_low, y_high = got[:count], got[count:]
    own = []
    for i, s in enumerate(sums):
        own.append(
            [add(s[0][j], x_low[i][j], y_low[i][j]) for j in range(half)]
            + [add(s[0][half + j], x_high[i][j], y_high[i][j]) for j in range(links.line - half)]
        )
    got = yield [links.send(blocks[step], step) for blocks in own for step in range(1, links.line)]
    each = links.line - 1
    total = [add(blocks[0], *got[i * each : (i + 1) * each]) for i, blocks in enumerate(own)]
    if links.dp > 4:
        total = [lax.psum(t, "dp", axis_index_groups=links.rest) for t in total]
    got = yield [links.x(t) for t in total] + [links.y(t) for t in total]
    both = yield [links.y(t) for t in got[:count]]
    return [(t, got[i], got[count + i], both[i]) for i, t in enumerate(total)]


def in_order(links, quarters):
    whole = jnp.zeros((4, *quarters[0].shape), quarters[0].dtype)
    for place, block in enumerate(quarters):
        whole = lax.dynamic_update_index_in_dim(whole, block, links.quarter ^ place, 0)
    return whole


def own_quarter(links, packed, axis):
    shape = packed.shape[:axis] + (4, packed.shape[axis] // 4) + packed.shape[axis + 1 :]
    return lax.dynamic_index_in_dim(packed.reshape(shape), links.quarter, axis, False)


def attention_weights(links, blocks, rows):
    part, width = blocks[0][0].shape[1:]
    whole = jnp.zeros((links.line, 2, 4, part, width), jnp.bfloat16)
    for core in range(2):
        for place in range(4):
            whole = lax.dynamic_update_slice(
                whole,
                jnp.roll(blocks[core][place], links.chip, axis=0)[:, None, None],
                (0, links.core ^ core, links.quarter ^ place, 0, 0),
            )
    whole = whole.reshape(links.col, 4 * part, width)
    a, b = rows[0], rows[0] + rows[1]
    return (
        jnp.concatenate([whole[:, :a].reshape(-1, width), whole[:, a:b].reshape(-1, width)]),
        whole[:, b:].reshape(-1, width),
    )


def attention_blocks(links, qkv_grad, output_grad, rows):
    width = output_grad.shape[1]
    cut = rows[0] * links.col
    parts = [g.reshape(links.col, -1, width) for g in (qkv_grad[:cut], qkv_grad[cut:], output_grad)]
    whole = jnp.concatenate(parts, axis=1)
    whole = whole.reshape(links.line, 2, 4, -1, width)
    whole = jnp.roll(whole, -links.chip, axis=0)
    return [
        jnp.stack(
            [
                lax.dynamic_slice(
                    whole,
                    (0, links.core ^ core, links.quarter ^ place, 0, 0),
                    (links.line, 1, 1, *whole.shape[3:]),
                )[:, 0, 0]
                for place in range(4)
            ]
        )
        for core in range(2)
    ]


def rms_pull(value, gain, grad):
    scale = lax.rsqrt(jnp.mean(value * value, axis=-1, keepdims=True) + epsilon)
    scaled = value * scale
    pulled = grad * gain
    inner = jnp.mean(pulled * scaled, axis=-1, keepdims=True)
    return scale * (pulled - scaled * inner), jnp.sum(grad * scaled, axis=0)


def per_device(
    dp,
    col,
    inputs,
    segment_ids,
    cotangent,
    attn_gain,
    query_weight,
    key_value_weight,
    output_weight,
    ffn_gain,
    gate_weight,
    upward_weight,
    down_weight,
):
    links = Links(dp, col)
    layers, width = attn_gain.shape
    rows = (query_weight.shape[2], key_value_weight.shape[2], output_weight.shape[1])
    segments = segment_ids[0]
    where = (*tables(segments, HEAD_WIDTH), segments[:, None], segments[None, :])
    attn_gains = attn_gain.astype(jnp.float32)
    ffn_gains = ffn_gain.astype(jnp.float32)

    weights = []
    previous = None
    for layer in range(layers):
        attn_part = jnp.concatenate([query_weight[layer].T, key_value_weight[layer].T, output_weight[layer]])
        ffn_part = jnp.stack([gate_weight[layer].T, upward_weight[layer].T, down_weight[layer]])
        attn_part = own_quarter(links, attn_part, 0)
        ffn_part = own_quarter(links, ffn_part, 1)
        if previous is not None:
            attn_part = advance(attn_part, previous)
        attn_move = Transfer(gather_stages(links, attn_part))
        ffn_part = advance(ffn_part, attn_move)
        previous = Transfer(gather_stages(links, ffn_part))
        weights.append((attn_move, previous))

    hidden = inputs[0].astype(jnp.float32)
    saved = []
    for layer in range(layers):
        attn_move, ffn_move = weights[layer]
        qkv_w, output_w = attention_weights(links, attn_move.finish(), rows)
        normed = rms_norm(hidden, attn_gains[layer]).astype(jnp.bfloat16)
        raw = dot(normed, qkv_w, NT)
        qkv, attended, logsum = attention_forward(raw, *where)
        middle = hidden + dot(attended, output_w)
        normed2 = rms_norm(middle, ffn_gains[layer]).astype(jnp.bfloat16)
        ffn_w = [
            [jnp.concatenate([block[:, kind].reshape(-1, width) for block in half]) for kind in range(3)]
            for half in ffn_move.finish()
        ]
        result, *products = ffn_forward(middle, normed2, *ffn_w)
        saved.append((hidden, normed, qkv, attended, logsum, middle, normed2, products, qkv_w, output_w, ffn_w))
        hidden = result
    final = hidden.astype(jnp.bfloat16)[None]

    grad = cotangent[0].astype(jnp.float32)
    moves = [None] * layers
    gain_terms = [None] * layers
    attn_move = ffn_move = None
    for layer in reversed(range(layers)):
        hidden, normed, qkv, attended, logsum, middle, normed2, products, qkv_w, output_w, ffn_w = saved[layer]
        before = [] if attn_move is None else [attn_move]
        both = [] if attn_move is None else [ffn_move, attn_move]
        grad_low = grad.astype(jnp.bfloat16)
        shape = (4, links.line, -1, width)
        *there, grad_normed = ffn_backward(grad_low, normed2, *products[2:], *ffn_w[1])
        here = []
        new_move = Transfer(scatter_stages(links, here, [g.reshape(shape) for g in there]))
        grad_normed = advance(grad_normed, *before)
        *own, grad_normed = ffn_backward(grad_low, normed2, *products[:2], *ffn_w[0], grad_normed)
        here += [g.reshape(shape) for g in own]
        grad_normed = advance(grad_normed, new_move, *both)
        pulled, ffn_gain_grad = rms_pull(middle, ffn_gains[layer], grad_normed)
        grad = grad + pulled
        grad_low = grad.astype(jnp.bfloat16)
        output_grad = dot(attended, grad_low, TN).astype(jnp.bfloat16)
        attended_grad = dot(grad_low, output_w, NT).astype(jnp.bfloat16)
        attended_grad = advance(attended_grad, *both)
        qkv_grad = attention_backward(qkv, attended_grad, logsum, *where)
        qkv_grad = advance(qkv_grad, new_move, *both)
        qkv_w_grad = dot(qkv_grad, normed, TN).astype(jnp.bfloat16)
        blocks = attention_blocks(links, qkv_w_grad, output_grad, rows)
        ffn_move = new_move
        attn_move = Transfer(scatter_stages(links, blocks[:1], blocks[1:]))
        pulled, attn_gain_grad = rms_pull(hidden, attn_gains[layer], dot(qkv_grad, qkv_w))
        grad = grad + pulled
        if layer:
            grad = advance(grad, ffn_move, attn_move)
        moves[layer] = (attn_move, ffn_move)
        gain_terms[layer] = jnp.stack([attn_gain_grad, ffn_gain_grad])

    gains = links.sum_all(jnp.stack(gain_terms, axis=1))
    sums = [[] for _ in range(6)]
    for attn_move, ffn_move in moves:
        total = in_order(links, attn_move.finish()[0]).reshape(-1, width).astype(jnp.float32)
        a, b = rows[0], rows[0] + rows[1]
        sums[0].append(total[:a].T)
        sums[1].append(total[a:b].T)
        sums[2].append(total[b:])
        for kind, quarters in enumerate(ffn_move.finish()):
            total = in_order(links, quarters).reshape(-1, width).astype(jnp.float32)
            sums[3 + kind].append(total if kind == 2 else total.T)
    sums = [jnp.stack(values) for values in sums]
    return (final, grad[None], gains[0], *sums[:3], gains[1], *sums[3:])


def solution(mesh):
    placed = (
        P(("dp", "col"), None, None),
        P(("dp", "col"), None),
        P(("dp", "col"), None, None),
        P(),
        P(None, None, "col"),
        P(None, None, "col"),
        P(None, "col", None),
        P(),
        P(None, None, "col"),
        P(None, None, "col"),
        P(None, "col", None),
    )
    return jax.shard_map(
        functools.partial(per_device, mesh.shape["dp"], mesh.shape["col"]),
        mesh=mesh,
        in_specs=placed,
        out_specs=(
            P(("dp", "col"), None, None),
            P(("dp", "col"), None, None),
            P(),
            P(None, None, "col"),
            P(None, None, "col"),
            P(None, "col", None),
            P(),
            P(None, None, "col"),
            P(None, None, "col"),
            P(None, "col", None),
        ),
        check_vma=False,
    )
```

time: 1530 us -> 961 us (0.63)
  waiting for transfers between devices: 838 us -> 266 us
  matrix products: 435 us -> 48.3 us
  Pallas kernels: 0 us -> 220 us
  starting transfers between devices: 2.12 us -> 178 us
  local copies, waits for them, and re-layouts: 57.4 us -> 118 us
  blocking collectives: 38.5 us -> 0 us
  other arithmetic: 135 us -> 119 us
    reduce_scatter x10 -> x0, waiting for transfers between devices: 428 us -> none  [the longest x2 119 us: per_device(): lax.psum_scatter(upward_grad.astype(jnp.bfloat16), 'col', scatter_dimensi...]
    dot_general x48 -> x12, matrix products: 435 us -> 48.3 us  [dot(): lax.dot_general(left, right, (dims, ((), ())), preferred_element_type=jnp...]
    all_gather x12 -> x0, waiting for transfers between devices: 342 us -> none  [the longest x2 95.9 us: per_device(): lax.all_gather(upward_weight[layer], 'col', axis=1, tiled=True)]
    ppermute x0 -> x157, waiting for transfers between devices: none -> 266 us  [the longest x48 97.8 us: y(): return lax.ppermute(value, 'dp', [(i, i ^ 2) for i in range(self.dp)])]
    pallas_call x0 -> x10, Pallas kernels: none -> 220 us  [call(): pl.pallas_call(run, out_shape=outs, in_specs=list(specs) + [pl.BlockSpec(...]
    ppermute x0 -> x157, starting transfers between devices: none -> 178 us  [the longest x36 69.5 us: send(): lax.ppermute(value, 'col', [(i, (i + 2 * step) % self.col) for i in range...]
    psum x1 -> x0, waiting for transfers between devices: 56.2 us -> none  [per_device(): lax.psum(stacked[0].astype(jnp.bfloat16), 'dp').astype(jnp.float32)]
    slice x8 -> x66, local copies, waits for them, and re-layouts: 3.53 us -> 47.6 us  [the longest x16 18.2 us: per_device(): block[:, kind].reshape(-1, width)]
  transfers between devices with their start and end apart: 25 -> 157, of which waited for: 20 -> 65; matrix products, arithmetic and copies ran while one was open for 28% -> 23% of each run, Pallas kernels for 0% -> 19%
where the time goes in v1:
time: 961 us; the launch traced here: 953 us
  waiting for transfers between devices  266 us (28%)
  Pallas kernels  220 us (23%)
  starting transfers between devices  178 us (19%)
  other arithmetic  119 us (12%)
  local copies, waits for them, and re-layouts  118 us (12%)
  matrix products  48.3 us (5%)
    pallas_call x10, Pallas kernels, call(): pl.pallas_call(run, out_shape=outs, in_specs=list(specs) + [pl.BlockSpec(...  220 us
    ppermute x48, waiting for transfers between devices, y(): return lax.ppermute(value, 'dp', [(i, i ^ 2) for i in range(self.dp)])  97.8 us
    ppermute x36, waiting for transfers between devices, send(): lax.ppermute(value, 'col', [(i, (i + 2 * step) % self.col) for i in range...  94.9 us
    ppermute x36, starting transfers between devices, send(): lax.ppermute(value, 'col', [(i, (i + 2 * step) % self.col) for i in range...  69.5 us
    ppermute x40, waiting for transfers between devices, x(): return lax.ppermute(value, 'dp', [(i, i ^ 1) for i in range(self.dp)])  64.4 us
    ppermute x48, starting transfers between devices, y(): return lax.ppermute(value, 'dp', [(i, i ^ 2) for i in range(self.dp)])  55.5 us
    dot_general x12, matrix products, dot(): lax.dot_general(left, right, (dims, ((), ())), preferred_element_type=jnp...  48.3 us
    convert_element_type x34, other arithmetic, add(): return total.astype(jnp.bfloat16)  44.7 us
  transfers between devices with their start and end apart: 157, of which 65 were waited for; matrix products, arithmetic and copies ran while one was open for 23% of the time, Pallas kernels for 19%

profile of v1, /device:TPU:0, one launch (start us, length us, event | category | flops | bytes accessed | tf_op | source)
XLA Modules:
  0.0 953.1 jit_solution(6913089965268963974)
XLA Ops:
  54.1 22.5 %collective-permute-done.13 = bf16[3,80,960]{2,1,0:T(8,128)(2,1)} collective-permute-done((bf16[3,80,960]{2,1,0:T(8,128)(2,1)}, bf16[3,80,960]{2,1,0:T(8,128)(2,1)}, u32[]{:S(2)}, u32[]{:S(2)}) %collective-permute-start.13) | collective-permute-done | bytes 460832 | tf_op jit(solution)/shard_map/ppermute | solution.py:310
  82.7 8.1 collective-permute-start.26
  116.0 11.2 %collective-permute-done.37 = bf16[3,80,960]{2,1,0:T(8,128)(2,1)S(1)} collective-permute-done((bf16[3,80,960]{2,1,0:T(8,128)(2,1)S(1)}, bf16[3,80,960]{2,1,0:T(8,128)(2,1)S(1)}, u32[]{:S(2)}, u32[]{:S(2)}) %collective-permute-start.37) | collective-permute-done | bytes 460832 | tf_op jit(solution)/shard_map/ppermute | solution.py:310
  159.6 23.7 %shard_map.186 = (bf16[768,1600]{1,0:T(8,128)(2,1)}, bf16[768,960]{1,0:T(8,128)(2,1)}, f32[16,768]{1,0:T(8,128)}) custom-call(f32[768,1600]{1,0:T(8,128)} %fusion.15.refs_0_, f32[768,128]{1,0:T(8,128)} %copy.143.refs_1_.refs_3_, f32[768,128]{1,0:T(8,128)} %copy.144.refs_2_.refs_4_, s32[768,1]{1,0:T(8,128)} %copy.145.refs_3_.refs_5_, s32[1,768]{1,0:T(1,128)} %refs_6_.3), custom_call_target="tpu_custom_call" | custom-call | flops 15000000512 | bytes 15728640 | tf_op jit(solution)/shard_map/pallas_call | solution.py:54
  204.4 27.1 %collective-permute-done.39 = bf16[4,3,80,960]{3,2,0,1:T(8,128)(2,1)S(1)} collective-permute-done((bf16[4,3,80,960]{3,2,0,1:T(8,128)(2,1)S(1)}, bf16[4,3,80,960]{3,2,0,1:T(8,128)(2,1)S(1)}, u32[]{:S(2)}, u32[]{:S(2)}) %collective-permute-start.39) | collective-permute-done | bytes 1843232 | tf_op jit(solution)/shard_map/ppermute | solution.py:301
  240.4 14.2 %collective-permute-done.17 = bf16[2,3,80,960]{3,2,0,1:T(8,128)(2,1)S(1)} collective-permute-done((bf16[2,3,80,960]{3,2,0,1:T(8,128)(2,1)S(1)}, bf16[2,3,80,960]{3,2,0,1:T(8,128)(2,1)S(1)}, u32[]{:S(2)}, u32[]{:S(2)}) %collective-permute-start.17) | collective-permute-done | bytes 921632 | tf_op jit(solution)/shard_map/ppermute | solution.py:304
  259.7 15.4 %collective-permute-done.41 = bf16[2,3,80,960]{3,2,0,1:T(8,128)(2,1)} collective-permute-done((bf16[2,3,80,960]{3,2,0,1:T(8,128)(2,1)S(1)}, bf16[2,3,80,960]{3,2,0,1:T(8,128)(2,1)}, u32[]{:S(2)}, u32[]{:S(2)}) %collective-permute-start.41) | collective-permute-done | bytes 921632 | tf_op jit(solution)/shard_map/ppermute | solution.py:304
  290.8 21.4 %shard_map.187 = (f32[768,960]{1,0:T(8,128)}, bf16[768,1280]{1,0:T(8,128)(2,1)}, bf16[768,1280]{1,0:T(8,128)(2,1)}, bf16[768,1280]{1,0:T(8,128)(2,1)}, bf16[768,1280]{1,0:T(8,128)(2,1)}) custom-call(f32[768,960]{1,0:T(8,128)} %copy-done, bf16[768,960]{1,0:T(8,128)(2,1)} %multiply_convert_fusion.2.refs_1_, ...), custom_call_target="tpu_custom_call" | custom-call | flops 11000000512 | bytes 20971520 | tf_op jit(solution)/shard_map/pallas_call | solution.py:54
  315.1 6.7 fusion.13.refs_0_
  321.8 23.4 %shard_map.188 = (bf16[768,1600]{1,0:T(8,128)(2,1)}, bf16[768,960]{1,0:T(8,128)(2,1)}, f32[16,768]{1,0:T(8,128)}) custom-call(f32[768,1600]{1,0:T(8,128)} %fusion.13.refs_0_, f32[768,128]{1,0:T(8,128)} %copy.143.refs_1_.refs_3_, f32[768,128]{1,0:T(8,128)} %copy.144.refs_2_.refs_4_, s32[768,1]{1,0:T(8,128)} %copy.145.refs_3_.refs_5_, s32[1,768]{1,0:T(1,128)} %refs_6_.3), custom_call_target="tpu_custom_call" | custom-call | flops 15000000512 | bytes 15728640 | tf_op jit(solution)/shard_map/pallas_call | solution.py:54
  363.8 21.7 %shard_map.189 = (f32[768,960]{1,0:T(8,128)}, bf16[768,1280]{1,0:T(8,128)(2,1)}, bf16[768,1280]{1,0:T(8,128)(2,1)}, bf16[768,1280]{1,0:T(8,128)(2,1)}, bf16[768,1280]{1,0:T(8,128)(2,1)}) custom-call(f32[768,960]{1,0:T(8,128)} %copy-done.2, bf16[768,960]{1,0:T(8,128)(2,1)} %multiply_convert_fusion.refs_1_, ...), custom_call_target="tpu_custom_call" | custom-call | flops 11000000512 | bytes 20971520 | tf_op jit(solution)/shard_map/pallas_call | solution.py:54
  389.2 19.2 %shard_map.190 = (bf16[1280,960]{1,0:T(8,128)(2,1)}, bf16[1280,960]{1,0:T(8,128)(2,1)}, bf16[1280,960]{1,0:T(8,128)(2,1)}, f32[768,960]{1,0:T(8,128)}) custom-call(bf16[768,960]{1,0:T(8,128)(2,1)} %bitcast.680, bf16[768,960]{1,0:T(8,128)(2,1)} %multiply_convert_fusion.refs_1_, bf16[768,1280]{1,0:T(8,128)(2,1)} %get-tuple-element.147.refs_2_, ...), custom_call_target="tpu_custom_call" | custom-call | flops 22000001024 | bytes 47185920 | tf_op jit(solution)/shard_map/pallas_call | solution.py:54
  409.0 20.1 %shard_map.191 = (bf16[1280,960]{1,0:T(8,128)(2,1)}, bf16[1280,960]{1,0:T(8,128)(2,1)}, bf16[1280,960]{1,0:T(8,128)(2,1)}, f32[768,960]{1,0:T(8,128)}) custom-call(bf16[768,960]{1,0:T(8,128)(2,1)} %bitcast.681, bf16[768,960]{1,0:T(8,128)(2,1)} %multiply_convert_fusion.refs_1_, bf16[768,1280]{1,0:T(8,128)(2,1)} %get-tuple-element.145.refs_2_, ...), custom_call_target="tpu_custom_call" | custom-call | flops 22000001024 | bytes 47185920 | tf_op jit(solution)/shard_map/pallas_call | solution.py:54
  462.0 25.5 %shard_map.192 = bf16[768,1600]{1,0:T(8,128)(2,1)} custom-call(bf16[768,1600]{1,0:T(8,128)(2,1)} %get-tuple-element.155.refs_0_, bf16[768,960]{1,0:T(8,128)(2,1)} %copy.160.refs_1_, f32[16,768]{1,0:T(8,128)} %get-tuple-element.156.refs_2_, f32[768,128]{1,0:T(8,128)} %copy.143.refs_1_.refs_3_, f32[768,128]{1,0:T(8,128)} %copy.144.refs_2_.refs_4_, ...), custom_call_target="tpu_custom_call" | custom-call | flops 30000001024 | bytes 20971520 | tf_op jit(solution)/shard_map/pallas_call | solution.py:54
  549.8 7.0 collective-permute-done.67
  572.7 9.5 collective-permute-start.77
  582.3 19.6 %shard_map.193 = (bf16[1280,960]{1,0:T(8,128)(2,1)}, bf16[1280,960]{1,0:T(8,128)(2,1)}, bf16[1280,960]{1,0:T(8,128)(2,1)}, f32[768,960]{1,0:T(8,128)}) custom-call(bf16[768,960]{1,0:T(8,128)(2,1)} %convert_element_type.1517.refs_0_, bf16[768,960]{1,0:T(8,128)(2,1)} %multiply_convert_fusion.2.refs_1_, bf16[768,1280]{1,0:T(8,128)(2,1)} %get-tuple-element.173.refs_2_, ...), custom_call_target="tpu_custom_call" | custom-call | flops 22000001024 | bytes 47185920 | tf_op jit(solution)/shard_map/pallas_call | solution.py:54
  609.2 20.0 %shard_map.194 = (bf16[1280,960]{1,0:T(8,128)(2,1)}, bf16[1280,960]{1,0:T(8,128)(2,1)}, bf16[1280,960]{1,0:T(8,128)(2,1)}, f32[768,960]{1,0:T(8,128)}) custom-call(bf16[768,960]{1,0:T(8,128)(2,1)} %convert_element_type.1517.refs_0_, bf16[768,960]{1,0:T(8,128)(2,1)} %multiply_convert_fusion.2.refs_1_, bf16[768,1280]{1,0:T(8,128)(2,1)} %get-tuple-element.171.refs_2_, ...), custom_call_target="tpu_custom_call" | custom-call | flops 22000001024 | bytes 47185920 | tf_op jit(solution)/shard_map/pallas_call | solution.py:54
  638.3 6.3 collective-permute-done.81
  715.7 25.3 %shard_map.195 = bf16[768,1600]{1,0:T(8,128)(2,1)} custom-call(bf16[768,1600]{1,0:T(8,128)(2,1)} %get-tuple-element.197.refs_0_, bf16[768,960]{1,0:T(8,128)(2,1)} %convolution_convert_fusion.4.refs_1_, f32[16,768]{1,0:T(8,128)} %get-tuple-element.212.refs_2_, f32[768,128]{1,0:T(8,128)} %copy.143.refs_1_.refs_3_, f32[768,128]{1,0:T(8,128)} %copy.144.refs_2_.refs_4_, ...), custom_call_target="tpu_custom_call" | custom-call | flops 30000001024 | bytes 20971520 | tf_op jit(solution)/shard_map/pallas_call | solution.py:54
  783.5 5.6 fusion.10
  853.7 11.4 %collective-permute-done.136 = bf16[80,960]{1,0:T(8,128)(2,1)S(1)} collective-permute-done((bf16[80,960]{1,0:T(8,128)(2,1)S(1)}, bf16[80,960]{1,0:T(8,128)(2,1)S(1)}, u32[]{:S(2)}, u32[]{:S(2)}) %collective-permute-start.136) | collective-permute-done | bytes 153632 | tf_op jit(solution)/shard_map/ppermute | solution.py:310
  871.9 7.9 collective-permute-done.144
  932.5 5.8 collective-permute-done.127
  (893 shorter events, 570.5 us)
Async XLA Ops:
  33.5 43.1 %collective-permute-start.13 = (bf16[3,80,960]{2,1,0:T(8,128)(2,1)}, bf16[3,80,960]{2,1,0:T(8,128)(2,1)}, u32[]{:S(2)}, u32[]{:S(2)}) collective-permute-start(bf16[3,80,960]{2,1,0:T(8,128)(2,1)} %fusion.149), channel_id=1, source_target_pairs={{0,4},{1,5},{2,6},{3,7},{4,0},{5,1},{6,2},{7,3},{8,12},{9,13},{10,... | collective-permute-start | bytes 1382408 | tf_op jit(solution)/shard_map/ppermute | solution.py:310
  34.6 42.0 %collective-permute-start.14 = (bf16[3,80,960]{2,1,0:T(8,128)(2,1)}, bf16[3,80,960]{2,1,0:T(8,128)(2,1)}, u32[]{:S(2)}, u32[]{:S(2)}) collective-permute-start(bf16[3,80,960]{2,1,0:T(8,128)(2,1)} %fusion.149), channel_id=1, source_target_pairs={{0,2},{1,3},{2,4},{3,5},{4,6},{5,7},{6,0},{7,1},{8,10},{9,11},{10,... | collective-permute-start | bytes 1382408 | tf_op jit(solution)/shard_map/ppermute | solution.py:310
  48.0 49.9 %collective-permute-start.3 = (bf16[4,80,960]{2,1,0:T(8,128)(2,1)S(1)}, bf16[4,80,960]{2,1,0:T(8,128)(2,1)S(1)}, u32[]{:S(2)}, u32[]{:S(2)}) collective-permute-start(bf16[4,80,960]{2,1,0:T(8,128)(2,1)S(1)} %pad_maximum_fusion.27), channel_id=1, source_target_pairs={{0,8},{8,0},{16,24},{24,16},{1,9},{9,1},{17,25},{25,17},{2,10},{10... | collective-permute-start | bytes 1843208 | tf_op jit(solution)/shard_map/ppermute | solution.py:301
  49.5 51.7 %collective-permute-start.4 = (bf16[4,80,960]{2,1,0:T(8,128)(2,1)S(1)}, bf16[4,80,960]{2,1,0:T(8,128)(2,1)S(1)}, u32[]{:S(2)}, u32[]{:S(2)}) collective-permute-start(bf16[4,80,960]{2,1,0:T(8,128)(2,1)S(1)} %pad_maximum_fusion.27), channel_id=1, source_target_pairs={{0,16},{8,24},{16,0},{24,8},{1,17},{9,25},{17,1},{25,9},{2,18},{10... | collective-permute-start | bytes 1843208 | tf_op jit(solution)/shard_map/ppermute | solution.py:304
  54.0 48.8 %collective-permute-start.7 = (bf16[4,80,960]{2,1,0:T(8,128)(2,1)S(1)}, bf16[4,80,960]{2,1,0:T(8,128)(2,1)S(1)}, u32[]{:S(2)}, u32[]{:S(2)}) collective-permute-start(bf16[4,80,960]{2,1,0:T(8,128)(2,1)S(1)} %pad_maximum_fusion.27), channel_id=1, source_target_pairs={{0,1},{1,0},{2,3},{3,2},{4,5},{5,4},{6,7},{7,6},{8,9},{9,8},{10,11... | collective-permute-start | bytes 1843208 | tf_op jit(solution)/shard_map/ppermute | solution.py:307
  143.7 45.8 %collective-permute-start.15 = (bf16[4,3,80,960]{3,2,0,1:T(8,128)(2,1)S(1)}, bf16[4,3,80,960]{3,2,0,1:T(8,128)(2,1)}, u32[]{:S(2)}, u32[]{:S(2)}) collective-permute-start(bf16[4,3,80,960]{3,2,0,1:T(8,128)(2,1)S(1)} %pad_maximum_fusion.22), channel_id=1, source_target_pairs={{0,8},{8,0},{16,24},{24,16},{1,9},{9,1},{17,25},{25,17},{2,10},{10... | collective-permute-start | bytes 5529608 | tf_op jit(solution)/shard_map/ppermute | solution.py:301
  145.7 50.2 %collective-permute-start.16 = (bf16[4,3,80,960]{3,2,0,1:T(8,128)(2,1)S(1)}, bf16[4,3,80,960]{3,2,0,1:T(8,128)(2,1)}, u32[]{:S(2)}, u32[]{:S(2)}) collective-permute-start(bf16[4,3,80,960]{3,2,0,1:T(8,128)(2,1)S(1)} %pad_maximum_fusion.22), channel_id=1, source_target_pairs={{0,16},{8,24},{16,0},{24,8},{1,17},{9,25},{17,1},{25,9},{2,18},{10... | collective-permute-start | bytes 5529608 | tf_op jit(solution)/shard_map/ppermute | solution.py:304
  146.3 54.9 %collective-permute-start.19 = (bf16[4,3,80,960]{3,2,0,1:T(8,128)(2,1)S(1)}, bf16[4,3,80,960]{3,2,0,1:T(8,128)(2,1)}, u32[]{:S(2)}, u32[]{:S(2)}) collective-permute-start(bf16[4,3,80,960]{3,2,0,1:T(8,128)(2,1)S(1)} %pad_maximum_fusion.22), channel_id=1, source_target_pairs={{0,1},{1,0},{2,3},{3,2},{4,5},{5,4},{6,7},{7,6},{8,9},{9,8},{10,11... | collective-permute-start | bytes 5529608 | tf_op jit(solution)/shard_map/ppermute | solution.py:307
  146.3 85.3 %collective-permute-start.39 = (bf16[4,3,80,960]{3,2,0,1:T(8,128)(2,1)S(1)}, bf16[4,3,80,960]{3,2,0,1:T(8,128)(2,1)S(1)}, u32[]{:S(2)}, u32[]{:S(2)}) collective-permute-start(bf16[4,3,80,960]{3,2,0,1:T(8,128)(2,1)S(1)} %pad_maximum_fusion.23), channel_id=1, source_target_pairs={{0,8},{8,0},{16,24},{24,16},{1,9},{9,1},{17,25},{25,17},{2,10},{10... | collective-permute-start | bytes 5529608 | tf_op jit(solution)/shard_map/ppermute | solution.py:301
  146.9 86.8 %collective-permute-start.40 = (bf16[4,3,80,960]{3,2,0,1:T(8,128)(2,1)S(1)}, bf16[4,3,80,960]{3,2,0,1:T(8,128)(2,1)}, u32[]{:S(2)}, u32[]{:S(2)}) collective-permute-start(bf16[4,3,80,960]{3,2,0,1:T(8,128)(2,1)S(1)} %pad_maximum_fusion.23), channel_id=1, source_target_pairs={{0,16},{8,24},{16,0},{24,8},{1,17},{9,25},{17,1},{25,9},{2,18},{10... | collective-permute-start | bytes 5529608 | tf_op jit(solution)/shard_map/ppermute | solution.py:304
  189.5 49.0 %collective-permute-start.43 = (bf16[4,3,80,960]{3,2,0,1:T(8,128)(2,1)S(1)}, bf16[4,3,80,960]{3,2,0,1:T(8,128)(2,1)S(1)}, u32[]{:S(2)}, u32[]{:S(2)}) collective-permute-start(bf16[4,3,80,960]{3,2,0,1:T(8,128)(2,1)S(1)} %pad_maximum_fusion.23), channel_id=1, source_target_pairs={{0,1},{1,0},{2,3},{3,2},{4,5},{5,4},{6,7},{7,6},{8,9},{9,8},{10,11... | collective-permute-start | bytes 5529608 | tf_op jit(solution)/shard_map/ppermute | solution.py:307
  195.9 58.7 %collective-permute-start.17 = (bf16[2,3,80,960]{3,2,0,1:T(8,128)(2,1)S(1)}, bf16[2,3,80,960]{3,2,0,1:T(8,128)(2,1)S(1)}, u32[]{:S(2)}, u32[]{:S(2)}) collective-permute-start(bf16[2,3,80,960]{3,2,0,1:T(8,128)(2,1)S(1)} %slice.1198), channel_id=1, source_target_pairs={{0,16},{8,24},{16,0},{24,8},{1,17},{9,25},{17,1},{25,9},{2,18},{10... | collective-permute-start | bytes 2764808 | tf_op jit(solution)/shard_map/ppermute | solution.py:304
  201.2 54.0 %collective-permute-start.18 = (bf16[2,3,80,960]{3,2,0,1:T(8,128)(2,1)S(1)}, bf16[2,3,80,960]{3,2,0,1:T(8,128)(2,1)S(1)}, u32[]{:S(2)}, u32[]{:S(2)}) collective-permute-start(bf16[2,3,80,960]{3,2,0,1:T(8,128)(2,1)S(1)} %slice.1199), channel_id=1, source_target_pairs={{0,8},{8,0},{16,24},{24,16},{1,9},{9,1},{17,25},{25,17},{2,10},{10... | collective-permute-start | bytes 2764808 | tf_op jit(solution)/shard_map/ppermute | solution.py:301
  231.5 51.0 %collective-permute-start.21 = (bf16[4,3,80,960]{3,2,0,1:T(8,128)(2,1)}, bf16[4,3,80,960]{3,2,0,1:T(8,128)(2,1)S(1)}, u32[]{:S(2)}, u32[]{:S(2)}) collective-permute-start(bf16[4,3,80,960]{3,2,0,1:T(8,128)(2,1)} %collective-permute-done.16), channel_id=1, source_target_pairs={{0,1},{1,0},{2,3},{3,2},{4,5},{5,4},{6,7},{7,6},{8,9},{9,8},{10,11... | collective-permute-start | bytes 5529608 | tf_op jit(solution)/shard_map/ppermute | solution.py:307
  233.7 49.6 %collective-permute-start.20 = (bf16[4,3,80,960]{3,2,0,1:T(8,128)(2,1)}, bf16[4,3,80,960]{3,2,0,1:T(8,128)(2,1)S(1)}, u32[]{:S(2)}, u32[]{:S(2)}) collective-permute-start(bf16[4,3,80,960]{3,2,0,1:T(8,128)(2,1)} %collective-permute-done.15), channel_id=1, source_target_pairs={{0,1},{1,0},{2,3},{3,2},{4,5},{5,4},{6,7},{7,6},{8,9},{9,8},{10,11... | collective-permute-start | bytes 5529608 | tf_op jit(solution)/shard_map/ppermute | solution.py:307
  255.3 98.0 %collective-permute-start.45 = (bf16[4,3,80,960]{3,2,0,1:T(8,128)(2,1)}, bf16[4,3,80,960]{3,2,0,1:T(8,128)(2,1)}, u32[]{:S(2)}, u32[]{:S(2)}) collective-permute-start(bf16[4,3,80,960]{3,2,0,1:T(8,128)(2,1)} %collective-permute-done.40), channel_id=1, source_target_pairs={{0,1},{1,0},{2,3},{3,2},{4,5},{5,4},{6,7},{7,6},{8,9},{9,8},{10,11... | collective-permute-start | bytes 5529608 | tf_op jit(solution)/shard_map/ppermute | solution.py:307
  282.5 72.5 %collective-permute-start.44 = (bf16[4,3,80,960]{3,2,0,1:T(8,128)(2,1)S(1)}, bf16[4,3,80,960]{3,2,0,1:T(8,128)(2,1)}, u32[]{:S(2)}, u32[]{:S(2)}) collective-permute-start(bf16[4,3,80,960]{3,2,0,1:T(8,128)(2,1)S(1)} %collective-permute-done.39), channel_id=1, source_target_pairs={{0,1},{1,0},{2,3},{3,2},{4,5},{5,4},{6,7},{7,6},{8,9},{9,8},{10,11... | collective-permute-start | bytes 5529608 | tf_op jit(solution)/shard_map/ppermute | solution.py:307
  283.3 67.1 %collective-permute-start.46 = (bf16[2,3,80,960]{3,2,0,1:T(8,128)(2,1)}, bf16[2,3,80,960]{3,2,0,1:T(8,128)(2,1)}, u32[]{:S(2)}, u32[]{:S(2)}) collective-permute-start(bf16[2,3,80,960]{3,2,0,1:T(8,128)(2,1)} %collective-permute-done.41), channel_id=1, source_target_pairs={{0,1},{1,0},{2,3},{3,2},{4,5},{5,4},{6,7},{7,6},{8,9},{9,8},{10,11... | collective-permute-start | bytes 2764808 | tf_op jit(solution)/shard_map/ppermute | solution.py:307
  283.5 68.1 %collective-permute-start.47 = (bf16[2,3,80,960]{3,2,0,1:T(8,128)(2,1)}, bf16[2,3,80,960]{3,2,0,1:T(8,128)(2,1)}, u32[]{:S(2)}, u32[]{:S(2)}) collective-permute-start(bf16[2,3,80,960]{3,2,0,1:T(8,128)(2,1)} %collective-permute-done.42), channel_id=1, source_target_pairs={{0,1},{1,0},{2,3},{3,2},{4,5},{5,4},{6,7},{7,6},{8,9},{9,8},{10,11... | collective-permute-start | bytes 2764808 | tf_op jit(solution)/shard_map/ppermute | solution.py:307
  564.0 42.1 %collective-permute-start.70 = (bf16[2,80,960]{2,1,0:T(8,128)(2,1)S(1)}, bf16[2,80,960]{2,1,0:T(8,128)(2,1)}, u32[]{:S(2)}, u32[]{:S(2)}) collective-permute-start(bf16[2,80,960]{2,1,0:T(8,128)(2,1)S(1)} %get-tuple-element.467), channel_id=1, source_target_pairs={{0,16},{8,24},{16,0},{24,8},{1,17},{9,25},{17,1},{25,9},{2,18},{10... | collective-permute-start | bytes 921608 | tf_op jit(solution)/shard_map/ppermute | solution.py:304
  606.2 63.2 %collective-permute-start.74 = (bf16[4,4,80,960]{3,2,1,0:T(8,128)(2,1)}, bf16[4,4,80,960]{3,2,1,0:T(8,128)(2,1)}, u32[]{:S(2)}, u32[]{:S(2)}) collective-permute-start(bf16[4,4,80,960]{3,2,1,0:T(8,128)(2,1)} %bitcast.169), channel_id=1, source_target_pairs={{0,1},{1,0},{2,3},{3,2},{4,5},{5,4},{6,7},{7,6},{8,9},{9,8},{10,11... | collective-permute-start | bytes 7372808 | tf_op jit(solution)/shard_map/ppermute | solution.py:307
  606.2 63.2 %collective-permute-start.75 = (bf16[4,4,80,960]{3,2,1,0:T(8,128)(2,1)}, bf16[4,4,80,960]{3,2,1,0:T(8,128)(2,1)}, u32[]{:S(2)}, u32[]{:S(2)}) collective-permute-start(bf16[4,4,80,960]{3,2,1,0:T(8,128)(2,1)} %bitcast.170), channel_id=1, source_target_pairs={{0,1},{1,0},{2,3},{3,2},{4,5},{5,4},{6,7},{7,6},{8,9},{9,8},{10,11... | collective-permute-start | bytes 7372808 | tf_op jit(solution)/shard_map/ppermute | solution.py:307
  606.7 62.7 %collective-permute-start.76 = (bf16[4,4,80,960]{3,2,1,0:T(8,128)(2,1)}, bf16[4,4,80,960]{3,2,1,0:T(8,128)(2,1)S(1)}, u32[]{:S(2)}, u32[]{:S(2)}) collective-permute-start(bf16[4,4,80,960]{3,2,1,0:T(8,128)(2,1)} %bitcast.171), channel_id=1, source_target_pairs={{0,1},{1,0},{2,3},{3,2},{4,5},{5,4},{6,7},{7,6},{8,9},{9,8},{10,11... | collective-permute-start | bytes 7372808 | tf_op jit(solution)/shard_map/ppermute | solution.py:307
  810.1 90.9 %collective-permute-start.119 = (bf16[4,4,80,960]{3,2,1,0:T(8,128)(2,1)S(1)}, bf16[4,4,80,960]{3,2,1,0:T(8,128)(2,1)S(1)}, u32[]{:S(2)}, u32[]{:S(2)}) collective-permute-start(bf16[4,4,80,960]{3,2,1,0:T(8,128)(2,1)S(1)} %pad_maximum_fusion.17), channel_id=1, source_target_pairs={{0,1},{1,0},{2,3},{3,2},{4,5},{5,4},{6,7},{7,6},{8,9},{9,8},{10,11... | collective-permute-start | bytes 7372808 | tf_op jit(solution)/shard_map/ppermute | solution.py:307
  (294 other events, 4432.6 us)

commit v2 on v1

--- a/solution.py
+++ b/solution.py
@@ -200,92 +200,140 @@
 TILE = 256
 
 
-def ffn_forward(middle, normed, here, there, after=()):
+def collect(pieces, store, semaphores):
+    copies = [[], [], []]
+    for kind in range(3):
+        at = 0
+        for piece in pieces:
+            line, _, rows, _ = piece.shape
+            for z in range(line):
+                copies[kind].append(
+                    pltpu.make_async_copy(
+                        piece.at[z, kind], store.at[kind, pl.ds(at, rows)], semaphores.at[kind, len(copies[kind])]
+                    )
+                )
+                at += rows
+    return copies
+
+
+def blocks_of(pieces):
+    return sum(piece.shape[0] for piece in pieces)
+
+
+def units_of(pieces):
+    return sum(piece.shape[0] * piece.shape[2] for piece in pieces)
+
+
+def ffn_forward(middle, normed, here, there):
     length, width = middle.shape
-    units = here[0].shape[0]
+    units = units_of(here)
     tile = math.gcd(TILE, units)
-    steps = units // tile
-
-    def body(middle, normed, gate_a, upward_a, down_a, gate_b, upward_b, down_b, out, gate_one, up_one, gate_two, up_two):
-        step = pl.program_id(0)
-
-        @pl.when(step == 0)
-        def _():
-            out[...] = middle[...]
-
-        def half(gate_w, upward_w, down_w, gate_out, upward_out):
-            gate = dot(normed[...], gate_w[...], NT)
-            upward = dot(normed[...], upward_w[...], NT)
-            gate_out[...] = gate.astype(jnp.bfloat16)
-            upward_out[...] = upward.astype(jnp.bfloat16)
-            active = (gate * jax.nn.sigmoid(gate) * upward).astype(jnp.bfloat16)
-            out[...] += dot(active, down_w[...])
-
-        @pl.when(step < steps)
-        def _():
-            half(gate_a, upward_a, down_a, gate_one, up_one)
-
-        @pl.when(step >= steps)
-        def _():
-            half(gate_b, upward_b, down_b, gate_two, up_two)
-
-    whole = pl.BlockSpec((length, width), lambda i: (0, 0))
-    weight_a = pl.BlockSpec((tile, width), lambda i: (jnp.minimum(i, steps - 1), 0))
-    weight_b = pl.BlockSpec((tile, width), lambda i: (jnp.maximum(i - steps, 0), 0))
-    columns_a = pl.BlockSpec((length, tile), lambda i: (0, jnp.minimum(i, steps - 1)))
-    columns_b = pl.BlockSpec((length, tile), lambda i: (0, jnp.maximum(i - steps, 0)))
+
+    def body(middle, normed, *rest):
+        pieces = rest[: len(here) + len(there)]
+        out, gate_one, up_one, gate_two, up_two, store, semaphores = rest[len(pieces) :]
+        halves = (pieces[: len(here)], pieces[len(here) :])
+        copies = [collect(halves[i], store.at[i], semaphores.at[i]) for i in range(2)]
+        for half in copies:
+            for kind in half:
+                for copy in kind:
+                    copy.start()
+        out[...] = middle[...]
+        for i, (gate_out, upward_out) in enumerate(((gate_one, up_one), (gate_two, up_two))):
+            for kind in copies[i]:
+                for copy in kind:
+                    copy.wait()
+
+            def step(t, carry, i=i, gate_out=gate_out, upward_out=upward_out):
+                rows = pl.ds(pl.multiple_of(t * tile, tile), tile)
+                gate = dot(normed[...], store[i, 0, rows, :], NT)
+                upward = dot(normed[...], store[i, 1, rows, :], NT)
+                gate_out[:, rows] = gate.astype(jnp.bfloat16)
+                upward_out[:, rows] = upward.astype(jnp.bfloat16)
+                active = (gate * jax.nn.sigmoid(gate) * upward).astype(jnp.bfloat16)
+                out[...] += dot(active, store[i, 2, rows, :])
+                return carry
+
+            lax.fori_loop(0, units // tile, step, 0)
+
     low = jax.ShapeDtypeStruct((length, units), jnp.bfloat16)
     return call(
         body,
         [jax.ShapeDtypeStruct((length, width), jnp.float32), low, low, low, low],
         [middle, normed, *here, *there],
-        after,
-        grid=(2 * steps,),
-        in_specs=[whole, whole] + [weight_a] * 3 + [weight_b] * 3,
-        out_specs=[whole, columns_a, columns_a, columns_b, columns_b],
+        (),
+        [
+            pltpu.VMEM((2, 3, units, width), jnp.bfloat16),
+            pltpu.SemaphoreType.DMA((2, 3, blocks_of(here))),
+        ],
+        in_specs=[pl.BlockSpec(memory_space=pltpu.VMEM)] * 2
+        + [pl.BlockSpec(memory_space=pl.ANY)] * (len(here) + len(there)),
         flops=11 * 10**9,
-        nbytes=20 * MEGA,
-    )
-
-
-def ffn_backward(grad_low, normed, gate, upward, gate_full, upward_full, down_full, earlier=None):
+        nbytes=30 * MEGA,
+    )
+
+
+def ffn_backward(grad_low, normed, gate, upward, pieces, earlier=None):
     length, width = normed.shape
-    units = gate_full.shape[0]
+    units = units_of(pieces)
     tile = math.gcd(TILE, units)
-
-    def body(grad_low, normed, gate, upward, gate_w, upward_w, down_w, *rest):
-        *before, gate_grad, upward_grad, down_grad, out = rest
-
-        @pl.when(pl.program_id(0) == 0)
-        def _():
-            out[...] = before[0][...] if before else jnp.zeros_like(out)
-
-        grad_active = dot(grad_low[...], down_w[...], NT)
-        gate_value = gate[...].astype(jnp.float32)
-        up_value = upward[...].astype(jnp.float32)
-        sigma = jax.nn.sigmoid(gate_value)
-        silu = gate_value * sigma
-        down_grad[...] = dot((silu * up_value).astype(jnp.bfloat16), grad_low[...], TN).astype(jnp.bfloat16)
-        grad_up = (grad_active * silu).astype(jnp.bfloat16)
-        grad_gate = (grad_active * up_value * (sigma + silu * (1.0 - sigma))).astype(jnp.bfloat16)
-        gate_grad[...] = dot(grad_gate, normed[...], TN).astype(jnp.bfloat16)
-        upward_grad[...] = dot(grad_up, normed[...], TN).astype(jnp.bfloat16)
-        out[...] += dot(grad_gate, gate_w[...]) + dot(grad_up, upward_w[...])
-
-    whole = pl.BlockSpec((length, width), lambda i: (0, 0))
-    weight = pl.BlockSpec((tile, width), lambda i: (i, 0))
-    columns = pl.BlockSpec((length, tile), lambda i: (0, i))
-    shape = jax.ShapeDtypeStruct((units, width), jnp.bfloat16)
     before = [] if earlier is None else [earlier]
+
+    def body(grad_low, normed, gate, upward, *rest):
+        before, rest = rest[: len(rest) - 6 - len(pieces)], rest[len(rest) - 6 - len(pieces) :]
+        parts, (grads, out, store, ready, semaphores, sent) = rest[: len(pieces)], rest[len(pieces) :]
+        copies = collect(parts, store, semaphores)
+        for kind in (2, 0, 1):
+            for copy in copies[kind]:
+                copy.start()
+        out[...] = before[0][...] if before else jnp.zeros_like(out)
+        for kind in (2, 0, 1):
+            for copy in copies[kind]:
+                copy.wait()
+
+        def step(t, carry):
+            rows = pl.ds(pl.multiple_of(t * tile, tile), tile)
+            grad_active = dot(grad_low[...], store[2, rows, :], NT)
+            gate_value = gate[:, rows].astype(jnp.float32)
+            up_value = upward[:, rows].astype(jnp.float32)
+            sigma = jax.nn.sigmoid(gate_value)
+            silu = gate_value * sigma
+            active = (silu * up_value).astype(jnp.bfloat16)
+            grad_up = (grad_active * silu).astype(jnp.bfloat16)
+            grad_gate = (grad_active * up_value * (sigma + silu * (1.0 - sigma))).astype(jnp.bfloat16)
+            ready[2, rows, :] = dot(active, grad_low[...], TN).astype(jnp.bfloat16)
+            ready[0, rows, :] = dot(grad_gate, normed[...], TN).astype(jnp.bfloat16)
+            ready[1, rows, :] = dot(grad_up, normed[...], TN).astype(jnp.bfloat16)
+            out[...] += dot(grad_gate, store[0, rows, :]) + dot(grad_up, store[1, rows, :])
+            for kind in range(3):
+                pltpu.make_async_copy(ready.at[kind, rows], grads.at[kind, rows], sent.at[kind, t]).start()
+            return carry
+
+        lax.fori_loop(0, units // tile, step, 0)
+        for t in range(units // tile):
+            rows = pl.ds(t * tile, tile)
+            for kind in range(3):
+                pltpu.make_async_copy(ready.at[kind, rows], grads.at[kind, rows], sent.at[kind, t]).wait()
+
     return call(
         body,
-        [shape, shape, shape, jax.ShapeDtypeStruct((length, width), jnp.float32)],
-        [grad_low, normed, gate, upward, gate_full, upward_full, down_full, *before],
-        grid=(units // tile,),
-        in_specs=[whole, whole, columns, columns, weight, weight, weight] + [whole] * len(before),
-        out_specs=[weight, weight, weight, whole],
-        flops=22 * 10**9,
-        nbytes=45 * MEGA,
+        [
+            jax.ShapeDtypeStruct((3, units, width), jnp.bfloat16),
+            jax.ShapeDtypeStruct((length, width), jnp.float32),
+        ],
+        [grad_low, normed, gate, upward, *before, *pieces],
+        (),
+        [
+            pltpu.VMEM((3, units, width), jnp.bfloat16),
+            pltpu.VMEM((3, units, width), jnp.bfloat16),
+            pltpu.SemaphoreType.DMA((3, blocks_of(pieces))),
+            pltpu.SemaphoreType.DMA((3, units // tile)),
+        ],
+        in_specs=[pl.BlockSpec(memory_space=pltpu.VMEM)] * (4 + len(before))
+        + [pl.BlockSpec(memory_space=pl.ANY)] * len(pieces),
+        out_specs=[pl.BlockSpec(memory_space=pl.ANY), pl.BlockSpec(memory_space=pltpu.VMEM)],
+        flops=11 * 10**9,
+        nbytes=30 * MEGA,
     )
 
 
@@ -353,7 +401,7 @@
 
 def gather_stages(links, part):
     far = yield [links.send(part, -step) for step in range(1, links.line)]
-    own = jnp.stack([part, *far])
+    own = jnp.roll(jnp.stack([part, *far]), links.chip, axis=0)
     half = links.line // 2
     from_x, from_y, own_c = yield [links.x(own), links.y(own), links.other_core(own)]
     low, high, x_c, y_c = yield [
@@ -363,43 +411,43 @@
         links.other_core(from_y),
     ]
     low_c, high_c = yield [links.other_core(low), links.other_core(high)]
-    return [
-        [own, from_x, from_y, jnp.concatenate([low, high])],
-        [own_c, x_c, y_c, jnp.concatenate([low_c, high_c])],
+    return [[own, from_x, from_y, low, high], [own_c, x_c, y_c, low_c, high_c]]
+
+
+def scatter_stages(links, kept, there, pick):
+    (got,) = yield [links.other_core(there)]
+    here = kept[0]
+    half = links.line // 2
+    low, high = slice(0, half), slice(half, links.line)
+
+    def part(place, piece):
+        return add(pick(here, place, piece), pick(got, place, piece))
+
+    from_x, from_y = yield [
+        links.x(jnp.stack([part(3, high), part(1, high)])),
+        links.y(jnp.stack([part(3, low), part(2, low)])),
     ]
-
-
-def scatter_stages(links, here, there):
-    got = yield [links.other_core(block) for block in there]
-    half = links.line // 2
-    count = len(here)
-    sums = [[add(mine[j], theirs[j]) for j in range(4)] for mine, theirs in zip(here, got, strict=True)]
-    got = yield (
-        [links.y(s[3][:half]) for s in sums]
-        + [links.x(s[3][half:]) for s in sums]
-        + [links.x(s[1][half:]) for s in sums]
-        + [links.y(s[2][:half]) for s in sums]
-    )
-    low, high, x_high, y_low = (got[i * count : (i + 1) * count] for i in range(4))
-    got = yield (
-        [links.x(add(s[1][:half], v)) for s, v in zip(sums, low, strict=True)]
-        + [links.y(add(s[2][half:], v)) for s, v in zip(sums, high, strict=True)]
-    )
-    x_low, y_high = got[:count], got[count:]
-    own = []
-    for i, s in enumerate(sums):
-        own.append(
-            [add(s[0][j], x_low[i][j], y_low[i][j]) for j in range(half)]
-            + [add(s[0][half + j], x_high[i][j], y_high[i][j]) for j in range(links.line - half)]
-        )
-    got = yield [links.send(blocks[step], step) for blocks in own for step in range(1, links.line)]
-    each = links.line - 1
-    total = [add(blocks[0], *got[i * each : (i + 1) * each]) for i, blocks in enumerate(own)]
+    x_low, y_high = yield [
+        links.x(add(pick(here, 1, low), pick(got, 1, low), from_y[0])),
+        links.y(add(pick(here, 2, high), pick(got, 2, high), from_x[0])),
+    ]
+    own = jnp.concatenate(
+        [
+            add(pick(here, 0, low), pick(got, 0, low), from_y[1], x_low),
+            add(pick(here, 0, high), pick(got, 0, high), from_x[1], y_high),
+        ]
+    )
+
+    def chip(step):
+        return lax.dynamic_index_in_dim(own, (links.chip + step) % links.line, 0, False)
+
+    far = yield [links.send(chip(step), step) for step in range(1, links.line)]
+    total = add(chip(0), *far)
     if links.dp > 4:
-        total = [lax.psum(t, "dp", axis_index_groups=links.rest) for t in total]
-    got = yield [links.x(t) for t in total] + [links.y(t) for t in total]
-    both = yield [links.y(t) for t in got[:count]]
-    return [(t, got[i], got[count + i], both[i]) for i, t in enumerate(total)]
+        total = lax.psum(total, "dp", axis_index_groups=links.rest)
+    at_x, at_y = yield [links.x(total), links.y(total)]
+    (at_both,) = yield [links.y(at_x)]
+    return (total, at_x, at_y, at_both)
 
 
 def in_order(links, quarters):
@@ -416,13 +464,12 @@
 
 def attention_weights(links, blocks, rows):
     part, width = blocks[0][0].shape[1:]
+    half = links.line // 2
     whole = jnp.zeros((links.line, 2, 4, part, width), jnp.bfloat16)
     for core in range(2):
-        for place in range(4):
+        for place, start, block in zip((0, 1, 2, 3, 3), (0, 0, 0, 0, half), blocks[core], strict=True):
             whole = lax.dynamic_update_slice(
-                whole,
-                jnp.roll(blocks[core][place], links.chip, axis=0)[:, None, None],
-                (0, links.core ^ core, links.quarter ^ place, 0, 0),
+                whole, block[:, None, None], (start, links.core ^ core, links.quarter ^ place, 0, 0)
             )
     whole = whole.reshape(links.col, 4 * part, width)
     a, b = rows[0], rows[0] + rows[1]
@@ -432,26 +479,20 @@
     )
 
 
-def attention_blocks(links, qkv_grad, output_grad, rows):
+def attention_shares(links, qkv_grad, output_grad, rows):
     width = output_grad.shape[1]
     cut = rows[0] * links.col
     parts = [g.reshape(links.col, -1, width) for g in (qkv_grad[:cut], qkv_grad[cut:], output_grad)]
-    whole = jnp.concatenate(parts, axis=1)
-    whole = whole.reshape(links.line, 2, 4, -1, width)
-    whole = jnp.roll(whole, -links.chip, axis=0)
-    return [
-        jnp.stack(
-            [
-                lax.dynamic_slice(
-                    whole,
-                    (0, links.core ^ core, links.quarter ^ place, 0, 0),
-                    (links.line, 1, 1, *whole.shape[3:]),
-                )[:, 0, 0]
-                for place in range(4)
-            ]
-        )
-        for core in range(2)
-    ]
+    whole = jnp.concatenate(parts, axis=1).reshape(links.line, 2, 4, -1, width)
+    return [lax.dynamic_index_in_dim(whole, links.core ^ core, 1, False) for core in range(2)]
+
+
+def ffn_pieces(blocks):
+    if blocks[0].shape[2] % 16 == 0:
+        return blocks
+    line, kinds, _, width = blocks[0].shape
+    joined = [jnp.moveaxis(block, 1, 0).reshape(kinds, -1, width) for block in blocks]
+    return [jnp.concatenate(joined, axis=1)[None]]
 
 
 def rms_pull(value, gain, grad):
@@ -492,48 +533,64 @@
         ffn_part = jnp.stack([gate_weight[layer].T, upward_weight[layer].T, down_weight[layer]])
         attn_part = own_quarter(links, attn_part, 0)
         ffn_part = own_quarter(links, ffn_part, 1)
-        if previous is not None:
-            attn_part = advance(attn_part, previous)
-        attn_move = Transfer(gather_stages(links, attn_part))
-        ffn_part = advance(ffn_part, attn_move)
-        previous = Transfer(gather_stages(links, ffn_part))
-        weights.append((attn_move, previous))
+        weights.append((attn_part, ffn_part))
 
     hidden = inputs[0].astype(jnp.float32)
     saved = []
+    attn_move = Transfer(gather_stages(links, weights[0][0]))
     for layer in range(layers):
-        attn_move, ffn_move = weights[layer]
+        ffn_part = weights[layer][1]
+        if layer == 0:
+            ffn_part = advance(ffn_part, attn_move)
+            ffn_move = Transfer(gather_stages(links, ffn_part))
+            hidden = advance(hidden, attn_move)
+            hidden = advance(hidden, attn_move)
         qkv_w, output_w = attention_weights(links, attn_move.finish(), rows)
         normed = rms_norm(hidden, attn_gains[layer]).astype(jnp.bfloat16)
         raw = dot(normed, qkv_w, NT)
+        raw = advance(raw, ffn_move)
+        if layer + 1 < layers:
+            attn_part, raw = lax.optimization_barrier((weights[layer + 1][0], raw))
+            attn_move = Transfer(gather_stages(links, attn_part))
         qkv, attended, logsum = attention_forward(raw, *where)
         middle = hidden + dot(attended, output_w)
         normed2 = rms_norm(middle, ffn_gains[layer]).astype(jnp.bfloat16)
-        ffn_w = [
-            [jnp.concatenate([block[:, kind].reshape(-1, width) for block in half]) for kind in range(3)]
-            for half in ffn_move.finish()
-        ]
+        normed2 = advance(normed2, ffn_move)
+        if layer + 1 < layers:
+            ffn_part = advance(weights[layer + 1][1], attn_move)
+            next_move = Transfer(gather_stages(links, ffn_part))
+        ffn_w = [ffn_pieces(half) for half in ffn_move.finish()]
+        if layer + 1 < layers:
+            normed2 = advance(normed2, attn_move)
         result, *products = ffn_forward(middle, normed2, *ffn_w)
         saved.append((hidden, normed, qkv, attended, logsum, middle, normed2, products, qkv_w, output_w, ffn_w))
         hidden = result
+        if layer + 1 < layers:
+            hidden = advance(hidden, attn_move)
+            ffn_move = next_move
     final = hidden.astype(jnp.bfloat16)[None]
 
     grad = cotangent[0].astype(jnp.float32)
     moves = [None] * layers
     gain_terms = [None] * layers
     attn_move = ffn_move = None
+
+    def ffn_pick(share, place, part):
+        return jnp.moveaxis(share.reshape(3, 4, links.line, -1, width)[:, place, part], 1, 0)
+
+    def attn_pick(share, place, part):
+        return lax.dynamic_index_in_dim(share[part], links.quarter ^ place, 1, False)
+
     for layer in reversed(range(layers)):
         hidden, normed, qkv, attended, logsum, middle, normed2, products, qkv_w, output_w, ffn_w = saved[layer]
-        before = [] if attn_move is None else [attn_move]
         both = [] if attn_move is None else [ffn_move, attn_move]
         grad_low = grad.astype(jnp.bfloat16)
-        shape = (4, links.line, -1, width)
-        *there, grad_normed = ffn_backward(grad_low, normed2, *products[2:], *ffn_w[1])
+        there, grad_normed = ffn_backward(grad_low, normed2, *products[2:], ffn_w[1])
         here = []
-        new_move = Transfer(scatter_stages(links, here, [g.reshape(shape) for g in there]))
-        grad_normed = advance(grad_normed, *before)
-        *own, grad_normed = ffn_backward(grad_low, normed2, *products[:2], *ffn_w[0], grad_normed)
-        here += [g.reshape(shape) for g in own]
+        new_move = Transfer(scatter_stages(links, here, there, ffn_pick))
+        grad_normed = advance(grad_normed, *both[1:])
+        own, grad_normed = ffn_backward(grad_low, normed2, *products[:2], ffn_w[0], grad_normed)
+        here.append(own)
         grad_normed = advance(grad_normed, new_move, *both)
         pulled, ffn_gain_grad = rms_pull(middle, ffn_gains[layer], grad_normed)
         grad = grad + pulled
@@ -544,9 +601,9 @@
         qkv_grad = attention_backward(qkv, attended_grad, logsum, *where)
         qkv_grad = advance(qkv_grad, new_move, *both)
         qkv_w_grad = dot(qkv_grad, normed, TN).astype(jnp.bfloat16)
-        blocks = attention_blocks(links, qkv_w_grad, output_grad, rows)
+        ours, others = attention_shares(links, qkv_w_grad, output_grad, rows)
         ffn_move = new_move
-        attn_move = Transfer(scatter_stages(links, blocks[:1], blocks[1:]))
+        attn_move = Transfer(scatter_stages(links, [ours], others, attn_pick))
         pulled, attn_gain_grad = rms_pull(hidden, attn_gains[layer], dot(qkv_grad, qkv_w))
         grad = grad + pulled
         if layer:
@@ -557,13 +614,14 @@
     gains = links.sum_all(jnp.stack(gain_terms, axis=1))
     sums = [[] for _ in range(6)]
     for attn_move, ffn_move in moves:
-        total = in_order(links, attn_move.finish()[0]).reshape(-1, width).astype(jnp.float32)
+        total = in_order(links, attn_move.finish()).reshape(-1, width).astype(jnp.float32)
         a, b = rows[0], rows[0] + rows[1]
         sums[0].append(total[:a].T)
         sums[1].append(total[a:b].T)
         sums[2].append(total[b:])
-        for kind, quarters in enumerate(ffn_move.finish()):
-            total = in_order(links, quarters).reshape(-1, width).astype(jnp.float32)
+        quarters = in_order(links, ffn_move.finish())
+        for kind in range(3):
+            total = quarters[:, kind].reshape(-1, width).astype(jnp.float32)
             sums[3 + kind].append(total if kind == 2 else total.T)
     sums = [jnp.stack(values) for values in sums]
     return (final, grad[None], gains[0], *sums[:3], gains[1], *sums[3:])

time: 961 us -> 970 us (level)
  starting transfers between devices: 178 us -> 102 us
  local copies, waits for them, and re-layouts: 118 us -> 173 us
  Pallas kernels: 220 us -> 251 us
  waiting for transfers between devices: 266 us -> 285 us
  other arithmetic: 119 us -> 101 us
    ppermute x48 -> x24, starting transfers between devices: 55.5 us -> 23 us  [y(): return lax.ppermute(value, 'dp', [(i, i ^ 2) for i in range(self.dp)])]
    ppermute x40 -> x20, waiting for transfers between devices: 64.4 us -> 95.9 us  [x(): return lax.ppermute(value, 'dp', [(i, i ^ 1) for i in range(self.dp)])]
    pallas_call x10, Pallas kernels: 220 us -> 251 us  [call(): pl.pallas_call(run, out_shape=outs, in_specs=list(specs) + [pl.BlockSpec(...]
    optimization_barrier x1 -> x4, local copies, waits for them, and re-layouts: 3.25 us -> 30.6 us  [advance(): value, flying = lax.optimization_barrier((value, flying))]
    pallas_call x0 -> x2, local copies, waits for them, and re-layouts: none -> 20.9 us  [call(): pl.pallas_call(run, out_shape=outs, in_specs=list(specs) + [pl.BlockSpec(...]
    ppermute x40 -> x20, starting transfers between devices: 41.3 us -> 20.4 us  [x(): return lax.ppermute(value, 'dp', [(i, i ^ 1) for i in range(self.dp)])]
    ppermute x36 -> x24, starting transfers between devices: 69.5 us -> 49.5 us  [send(): lax.ppermute(value, 'col', [(i, (i + 2 * step) % self.col) for i in range...]
    slice x52 -> x10, local copies, waits for them, and re-layouts: 36.2 us -> 16.6 us  [the longest x4 8.01 us: attention_shares(): qkv_grad[cut:]]
  transfers between devices with their start and end apart: 157 -> 97, of which waited for: 65 -> 37; matrix products, arithmetic and copies ran while one was open for 23% -> 20% of each run, Pallas kernels for 19% -> 19%
where the time goes in v2:
time: 970 us; the launch traced here: 965 us
  waiting for transfers between devices  285 us (29%)
  Pallas kernels  251 us (26%)
  local copies, waits for them, and re-layouts  173 us (18%)
  starting transfers between devices  102 us (11%)
  other arithmetic  101 us (10%)
  matrix products  50.3 us (5%)
    pallas_call x10, Pallas kernels, call(): pl.pallas_call(run, out_shape=outs, in_specs=list(specs) + [pl.BlockSpec(...  251 us
    ppermute x20, waiting for transfers between devices, x(): return lax.ppermute(value, 'dp', [(i, i ^ 1) for i in range(self.dp)])  95.9 us
    ppermute x24, waiting for transfers between devices, send(): lax.ppermute(value, 'col', [(i, (i + 2 * step) % self.col) for i in range...  87 us
    ppermute x24, waiting for transfers between devices, y(): return lax.ppermute(value, 'dp', [(i, i ^ 2) for i in range(self.dp)])  80.5 us
    dot_general x12, matrix products, dot(): lax.dot_general(left, right, (dims, ((), ())), preferred_element_type=jnp...  50.3 us
    ppermute x24, starting transfers between devices, send(): lax.ppermute(value, 'col', [(i, (i + 2 * step) % self.col) for i in range...  49.5 us
    optimization_barrier x4, local copies, waits for them, and re-layouts, advance(): value, flying = lax.optimization_barrier((value, flying))  30.6 us
    unnamed x189, local copies, waits for them, and re-layouts  26.5 us
  transfers between devices with their start and end apart: 97, of which 37 were waited for; matrix products, arithmetic and copies ran while one was open for 20% of the time, Pallas kernels for 19%

profile of v2, /device:TPU:0, one launch (start us, length us, event | category | flops | bytes accessed | tf_op | source)
XLA Modules:
  0.0 964.8 jit_solution(11466136533166775644)
XLA Ops:
  85.0 10.6 %collective-permute-done.13 = bf16[3,80,960]{2,1,0:T(8,128)(2,1)S(1)} collective-permute-done((bf16[3,80,960]{2,1,0:T(8,128)(2,1)S(1)}, bf16[3,80,960]{2,1,0:T(8,128)(2,1)S(1)}, u32[]{:S(2)}, u32[]{:S(2)}) %collective-permute-start.13) | collective-permute-done | bytes 460832 | tf_op jit(solution)/shard_map/ppermute | solution.py:358
  109.7 34.2 %shard_map.186 = (bf16[768,1600]{1,0:T(8,128)(2,1)}, bf16[768,960]{1,0:T(8,128)(2,1)}, f32[16,768]{1,0:T(8,128)}) custom-call(f32[768,1600]{1,0:T(8,128)} %copy.616.refs_0_, f32[768,128]{1,0:T(8,128)} %copy.617.refs_1_.refs_3_, f32[768,128]{1,0:T(8,128)} %copy.618.refs_2_.refs_4_, s32[768,1]{1,0:T(8,128)} %copy.619.refs_3_.refs_5_, s32[1,768]{1,0:T(1,128)} %refs_6_.3), custom_call_target="tpu_custom_call" | custom-call | flops 15000000512 | bytes 15728640 | tf_op jit(solution)/shard_map/pallas_call | solution.py:54
  175.9 24.5 %collective-permute-done.22 = bf16[4,80,960]{2,1,0:T(8,128)(2,1)S(1)} collective-permute-done((bf16[4,80,960]{2,1,0:T(8,128)(2,1)S(1)}, bf16[4,80,960]{2,1,0:T(8,128)(2,1)S(1)}, u32[]{:S(2)}, u32[]{:S(2)}) %collective-permute-start.22) | collective-permute-done | bytes 614432 | tf_op jit(solution)/shard_map/ppermute | solution.py:352
  208.0 23.7 %shard_map.187 = (f32[768,960]{1,0:T(8,128)}, bf16[768,1280]{1,0:T(8,128)(2,1)}, bf16[768,1280]{1,0:T(8,128)(2,1)}, bf16[768,1280]{1,0:T(8,128)(2,1)}, bf16[768,1280]{1,0:T(8,128)(2,1)}) custom-call(f32[768,960]{1,0:T(8,128)} %copy-done.2, bf16[768,960]{1,0:T(8,128)(2,1)} %multiply_convert_fusion.2.refs_1_, bf16[4,3,80,960]{3,2,1,0:T(8,128)(2,1)} %fusion.14.refs_2_.refs_5_, ...), custom_call_target="tpu_custom_call" | custom-call | flops 11000000512 | bytes 31457280 | tf_op jit(solution)/shard_map/pallas_call | solution.py:54
  253.0 13.8 %collective-permute-done.37 = bf16[3,80,960]{2,1,0:T(8,128)(2,1)S(1)} collective-permute-done((bf16[3,80,960]{2,1,0:T(8,128)(2,1)S(1)}, bf16[3,80,960]{2,1,0:T(8,128)(2,1)S(1)}, u32[]{:S(2)}, u32[]{:S(2)}) %collective-permute-start.37) | collective-permute-done | bytes 460832 | tf_op jit(solution)/shard_map/ppermute | solution.py:358
  278.7 23.4 %shard_map.188 = (bf16[768,1600]{1,0:T(8,128)(2,1)}, bf16[768,960]{1,0:T(8,128)(2,1)}, f32[16,768]{1,0:T(8,128)}) custom-call(f32[768,1600]{1,0:T(8,128)} %copy.632.refs_0_, f32[768,128]{1,0:T(8,128)} %copy.617.refs_1_.refs_3_, f32[768,128]{1,0:T(8,128)} %copy.618.refs_2_.refs_4_, s32[768,1]{1,0:T(8,128)} %copy.619.refs_3_.refs_5_, s32[1,768]{1,0:T(1,128)} %refs_6_.3), custom_call_target="tpu_custom_call" | custom-call | flops 15000000512 | bytes 15728640 | tf_op jit(solution)/shard_map/pallas_call | solution.py:54
  319.7 21.7 %collective-permute-done.42.refs_5_.refs_8_ = bf16[2,3,80,960]{3,2,1,0:T(8,128)(2,1)} collective-permute-done((bf16[2,3,80,960]{3,2,1,0:T(8,128)(2,1)S(1)}, bf16[2,3,80,960]{3,2,1,0:T(8,128)(2,1)}, u32[]{:S(2)}, u32[]{:S(2)}) %collective-permute-start.42) | collective-permute-done | bytes 921632 | tf_op jit(solution)/shard_map/ppermute | solution.py:352
  346.2 23.5 %shard_map.189 = (f32[768,960]{1,0:T(8,128)}, bf16[768,1280]{1,0:T(8,128)(2,1)}, bf16[768,1280]{1,0:T(8,128)(2,1)}, bf16[768,1280]{1,0:T(8,128)(2,1)}, bf16[768,1280]{1,0:T(8,128)(2,1)}) custom-call(f32[768,960]{1,0:T(8,128)} %copy-done.4, bf16[768,960]{1,0:T(8,128)(2,1)} %multiply_convert_fusion.refs_1_, bf16[4,3,80,960]{3,2,1,0:T(8,128)(2,1)} %fusion.7.refs_2_.refs_5_, ...), custom_call_target="tpu_custom_call" | custom-call | flops 11000000512 | bytes 31457280 | tf_op jit(solution)/shard_map/pallas_call | solution.py:54
  369.8 23.1 %shard_map.190 = (bf16[3,1280,960]{2,1,0:T(8,128)(2,1)}, f32[768,960]{1,0:T(8,128)}) custom-call(bf16[768,960]{1,0:T(8,128)(2,1)} %bitcast.783, bf16[768,960]{1,0:T(8,128)(2,1)} %multiply_convert_fusion.refs_1_, bf16[768,1280]{1,0:T(8,128)(2,1)} %get-tuple-element.161.refs_2_, bf16[768,1280]{1,0:T(8,128)(2,1)} %get-tuple-element.162.refs_3_, ...), custom_call_target="tpu_custom_call" | custom-call | flops 11000000512 | bytes 31457280 | tf_op jit(solution)/shard_map/pallas_call | solution.py:54
  403.6 24.4 %shard_map.191 = (bf16[3,1280,960]{2,1,0:T(8,128)(2,1)}, f32[768,960]{1,0:T(8,128)}) custom-call(bf16[768,960]{1,0:T(8,128)(2,1)} %bitcast.784, bf16[768,960]{1,0:T(8,128)(2,1)} %multiply_convert_fusion.refs_1_, bf16[768,1280]{1,0:T(8,128)(2,1)} %get-tuple-element.159.refs_2_, bf16[768,1280]{1,0:T(8,128)(2,1)} %get-tuple-element.160.refs_3_, ...), custom_call_target="tpu_custom_call" | custom-call | flops 11000000512 | bytes 31457280 | tf_op jit(solution)/shard_map/pallas_call | solution.py:54
  441.3 10.9 %copy.644 = bf16[3,1280,960]{2,1,0:T(8,128)(2,1)} copy(bf16[3,1280,960]{1,2,0:T(8,128)(2,1)} %collective-permute-done.48) | data formatting | bytes 14745600 | tf_op jit(solution)/shard_map/optimization_barrier | solution.py:396
  462.6 25.2 %shard_map.192 = bf16[768,1600]{1,0:T(8,128)(2,1)} custom-call(bf16[768,1600]{1,0:T(8,128)(2,1)} %get-tuple-element.167.refs_0_, bf16[768,960]{1,0:T(8,128)(2,1)} %copy.639.refs_1_, f32[16,768]{1,0:T(8,128)} %get-tuple-element.168.refs_2_, f32[768,128]{1,0:T(8,128)} %copy.617.refs_1_.refs_3_, f32[768,128]{1,0:T(8,128)} %copy.618.refs_2_.refs_4_, ...), custom_call_target="tpu_custom_call" | custom-call | flops 30000001024 | bytes 20971520 | tf_op jit(solution)/shard_map/pallas_call | solution.py:54
  487.8 16.5 %collective-permute-done.49 = bf16[2,2,3,80,960]{4,3,1,2,0:T(8,128)(2,1)S(1)} collective-permute-done((bf16[2,2,3,80,960]{4,3,1,2,0:T(8,128)(2,1)}, bf16[2,2,3,80,960]{4,3,1,2,0:T(8,128)(2,1)S(1)}, u32[]{:S(2)}, u32[]{:S(2)}) %collective-permute-start.49) | collective-permute-done | bytes 1843232 | tf_op jit(solution)/shard_map/ppermute | solution.py:349
  539.6 15.5 %collective-permute-done.51 = bf16[2,3,80,960]{3,2,0,1:T(8,128)(2,1)S(1)} collective-permute-done((bf16[2,3,80,960]{3,2,0,1:T(8,128)(2,1)S(1)}, bf16[2,3,80,960]{3,2,0,1:T(8,128)(2,1)S(1)}, u32[]{:S(2)}, u32[]{:S(2)}) %collective-permute-start.51) | collective-permute-done | bytes 921632 | tf_op jit(solution)/shard_map/ppermute | solution.py:349
  558.8 23.3 %shard_map.193 = (bf16[3,1280,960]{2,1,0:T(8,128)(2,1)}, f32[768,960]{1,0:T(8,128)}) custom-call(bf16[768,960]{1,0:T(8,128)(2,1)} %convert_element_type.1020.refs_0_, bf16[768,960]{1,0:T(8,128)(2,1)} %multiply_convert_fusion.2.refs_1_, bf16[768,1280]{1,0:T(8,128)(2,1)} %get-tuple-element.177.refs_2_, bf16[768,1280]{1,0:T(8,128)(2,1)} %get-tuple-element.178.refs_3_, ...), custom_call_target="tpu_custom_call" | custom-call | flops 11000000512 | bytes 31457280 | tf_op jit(solution)/shard_map/pallas_call | solution.py:54
  582.1 10.5 %copy.663 = bf16[3,1280,960]{1,2,0:T(8,128)(2,1)} copy(bf16[3,1280,960]{2,1,0:T(8,128)(2,1)} %get-tuple-element.183) | data formatting | bytes 14745600 | tf_op jit(solution)/shard_map/pallas_call | solution.py:54
  624.8 24.3 %shard_map.194 = (bf16[3,1280,960]{2,1,0:T(8,128)(2,1)}, f32[768,960]{1,0:T(8,128)}) custom-call(bf16[768,960]{1,0:T(8,128)(2,1)} %convert_element_type.1020.refs_0_, bf16[768,960]{1,0:T(8,128)(2,1)} %multiply_convert_fusion.2.refs_1_, bf16[768,1280]{1,0:T(8,128)(2,1)} %get-tuple-element.175.refs_2_, bf16[768,1280]{1,0:T(8,128)(2,1)} %get-tuple-element.176.refs_3_, ...), custom_call_target="tpu_custom_call" | custom-call | flops 11000000512 | bytes 31457280 | tf_op jit(solution)/shard_map/pallas_call | solution.py:54
  666.5 18.1 %collective-permute-start.64 = (bf16[80,960]{1,0:T(8,128)(2,1)S(1)}, bf16[80,960]{1,0:T(8,128)(2,1)S(1)}, u32[]{:S(2)}, u32[]{:S(2)}) collective-permute-start(bf16[80,960]{1,0:T(8,128)(2,1)S(1)} %get-tuple-element.368), channel_id=1, source_target_pairs={{0,2},{1,3},{2,4},{3,5},{4,6},{5,7},{6,0},{7,1},{8,10},{9,11},{10,... | collective-permute-start | bytes 460808 | tf_op jit(solution)/shard_map/ppermute | solution.py:358
  689.6 10.7 %copy.672 = bf16[3,1280,960]{2,1,0:T(8,128)(2,1)} copy(bf16[3,1280,960]{1,2,0:T(8,128)(2,1)} %collective-permute-done.56) | data formatting | bytes 14745600 | tf_op jit(solution)/shard_map/optimization_barrier | solution.py:396
  713.7 25.6 %shard_map.195 = bf16[768,1600]{1,0:T(8,128)(2,1)} custom-call(bf16[768,1600]{1,0:T(8,128)(2,1)} %get-tuple-element.189.refs_0_, bf16[768,960]{1,0:T(8,128)(2,1)} %convolution_convert_fusion.4.refs_1_, f32[16,768]{1,0:T(8,128)} %get-tuple-element.196.refs_2_, f32[768,128]{1,0:T(8,128)} %copy.617.refs_1_.refs_3_, f32[768,128]{1,0:T(8,128)} %copy.618.refs_2_.refs_4_, ...), custom_call_target="tpu_custom_call" | custom-call | flops 30000001024 | bytes 20971520 | tf_op jit(solution)/shard_map/pallas_call | solution.py:54
  788.6 19.7 %collective-permute-done.73 = f32[2,2,960]{2,1,0:T(2,128)S(1)} collective-permute-done((f32[2,2,960]{2,1,0:T(2,128)S(1)}, f32[2,2,960]{2,1,0:T(2,128)S(1)}, u32[]{:S(2)}, u32[]{:S(2)}) %collective-permute-start.73) | collective-permute-done | bytes 15392 | tf_op jit(solution)/shard_map/ppermute | solution.py:364
  824.2 15.6 %collective-permute-done.89 = bf16[2,3,80,960]{3,2,0,1:T(8,128)(2,1)} collective-permute-done((bf16[2,3,80,960]{3,2,0,1:T(8,128)(2,1)}, bf16[2,3,80,960]{3,2,0,1:T(8,128)(2,1)}, u32[]{:S(2)}, u32[]{:S(2)}) %collective-permute-start.89) | collective-permute-done | bytes 921632 | tf_op jit(solution)/shard_map/ppermute | solution.py:349
  856.8 31.8 %collective-permute-done.92 = bf16[3,80,960]{2,1,0:T(8,128)(2,1)S(1)} collective-permute-done((bf16[3,80,960]{2,1,0:T(8,128)(2,1)S(1)}, bf16[3,80,960]{2,1,0:T(8,128)(2,1)S(1)}, u32[]{:S(2)}, u32[]{:S(2)}) %collective-permute-start.92) | collective-permute-done | bytes 460832 | tf_op jit(solution)/shard_map/ppermute | solution.py:358
  904.3 10.8 %collective-permute-done.80 = bf16[2,2,80,960]{3,2,1,0:T(8,128)(2,1)S(1)} collective-permute-done((bf16[2,2,80,960]{3,2,1,0:T(8,128)(2,1)S(1)}, bf16[2,2,80,960]{3,2,1,0:T(8,128)(2,1)S(1)}, u32[]{:S(2)}, u32[]{:S(2)}) %collective-permute-start.80) | collective-permute-done | bytes 614432 | tf_op jit(solution)/shard_map/ppermute | solution.py:349
  (556 shorter events, 480.6 us)
Async XLA Ops:
  99.1 61.7 %collective-permute-start.15 = (bf16[4,3,80,960]{3,2,1,0:T(8,128)(2,1)}, bf16[4,3,80,960]{3,2,1,0:T(8,128)(2,1)}, u32[]{:S(2)}, u32[]{:S(2)}) collective-permute-start(bf16[4,3,80,960]{3,2,1,0:T(8,128)(2,1)} %fusion.14.refs_2_.refs_5_), channel_id=1, source_target_pairs={{0,8},{8,0},{16,24},{24,16},{1,9},{9,1},{17,25},{25,17},{2,10},{10... | collective-permute-start | bytes 5529608 | tf_op jit(solution)/shard_map/ppermute | solution.py:349
  99.6 61.1 %collective-permute-start.16 = (bf16[4,3,80,960]{3,2,1,0:T(8,128)(2,1)}, bf16[4,3,80,960]{3,2,1,0:T(8,128)(2,1)}, u32[]{:S(2)}, u32[]{:S(2)}) collective-permute-start(bf16[4,3,80,960]{3,2,1,0:T(8,128)(2,1)} %fusion.14.refs_2_.refs_5_), channel_id=1, source_target_pairs={{0,16},{8,24},{16,0},{24,8},{1,17},{9,25},{17,1},{25,9},{2,18},{10... | collective-permute-start | bytes 5529608 | tf_op jit(solution)/shard_map/ppermute | solution.py:352
  101.1 59.7 %collective-permute-start.17 = (bf16[4,3,80,960]{3,2,1,0:T(8,128)(2,1)}, bf16[4,3,80,960]{3,2,1,0:T(8,128)(2,1)}, u32[]{:S(2)}, u32[]{:S(2)}) collective-permute-start(bf16[4,3,80,960]{3,2,1,0:T(8,128)(2,1)} %fusion.14.refs_2_.refs_5_), channel_id=1, source_target_pairs={{0,1},{1,0},{2,3},{3,2},{4,5},{5,4},{6,7},{7,6},{8,9},{9,8},{10,11... | collective-permute-start | bytes 5529608 | tf_op jit(solution)/shard_map/ppermute | solution.py:355
  101.1 42.8 %collective-permute-start.18 = (bf16[80,960]{1,0:T(8,128)(2,1)S(1)}, bf16[80,960]{1,0:T(8,128)(2,1)S(1)}, u32[]{:S(2)}, u32[]{:S(2)}) collective-permute-start(bf16[80,960]{1,0:T(8,128)(2,1)S(1)} %dynamic-slice_bitcast_fusion.17), channel_id=1, source_target_pairs={{0,6},{1,7},{2,0},{3,1},{4,2},{5,3},{6,4},{7,5},{8,14},{9,15},{10,... | collective-permute-start | bytes 460808 | tf_op jit(solution)/shard_map/ppermute | solution.py:358
  101.1 48.1 %collective-permute-start.19 = (bf16[80,960]{1,0:T(8,128)(2,1)S(1)}, bf16[80,960]{1,0:T(8,128)(2,1)}, u32[]{:S(2)}, u32[]{:S(2)}) collective-permute-start(bf16[80,960]{1,0:T(8,128)(2,1)S(1)} %dynamic-slice_bitcast_fusion.17), channel_id=1, source_target_pairs={{0,4},{1,5},{2,6},{3,7},{4,0},{5,1},{6,2},{7,3},{8,12},{9,13},{10,... | collective-permute-start | bytes 460808 | tf_op jit(solution)/shard_map/ppermute | solution.py:358
  162.1 42.3 %collective-permute-start.26 = (bf16[4,3,80,960]{3,2,1,0:T(8,128)(2,1)}, bf16[4,3,80,960]{3,2,1,0:T(8,128)(2,1)S(1)}, u32[]{:S(2)}, u32[]{:S(2)}) collective-permute-start(bf16[4,3,80,960]{3,2,1,0:T(8,128)(2,1)} %collective-permute-done.15.refs_3_.refs_6_), channel_id=1, source_target_pairs={{0,1},{1,0},{2,3},{3,2},{4,5},{5,4},{6,7},{7,6},{8,9},{9,8},{10,11... | collective-permute-start | bytes 5529608 | tf_op jit(solution)/shard_map/ppermute | solution.py:355
  162.2 42.5 %collective-permute-start.27 = (bf16[4,3,80,960]{3,2,1,0:T(8,128)(2,1)}, bf16[4,3,80,960]{3,2,1,0:T(8,128)(2,1)S(1)}, u32[]{:S(2)}, u32[]{:S(2)}) collective-permute-start(bf16[4,3,80,960]{3,2,1,0:T(8,128)(2,1)} %collective-permute-done.16.refs_4_.refs_7_), channel_id=1, source_target_pairs={{0,1},{1,0},{2,3},{3,2},{4,5},{5,4},{6,7},{7,6},{8,9},{9,8},{10,11... | collective-permute-start | bytes 5529608 | tf_op jit(solution)/shard_map/ppermute | solution.py:355
  162.7 37.8 %collective-permute-start.24 = (bf16[2,3,80,960]{3,2,1,0:T(8,128)(2,1)S(1)}, bf16[2,3,80,960]{3,2,1,0:T(8,128)(2,1)S(1)}, u32[]{:S(2)}, u32[]{:S(2)}) collective-permute-start(bf16[2,3,80,960]{3,2,1,0:T(8,128)(2,1)S(1)} %slice.363), channel_id=1, source_target_pairs={{0,16},{8,24},{16,0},{24,8},{1,17},{9,25},{17,1},{25,9},{2,18},{10... | collective-permute-start | bytes 2764808 | tf_op jit(solution)/shard_map/ppermute | solution.py:352
  202.6 50.5 %collective-permute-start.36 = (bf16[3,80,960]{2,1,0:T(8,128)(2,1)S(1)}, bf16[3,80,960]{2,1,0:T(8,128)(2,1)S(1)}, u32[]{:S(2)}, u32[]{:S(2)}) collective-permute-start(bf16[3,80,960]{2,1,0:T(8,128)(2,1)S(1)} %copy-done.41), channel_id=1, source_target_pairs={{0,6},{1,7},{2,0},{3,1},{4,2},{5,3},{6,4},{7,5},{8,14},{9,15},{10,... | collective-permute-start | bytes 1382408 | tf_op jit(solution)/shard_map/ppermute | solution.py:358
  270.3 44.3 %collective-permute-start.39 = (bf16[4,3,80,960]{3,2,1,0:T(8,128)(2,1)}, bf16[4,3,80,960]{3,2,1,0:T(8,128)(2,1)}, u32[]{:S(2)}, u32[]{:S(2)}) collective-permute-start(bf16[4,3,80,960]{3,2,1,0:T(8,128)(2,1)} %fusion.7.refs_2_.refs_5_), channel_id=1, source_target_pairs={{0,8},{8,0},{16,24},{24,16},{1,9},{9,1},{17,25},{25,17},{2,10},{10... | collective-permute-start | bytes 5529608 | tf_op jit(solution)/shard_map/ppermute | solution.py:349
  271.8 44.0 %collective-permute-start.40 = (bf16[4,3,80,960]{3,2,1,0:T(8,128)(2,1)}, bf16[4,3,80,960]{3,2,1,0:T(8,128)(2,1)}, u32[]{:S(2)}, u32[]{:S(2)}) collective-permute-start(bf16[4,3,80,960]{3,2,1,0:T(8,128)(2,1)} %fusion.7.refs_2_.refs_5_), channel_id=1, source_target_pairs={{0,16},{8,24},{16,0},{24,8},{1,17},{9,25},{17,1},{25,9},{2,18},{10... | collective-permute-start | bytes 5529608 | tf_op jit(solution)/shard_map/ppermute | solution.py:352
  272.4 43.4 %collective-permute-start.41 = (bf16[4,3,80,960]{3,2,1,0:T(8,128)(2,1)}, bf16[4,3,80,960]{3,2,1,0:T(8,128)(2,1)}, u32[]{:S(2)}, u32[]{:S(2)}) collective-permute-start(bf16[4,3,80,960]{3,2,1,0:T(8,128)(2,1)} %fusion.7.refs_2_.refs_5_), channel_id=1, source_target_pairs={{0,1},{1,0},{2,3},{3,2},{4,5},{5,4},{6,7},{7,6},{8,9},{9,8},{10,11... | collective-permute-start | bytes 5529608 | tf_op jit(solution)/shard_map/ppermute | solution.py:355
  459.1 45.2 %collective-permute-start.49 = (bf16[2,2,3,80,960]{4,3,1,2,0:T(8,128)(2,1)}, bf16[2,2,3,80,960]{4,3,1,2,0:T(8,128)(2,1)S(1)}, u32[]{:S(2)}, u32[]{:S(2)}) collective-permute-start(bf16[2,2,3,80,960]{4,3,1,2,0:T(8,128)(2,1)} %pad_maximum_fusion.8), channel_id=1, source_target_pairs={{0,8},{8,0},{16,24},{24,16},{1,9},{9,1},{17,25},{25,17},{2,10},{10... | collective-permute-start | bytes 5529608 | tf_op jit(solution)/shard_map/ppermute | solution.py:349
  461.0 45.0 %collective-permute-start.50 = (bf16[2,2,3,80,960]{4,3,1,2,0:T(8,128)(2,1)}, bf16[2,2,3,80,960]{4,3,1,2,0:T(8,128)(2,1)S(1)}, u32[]{:S(2)}, u32[]{:S(2)}) collective-permute-start(bf16[2,2,3,80,960]{4,3,1,2,0:T(8,128)(2,1)} %pad_maximum_fusion.9), channel_id=1, source_target_pairs={{0,16},{8,24},{16,0},{24,8},{1,17},{9,25},{17,1},{25,9},{2,18},{10... | collective-permute-start | bytes 5529608 | tf_op jit(solution)/shard_map/ppermute | solution.py:352
  592.6 56.6 %collective-permute-start.56 = (bf16[3,1280,960]{1,2,0:T(8,128)(2,1)}, bf16[3,1280,960]{1,2,0:T(8,128)(2,1)}, u32[]{:S(2)}, u32[]{:S(2)}) collective-permute-start(bf16[3,1280,960]{1,2,0:T(8,128)(2,1)} %copy.663), channel_id=1, source_target_pairs={{0,1},{1,0},{2,3},{3,2},{4,5},{5,4},{6,7},{7,6},{8,9},{9,8},{10,11... | collective-permute-start | bytes 22118408 | tf_op jit(solution)/shard_map/ppermute | solution.py:355
  652.9 55.6 %collective-permute-start.62 = (bf16[3,80,960]{2,1,0:T(8,128)(2,1)}, bf16[3,80,960]{2,1,0:T(8,128)(2,1)}, u32[]{:S(2)}, u32[]{:S(2)}) collective-permute-start(bf16[3,80,960]{2,1,0:T(8,128)(2,1)} %get-tuple-element.291), channel_id=1, source_target_pairs={{0,8},{8,0},{16,24},{24,16},{1,9},{9,1},{17,25},{25,17},{2,10},{10... | collective-permute-start | bytes 1382408 | tf_op jit(solution)/shard_map/ppermute | solution.py:349
  654.3 54.2 %collective-permute-start.63 = (bf16[3,80,960]{2,1,0:T(8,128)(2,1)}, bf16[3,80,960]{2,1,0:T(8,128)(2,1)}, u32[]{:S(2)}, u32[]{:S(2)}) collective-permute-start(bf16[3,80,960]{2,1,0:T(8,128)(2,1)} %get-tuple-element.291), channel_id=1, source_target_pairs={{0,16},{8,24},{16,0},{24,8},{1,17},{9,25},{17,1},{25,9},{2,18},{10... | collective-permute-start | bytes 1382408 | tf_op jit(solution)/shard_map/ppermute | solution.py:352
  666.5 40.8 %collective-permute-start.64 = (bf16[80,960]{1,0:T(8,128)(2,1)S(1)}, bf16[80,960]{1,0:T(8,128)(2,1)S(1)}, u32[]{:S(2)}, u32[]{:S(2)}) collective-permute-start(bf16[80,960]{1,0:T(8,128)(2,1)S(1)} %get-tuple-element.368), channel_id=1, source_target_pairs={{0,2},{1,3},{2,4},{3,5},{4,6},{5,7},{6,0},{7,1},{8,10},{9,11},{10,... | collective-permute-start | bytes 460808 | tf_op jit(solution)/shard_map/ppermute | solution.py:358
  707.4 42.6 %collective-permute-start.67 = (bf16[2,2,3,80,960]{4,3,1,2,0:T(8,128)(2,1)S(1)}, bf16[2,2,3,80,960]{4,3,1,2,0:T(8,128)(2,1)}, u32[]{:S(2)}, u32[]{:S(2)}) collective-permute-start(bf16[2,2,3,80,960]{4,3,1,2,0:T(8,128)(2,1)S(1)} %pad_maximum_fusion.10), channel_id=1, source_target_pairs={{0,8},{8,0},{16,24},{24,16},{1,9},{9,1},{17,25},{25,17},{2,10},{10... | collective-permute-start | bytes 5529608 | tf_op jit(solution)/shard_map/ppermute | solution.py:349
  707.9 42.1 %collective-permute-start.68 = (bf16[2,2,3,80,960]{4,3,1,2,0:T(8,128)(2,1)}, bf16[2,2,3,80,960]{4,3,1,2,0:T(8,128)(2,1)S(1)}, u32[]{:S(2)}, u32[]{:S(2)}) collective-permute-start(bf16[2,2,3,80,960]{4,3,1,2,0:T(8,128)(2,1)} %pad_maximum_fusion.11), channel_id=1, source_target_pairs={{0,16},{8,24},{16,0},{24,8},{1,17},{9,25},{17,1},{25,9},{2,18},{10... | collective-permute-start | bytes 5529608 | tf_op jit(solution)/shard_map/ppermute | solution.py:352
  765.8 56.8 %collective-permute-start.88 = (bf16[80,960]{1,0:T(8,128)(2,1)S(1)}, bf16[80,960]{1,0:T(8,128)(2,1)}, u32[]{:S(2)}, u32[]{:S(2)}) collective-permute-start(bf16[80,960]{1,0:T(8,128)(2,1)S(1)} %collective-permute-done.70), channel_id=1, source_target_pairs={{0,16},{8,24},{16,0},{24,8},{1,17},{9,25},{17,1},{25,9},{2,18},{10... | collective-permute-start | bytes 460808 | tf_op jit(solution)/shard_map/ppermute | solution.py:352
  781.4 109.2 %collective-permute-start.77 = (bf16[4,4,80,960]{3,2,0,1:T(8,128)(2,1)}, bf16[4,4,80,960]{3,2,0,1:T(8,128)(2,1)}, u32[]{:S(2)}, u32[]{:S(2)}) collective-permute-start(bf16[4,4,80,960]{3,2,0,1:T(8,128)(2,1)} %copy.686), channel_id=1, source_target_pairs={{0,1},{1,0},{2,3},{3,2},{4,5},{5,4},{6,7},{7,6},{8,9},{9,8},{10,11... | collective-permute-start | bytes 7372808 | tf_op jit(solution)/shard_map/ppermute | solution.py:355
  845.1 43.6 %collective-permute-start.92 = (bf16[3,80,960]{2,1,0:T(8,128)(2,1)S(1)}, bf16[3,80,960]{2,1,0:T(8,128)(2,1)S(1)}, u32[]{:S(2)}, u32[]{:S(2)}) collective-permute-start(bf16[3,80,960]{2,1,0:T(8,128)(2,1)S(1)} %get-tuple-element.349), channel_id=1, source_target_pairs={{0,4},{1,5},{2,6},{3,7},{4,0},{5,1},{6,2},{7,3},{8,12},{9,13},{10,... | collective-permute-start | bytes 1382408 | tf_op jit(solution)/shard_map/ppermute | solution.py:358
  846.5 42.1 %collective-permute-start.91 = (bf16[3,80,960]{2,1,0:T(8,128)(2,1)S(1)}, bf16[3,80,960]{2,1,0:T(8,128)(2,1)S(1)}, u32[]{:S(2)}, u32[]{:S(2)}) collective-permute-start(bf16[3,80,960]{2,1,0:T(8,128)(2,1)S(1)} %get-tuple-element.348), channel_id=1, source_target_pairs={{0,2},{1,3},{2,4},{3,5},{4,6},{5,7},{6,0},{7,1},{8,10},{9,11},{10,... | collective-permute-start | bytes 1382408 | tf_op jit(solution)/shard_map/ppermute | solution.py:358
  (164 other events, 2338.7 us)

commit v3 on v2

--- a/solution.py
+++ b/solution.py
@@ -90,15 +90,24 @@
         bias[index, : high - low, :] = jnp.where((key <= query) & same, 0.0, -1e30)
 
 
-def attention_forward(raw, cosine, sine, seg_col, seg_row, after=()):
-    length, width = raw.shape
+def scale_of(value):
+    return lax.rsqrt(jnp.mean(value * value, axis=-1, keepdims=True) + epsilon)
+
+
+def attention_forward(hidden, gain, next_gain, qkv_w, output_w, cosine, sine, seg_col, seg_row):
+    length, model = hidden.shape
+    width = qkv_w.shape[0]
     q_width = QUERY_HEADS * HEAD_WIDTH
     kv_width = KEY_VALUE_HEADS * HEAD_WIDTH
     group = QUERY_HEADS // KEY_VALUE_HEADS
     rotated = q_width + kv_width
     most = max(high - low for _, low, high in spans(length))
 
-    def body(raw, cosine, sine, seg_col, seg_row, qkv, attended, logsum, bias, turned):
+    def body(hidden, gain, next_gain, qkv_w, output_w, cosine, sine, seg_col, seg_row, *rest):
+        normed, qkv, attended, logsum, middle, normed2, raw, bias, turned = rest
+        value = hidden[...]
+        normed[...] = (value * scale_of(value) * gain[...]).astype(jnp.bfloat16)
+        raw[...] = dot(normed[...], qkv_w[...], NT)
         for lane in range(0, rotated, 128):
             value = raw[:, lane : lane + 128]
             qkv[:, lane : lane + 128] = (value * cosine[...] + swap_halves(value) * sine[...]).astype(jnp.bfloat16)
@@ -121,45 +130,70 @@
                 columns.append(dot(value, expo.astype(jnp.bfloat16)) / total)
                 logsum[head : head + 1, start : start + BLOCK] = peak + jnp.log(total)
             attended[start : start + BLOCK, :] = jnp.concatenate(columns, axis=0).T.astype(jnp.bfloat16)
-
+        value = hidden[...] + dot(attended[...], output_w[...])
+        middle[...] = value
+        normed2[...] = (value * scale_of(value) * next_gain[...]).astype(jnp.bfloat16)
+
+    low = jax.ShapeDtypeStruct((length, model), jnp.bfloat16)
     return call(
         body,
         [
+            low,
             jax.ShapeDtypeStruct((length, width), jnp.bfloat16),
             jax.ShapeDtypeStruct((length, q_width), jnp.bfloat16),
             jax.ShapeDtypeStruct((16, length), jnp.float32),
+            jax.ShapeDtypeStruct((length, model), jnp.float32),
+            low,
         ],
-        [raw, cosine, sine, seg_col, seg_row],
-        after,
-        [
+        [hidden, gain, next_gain, qkv_w, output_w, cosine, sine, seg_col, seg_row],
+        (),
+        [
+            pltpu.VMEM((length, width), jnp.float32),
             pltpu.VMEM((length // BLOCK, most, BLOCK), jnp.float32),
             pltpu.VMEM((kv_width, length), jnp.bfloat16),
         ],
-        flops=15 * 10**9,
-        nbytes=15 * MEGA,
-    )
-
-
-def attention_backward(qkv, grad, logsum, cosine, sine, seg_col, seg_row, after=()):
-    length, width = qkv.shape
+        flops=20 * 10**9,
+        nbytes=20 * MEGA,
+    )
+
+
+def attention_backward(
+    grad, grad_normed2, hidden, normed, qkv, attended, logsum, middle, gain, next_gain, qkv_w, output_w, *where
+):
+    length, model = hidden.shape
+    width = qkv.shape[1]
     q_width = QUERY_HEADS * HEAD_WIDTH
     kv_width = KEY_VALUE_HEADS * HEAD_WIDTH
     group = QUERY_HEADS // KEY_VALUE_HEADS
     rotated = q_width + kv_width
     most = max(high - low for _, low, high in spans(length))
-    scale = 0.125
-
-    def body(qkv, grad, logsum, cosine, sine, seg_col, seg_row, out, bias, turned, key_sum, value_sum, query_sum):
+
+    def body(grad, grad_normed2, hidden, normed, qkv, attended, logsum, middle, gain, next_gain, qkv_w, output_w, *rest):
+        cosine, sine, seg_col, seg_row, *rest = rest
+        qkv_w_grad, output_w_grad, out, out_low, gain_grad, next_gain_grad, *rest = rest
+        bias, turned, key_sum, value_sum, query_sum, upstream_all, qkv_grad = rest
+
+        def pull(value, g, upstream, gain_out):
+            scale = scale_of(value)
+            scaled = value * scale
+            gain_out[...] = jnp.sum(upstream * scaled, axis=0, keepdims=True)
+            pulled = upstream * g
+            return scale * (pulled - scaled * jnp.mean(pulled * scaled, axis=-1, keepdims=True))
+
+        out[...] = grad[...] + pull(middle[...], next_gain[...], grad_normed2[...], next_gain_grad)
+        out_low[...] = out[...].astype(jnp.bfloat16)
+        output_w_grad[...] = dot(attended[...], out_low[...], TN).astype(jnp.bfloat16)
+        upstream_all[...] = dot(out_low[...], output_w[...], NT).astype(jnp.bfloat16)
         fill_bias(bias, seg_col, seg_row, length)
-        turned[...] = qkv[:, q_width:rotated].astype(jnp.float32).T.astype(jnp.bfloat16) * scale
+        turned[...] = qkv[:, q_width:rotated].astype(jnp.float32).T.astype(jnp.bfloat16) * 0.125
         key_sum[...] = jnp.zeros_like(key_sum)
         value_sum[...] = jnp.zeros_like(value_sum)
         for index, (start, low, high) in enumerate(spans(length)):
             for head in range(QUERY_HEADS):
                 kv = head // group
                 lanes = slice(head * HEAD_WIDTH, (head + 1) * HEAD_WIDTH)
-                query = qkv[start : start + BLOCK, lanes] * scale
-                upstream = grad[start : start + BLOCK, lanes]
+                query = qkv[start : start + BLOCK, lanes] * 0.125
+                upstream = upstream_all[start : start + BLOCK, lanes]
                 at = q_width + kv * HEAD_WIDTH
                 key = qkv[low:high, at : at + HEAD_WIDTH]
                 value = qkv[low:high, at + kv_width : at + kv_width + HEAD_WIDTH]
@@ -177,84 +211,100 @@
         raw = jnp.concatenate(raw, axis=1)
         for lane in range(0, rotated, 128):
             value = raw[:, lane : lane + 128]
-            out[:, lane : lane + 128] = (value * cosine[...] - swap_halves(value) * sine[...]).astype(jnp.bfloat16)
-        out[:, rotated:] = jnp.concatenate([value_sum[kv] for kv in range(KEY_VALUE_HEADS)], axis=1).astype(jnp.bfloat16)
-
+            qkv_grad[:, lane : lane + 128] = (value * cosine[...] - swap_halves(value) * sine[...]).astype(jnp.bfloat16)
+        values = [value_sum[kv] for kv in range(KEY_VALUE_HEADS)]
+        qkv_grad[:, rotated:] = jnp.concatenate(values, axis=1).astype(jnp.bfloat16)
+        qkv_w_grad[...] = dot(qkv_grad[...], normed[...], TN).astype(jnp.bfloat16)
+        pulled = pull(hidden[...], gain[...], dot(qkv_grad[...], qkv_w[...]), gain_grad)
+        out[...] += pulled
+        out_low[...] = out[...].astype(jnp.bfloat16)
+
+    gains = jax.ShapeDtypeStruct((1, model), jnp.float32)
+    args = [grad, grad_normed2, hidden, normed, qkv, attended, logsum, middle, gain, next_gain, qkv_w, output_w, *where]
     return call(
         body,
-        [jax.ShapeDtypeStruct((length, width), jnp.bfloat16)],
-        [qkv, grad, logsum, cosine, sine, seg_col, seg_row],
-        after,
+        [
+            jax.ShapeDtypeStruct(qkv_w.shape, jnp.bfloat16),
+            jax.ShapeDtypeStruct(output_w.shape, jnp.bfloat16),
+            jax.ShapeDtypeStruct((length, model), jnp.float32),
+            jax.ShapeDtypeStruct((length, model), jnp.bfloat16),
+            gains,
+            gains,
+        ],
+        args,
+        (),
         [
             pltpu.VMEM((length // BLOCK, most, BLOCK), jnp.float32),
             pltpu.VMEM((kv_width, length), jnp.bfloat16),
             pltpu.VMEM((KEY_VALUE_HEADS, length, HEAD_WIDTH), jnp.float32),
             pltpu.VMEM((KEY_VALUE_HEADS, length, HEAD_WIDTH), jnp.float32),
             pltpu.VMEM((q_width, length), jnp.float32),
+            pltpu.VMEM((length, q_width), jnp.bfloat16),
+            pltpu.VMEM((length, width), jnp.bfloat16),
         ],
-        flops=30 * 10**9,
-        nbytes=20 * MEGA,
-    )[0]
+        flops=35 * 10**9,
+        nbytes=40 * MEGA,
+    )
 
 
 TILE = 256
 
 
+def block_list(pieces):
+    blocks, at = [], 0
+    for piece in pieces:
+        for z in range(piece.shape[0]):
+            blocks.append((piece, z, at, at + piece.shape[2]))
+            at += piece.shape[2]
+    return blocks, at
+
+
 def collect(pieces, store, semaphores):
-    copies = [[], [], []]
-    for kind in range(3):
-        at = 0
-        for piece in pieces:
-            line, _, rows, _ = piece.shape
-            for z in range(line):
-                copies[kind].append(
-                    pltpu.make_async_copy(
-                        piece.at[z, kind], store.at[kind, pl.ds(at, rows)], semaphores.at[kind, len(copies[kind])]
-                    )
-                )
-                at += rows
-    return copies
-
-
-def blocks_of(pieces):
-    return sum(piece.shape[0] for piece in pieces)
-
-
-def units_of(pieces):
-    return sum(piece.shape[0] * piece.shape[2] for piece in pieces)
+    blocks, _ = block_list(pieces)
+    copies = [
+        [
+            pltpu.make_async_copy(piece.at[z, kind], store.at[kind, pl.ds(at, end - at)], semaphores.at[kind, i])
+            for kind in range(3)
+        ]
+        for i, (piece, z, at, end) in enumerate(blocks)
+    ]
+    for block in copies:
+        for copy in block:
+            copy.start()
+    waited = [0]
+
+    def until(limit):
+        while waited[0] < len(blocks) and blocks[waited[0]][2] < limit:
+            for copy in copies[waited[0]]:
+                copy.wait()
+            waited[0] += 1
+
+    return until
 
 
 def ffn_forward(middle, normed, here, there):
     length, width = middle.shape
-    units = units_of(here)
+    blocks, units = block_list(here)
     tile = math.gcd(TILE, units)
 
     def body(middle, normed, *rest):
         pieces = rest[: len(here) + len(there)]
         out, gate_one, up_one, gate_two, up_two, store, semaphores = rest[len(pieces) :]
-        halves = (pieces[: len(here)], pieces[len(here) :])
-        copies = [collect(halves[i], store.at[i], semaphores.at[i]) for i in range(2)]
-        for half in copies:
-            for kind in half:
-                for copy in kind:
-                    copy.start()
+        untils = [
+            collect(half, store.at[i], semaphores.at[i])
+            for i, half in enumerate((pieces[: len(here)], pieces[len(here) :]))
+        ]
         out[...] = middle[...]
         for i, (gate_out, upward_out) in enumerate(((gate_one, up_one), (gate_two, up_two))):
-            for kind in copies[i]:
-                for copy in kind:
-                    copy.wait()
-
-            def step(t, carry, i=i, gate_out=gate_out, upward_out=upward_out):
-                rows = pl.ds(pl.multiple_of(t * tile, tile), tile)
+            for at in range(0, units, tile):
+                untils[i](at + tile)
+                rows = slice(at, at + tile)
                 gate = dot(normed[...], store[i, 0, rows, :], NT)
                 upward = dot(normed[...], store[i, 1, rows, :], NT)
                 gate_out[:, rows] = gate.astype(jnp.bfloat16)
                 upward_out[:, rows] = upward.astype(jnp.bfloat16)
                 active = (gate * jax.nn.sigmoid(gate) * upward).astype(jnp.bfloat16)
                 out[...] += dot(active, store[i, 2, rows, :])
-                return carry
-
-            lax.fori_loop(0, units // tile, step, 0)
 
     low = jax.ShapeDtypeStruct((length, units), jnp.bfloat16)
     return call(
@@ -264,7 +314,7 @@
         (),
         [
             pltpu.VMEM((2, 3, units, width), jnp.bfloat16),
-            pltpu.SemaphoreType.DMA((2, 3, blocks_of(here))),
+            pltpu.SemaphoreType.DMA((2, 3, len(blocks))),
         ],
         in_specs=[pl.BlockSpec(memory_space=pltpu.VMEM)] * 2
         + [pl.BlockSpec(memory_space=pl.ANY)] * (len(here) + len(there)),
@@ -275,24 +325,20 @@
 
 def ffn_backward(grad_low, normed, gate, upward, pieces, earlier=None):
     length, width = normed.shape
-    units = units_of(pieces)
+    blocks, units = block_list(pieces)
+    rows_of_block = blocks[0][3]
     tile = math.gcd(TILE, units)
     before = [] if earlier is None else [earlier]
 
     def body(grad_low, normed, gate, upward, *rest):
         before, rest = rest[: len(rest) - 6 - len(pieces)], rest[len(rest) - 6 - len(pieces) :]
         parts, (grads, out, store, ready, semaphores, sent) = rest[: len(pieces)], rest[len(pieces) :]
-        copies = collect(parts, store, semaphores)
-        for kind in (2, 0, 1):
-            for copy in copies[kind]:
-                copy.start()
+        until = collect(parts, store, semaphores)
         out[...] = before[0][...] if before else jnp.zeros_like(out)
-        for kind in (2, 0, 1):
-            for copy in copies[kind]:
-                copy.wait()
-
-        def step(t, carry):
-            rows = pl.ds(pl.multiple_of(t * tile, tile), tile)
+        sends = []
+        for at in range(0, units, tile):
+            until(at + tile)
+            rows = slice(at, at + tile)
             grad_active = dot(grad_low[...], store[2, rows, :], NT)
             gate_value = gate[:, rows].astype(jnp.float32)
             up_value = upward[:, rows].astype(jnp.float32)
@@ -305,20 +351,25 @@
             ready[0, rows, :] = dot(grad_gate, normed[...], TN).astype(jnp.bfloat16)
             ready[1, rows, :] = dot(grad_up, normed[...], TN).astype(jnp.bfloat16)
             out[...] += dot(grad_gate, store[0, rows, :]) + dot(grad_up, store[1, rows, :])
-            for kind in range(3):
-                pltpu.make_async_copy(ready.at[kind, rows], grads.at[kind, rows], sent.at[kind, t]).start()
-            return carry
-
-        lax.fori_loop(0, units // tile, step, 0)
-        for t in range(units // tile):
-            rows = pl.ds(t * tile, tile)
-            for kind in range(3):
-                pltpu.make_async_copy(ready.at[kind, rows], grads.at[kind, rows], sent.at[kind, t]).wait()
+            while len(sends) < len(blocks) and blocks[len(sends)][3] <= at + tile:
+                i = len(sends)
+                span = pl.ds(blocks[i][2], rows_of_block)
+                sends.append(
+                    [
+                        pltpu.make_async_copy(ready.at[kind, span], grads.at[i, kind], sent.at[kind, i])
+                        for kind in range(3)
+                    ]
+                )
+                for copy in sends[-1]:
+                    copy.start()
+        for block in sends:
+            for copy in block:
+                copy.wait()
 
     return call(
         body,
         [
-            jax.ShapeDtypeStruct((3, units, width), jnp.bfloat16),
+            jax.ShapeDtypeStruct((len(blocks), 3, rows_of_block, width), jnp.bfloat16),
             jax.ShapeDtypeStruct((length, width), jnp.float32),
         ],
         [grad_low, normed, gate, upward, *before, *pieces],
@@ -326,8 +377,8 @@
         [
             pltpu.VMEM((3, units, width), jnp.bfloat16),
             pltpu.VMEM((3, units, width), jnp.bfloat16),
-            pltpu.SemaphoreType.DMA((3, blocks_of(pieces))),
-            pltpu.SemaphoreType.DMA((3, units // tile)),
+            pltpu.SemaphoreType.DMA((3, len(blocks))),
+            pltpu.SemaphoreType.DMA((3, len(blocks))),
         ],
         in_specs=[pl.BlockSpec(memory_space=pltpu.VMEM)] * (4 + len(before))
         + [pl.BlockSpec(memory_space=pl.ANY)] * len(pieces),
@@ -354,6 +405,9 @@
     def other_core(self, value):
         return lax.ppermute(value, "col", [(i, i ^ 1) for i in range(self.col)])
 
+    def both(self, value):
+        return lax.ppermute(value, "dp", [(i, i ^ 3) for i in range(self.dp)])
+
     def send(self, value, step):
         return lax.ppermute(value, "col", [(i, (i + 2 * step) % self.col) for i in range(self.col)])
 
@@ -401,7 +455,7 @@
 
 def gather_stages(links, part):
     far = yield [links.send(part, -step) for step in range(1, links.line)]
-    own = jnp.roll(jnp.stack([part, *far]), links.chip, axis=0)
+    own = jnp.stack([part, *far])
     half = links.line // 2
     from_x, from_y, own_c = yield [links.x(own), links.y(own), links.other_core(own)]
     low, high, x_c, y_c = yield [
@@ -414,7 +468,7 @@
     return [[own, from_x, from_y, low, high], [own_c, x_c, y_c, low_c, high_c]]
 
 
-def scatter_stages(links, kept, there, pick):
+def scatter_stages(links, kept, there, pick, in_line):
     (got,) = yield [links.other_core(there)]
     here = kept[0]
     half = links.line // 2
@@ -439,15 +493,16 @@
     )
 
     def chip(step):
+        if not in_line:
+            return own[step]
         return lax.dynamic_index_in_dim(own, (links.chip + step) % links.line, 0, False)
 
     far = yield [links.send(chip(step), step) for step in range(1, links.line)]
     total = add(chip(0), *far)
     if links.dp > 4:
         total = lax.psum(total, "dp", axis_index_groups=links.rest)
-    at_x, at_y = yield [links.x(total), links.y(total)]
-    (at_both,) = yield [links.y(at_x)]
-    return (total, at_x, at_y, at_both)
+    others = yield [links.x(total), links.y(total), links.both(total)]
+    return (total, *others)
 
 
 def in_order(links, quarters):
@@ -464,13 +519,38 @@
 
 def attention_weights(links, blocks, rows):
     part, width = blocks[0][0].shape[1:]
-    half = links.line // 2
-    whole = jnp.zeros((links.line, 2, 4, part, width), jnp.bfloat16)
-    for core in range(2):
-        for place, start, block in zip((0, 1, 2, 3, 3), (0, 0, 0, 0, half), blocks[core], strict=True):
-            whole = lax.dynamic_update_slice(
-                whole, block[:, None, None], (start, links.core ^ core, links.quarter ^ place, 0, 0)
-            )
+    line = links.line
+    places, starts = (0, 1, 2, 3, 3), (0, 0, 0, 0, line // 2)
+    pieces = blocks[0] + blocks[1]
+    total = sum(piece.shape[0] for piece in pieces)
+
+    def body(*refs):
+        whole, semaphores = refs[len(pieces) :]
+        quarter = lax.axis_index("dp") % 4
+        core = lax.axis_index("col") % 2
+        chip = lax.axis_index("col") // 2
+        copies = []
+        for i, piece in enumerate(refs[: len(pieces)]):
+            side, j = divmod(i, len(places))
+            for z in range(piece.shape[0]):
+                target = whole.at[(chip + starts[j] + z) % line, core ^ side, quarter ^ places[j]]
+                copies.append(pltpu.make_async_copy(piece.at[z], target, semaphores.at[len(copies)]))
+        for copy in copies:
+            copy.start()
+        for copy in copies:
+            copy.wait()
+
+    (whole,) = call(
+        body,
+        [jax.ShapeDtypeStruct((line, 2, 4, part, width), jnp.bfloat16)],
+        pieces,
+        (),
+        [pltpu.SemaphoreType.DMA((total,))],
+        in_specs=[pl.BlockSpec(memory_space=pl.ANY)] * len(pieces),
+        out_specs=[pl.BlockSpec(memory_space=pl.ANY)],
+        limit=16,
+        nbytes=10 * MEGA,
+    )
     whole = whole.reshape(links.col, 4 * part, width)
     a, b = rows[0], rows[0] + rows[1]
     return (
@@ -495,12 +575,10 @@
     return [jnp.concatenate(joined, axis=1)[None]]
 
 
-def rms_pull(value, gain, grad):
-    scale = lax.rsqrt(jnp.mean(value * value, axis=-1, keepdims=True) + epsilon)
-    scaled = value * scale
-    pulled = grad * gain
-    inner = jnp.mean(pulled * scaled, axis=-1, keepdims=True)
-    return scale * (pulled - scaled * inner), jnp.sum(grad * scaled, axis=0)
+def ffn_share(links, grads):
+    if grads.shape[0] == 1:
+        grads = jnp.moveaxis(grads.reshape(3, 4 * links.line, -1, grads.shape[-1]), 0, 1)
+    return grads.reshape(4, links.line, *grads.shape[1:])
 
 
 def per_device(
@@ -536,25 +614,23 @@
         weights.append((attn_part, ffn_part))
 
     hidden = inputs[0].astype(jnp.float32)
+    gains = [(attn_gains[layer][None], ffn_gains[layer][None]) for layer in range(layers)]
     saved = []
     attn_move = Transfer(gather_stages(links, weights[0][0]))
     for layer in range(layers):
-        ffn_part = weights[layer][1]
         if layer == 0:
-            ffn_part = advance(ffn_part, attn_move)
+            ffn_part = advance(weights[0][1], attn_move)
             ffn_move = Transfer(gather_stages(links, ffn_part))
             hidden = advance(hidden, attn_move)
             hidden = advance(hidden, attn_move)
         qkv_w, output_w = attention_weights(links, attn_move.finish(), rows)
-        normed = rms_norm(hidden, attn_gains[layer]).astype(jnp.bfloat16)
-        raw = dot(normed, qkv_w, NT)
-        raw = advance(raw, ffn_move)
+        qkv_w = advance(qkv_w, ffn_move)
         if layer + 1 < layers:
-            attn_part, raw = lax.optimization_barrier((weights[layer + 1][0], raw))
+            attn_part, qkv_w = lax.optimization_barrier((weights[layer + 1][0], qkv_w))
             attn_move = Transfer(gather_stages(links, attn_part))
-        qkv, attended, logsum = attention_forward(raw, *where)
-        middle = hidden + dot(attended, output_w)
-        normed2 = rms_norm(middle, ffn_gains[layer]).astype(jnp.bfloat16)
+        normed, qkv, attended, logsum, middle, normed2 = attention_forward(
+            hidden, *gains[layer], qkv_w, output_w, *where
+        )
         normed2 = advance(normed2, ffn_move)
         if layer + 1 < layers:
             ffn_part = advance(weights[layer + 1][1], attn_move)
@@ -563,55 +639,52 @@
         if layer + 1 < layers:
             normed2 = advance(normed2, attn_move)
         result, *products = ffn_forward(middle, normed2, *ffn_w)
-        saved.append((hidden, normed, qkv, attended, logsum, middle, normed2, products, qkv_w, output_w, ffn_w))
+        saved.append(((hidden, normed, qkv, attended, logsum, middle), normed2, products, (qkv_w, output_w), ffn_w))
         hidden = result
         if layer + 1 < layers:
             hidden = advance(hidden, attn_move)
             ffn_move = next_move
     final = hidden.astype(jnp.bfloat16)[None]
 
-    grad = cotangent[0].astype(jnp.float32)
+    grad_low = cotangent[0]
+    grad = grad_low.astype(jnp.float32)
     moves = [None] * layers
     gain_terms = [None] * layers
     attn_move = ffn_move = None
 
     def ffn_pick(share, place, part):
-        return jnp.moveaxis(share.reshape(3, 4, links.line, -1, width)[:, place, part], 1, 0)
+        return share[place, part]
 
     def attn_pick(share, place, part):
         return lax.dynamic_index_in_dim(share[part], links.quarter ^ place, 1, False)
 
     for layer in reversed(range(layers)):
-        hidden, normed, qkv, attended, logsum, middle, normed2, products, qkv_w, output_w, ffn_w = saved[layer]
+        kept, normed2, products, attn_w, ffn_w = saved[layer]
         both = [] if attn_move is None else [ffn_move, attn_move]
-        grad_low = grad.astype(jnp.bfloat16)
         there, grad_normed = ffn_backward(grad_low, normed2, *products[2:], ffn_w[1])
         here = []
-        new_move = Transfer(scatter_stages(links, here, there, ffn_pick))
-        grad_normed = advance(grad_normed, *both[1:])
+        new_move = Transfer(scatter_stages(links, here, ffn_share(links, there), ffn_pick, False))
+        grad_normed = advance(grad_normed, *both)
         own, grad_normed = ffn_backward(grad_low, normed2, *products[:2], ffn_w[0], grad_normed)
-        here.append(own)
+        here.append(ffn_share(links, own))
         grad_normed = advance(grad_normed, new_move, *both)
-        pulled, ffn_gain_grad = rms_pull(middle, ffn_gains[layer], grad_normed)
-        grad = grad + pulled
-        grad_low = grad.astype(jnp.bfloat16)
-        output_grad = dot(attended, grad_low, TN).astype(jnp.bfloat16)
-        attended_grad = dot(grad_low, output_w, NT).astype(jnp.bfloat16)
-        attended_grad = advance(attended_grad, *both)
-        qkv_grad = attention_backward(qkv, attended_grad, logsum, *where)
-        qkv_grad = advance(qkv_grad, new_move, *both)
-        qkv_w_grad = dot(qkv_grad, normed, TN).astype(jnp.bfloat16)
+        qkv_w_grad, output_grad, grad, grad_low, *gain_grads = attention_backward(
+            grad, grad_normed, *kept, *gains[layer], *attn_w, *where
+        )
         ours, others = attention_shares(links, qkv_w_grad, output_grad, rows)
+        (ours, others) = advance((ours, others), new_move, *both)
         ffn_move = new_move
-        attn_move = Transfer(scatter_stages(links, [ours], others, attn_pick))
-        pulled, attn_gain_grad = rms_pull(hidden, attn_gains[layer], dot(qkv_grad, qkv_w))
-        grad = grad + pulled
+        attn_move = Transfer(scatter_stages(links, [ours], others, attn_pick, True))
         if layer:
-            grad = advance(grad, ffn_move, attn_move)
+            grad_low = advance(grad_low, attn_move)
         moves[layer] = (attn_move, ffn_move)
-        gain_terms[layer] = jnp.stack([attn_gain_grad, ffn_gain_grad])
-
-    gains = links.sum_all(jnp.stack(gain_terms, axis=1))
+        gain_terms[layer] = jnp.stack(gain_grads)
+    advance(None, ffn_move, attn_move)
+    advance(None, attn_move)
+    advance(None, attn_move)
+    advance(None, ffn_move, attn_move)
+
+    gains = links.sum_all(jnp.concatenate(gain_terms, axis=1))
     sums = [[] for _ in range(6)]
     for attn_move, ffn_move in moves:
         total = in_order(links, attn_move.finish()).reshape(-1, width).astype(jnp.float32)

time: 970 us -> 893 us (0.921)
  local copies, waits for them, and re-layouts: 173 us -> 67.5 us
  matrix products: 50.3 us -> 0 us
  waiting for transfers between devices: 285 us -> 331 us
  Pallas kernels: 251 us -> 289 us
  other arithmetic: 101 us -> 78.6 us
  starting transfers between devices: 102 us -> 114 us
    dot_general x12 -> x0, matrix products: 50.3 us -> none  [dot(): lax.dot_general(left, right, (dims, ((), ())), preferred_element_type=jnp...]
    pallas_call x10 -> x12, Pallas kernels: 251 us -> 289 us  [call(): pl.pallas_call(run, out_shape=outs, in_specs=list(specs) + [pl.BlockSpec(...]
    ppermute x24, waiting for transfers between devices: 87 us -> 124 us  [send(): lax.ppermute(value, 'col', [(i, (i + 2 * step) % self.col) for i in range...]
    optimization_barrier x5 -> x0, local copies, waits for them, and re-layouts: 36.8 us -> none  [the longest x4 30.6 us: advance(): value, flying = lax.optimization_barrier((value, flying))]
    pallas_call x2 -> x0, local copies, waits for them, and re-layouts: 20.9 us -> none  [call(): pl.pallas_call(run, out_shape=outs, in_specs=list(specs) + [pl.BlockSpec(...]
    dynamic_update_slice x18 -> x0, local copies, waits for them, and re-layouts: 19.3 us -> none  [attention_weights(): lax.dynamic_update_slice(whole, block[:, None, None], (start, links.core...]
    ppermute x24 -> x20, waiting for transfers between devices: 80.5 us -> 92.1 us  [y(): return lax.ppermute(value, 'dp', [(i, i ^ 2) for i in range(self.dp)])]
    another operation x6 -> x4, other arithmetic: 14.6 us -> 3.03 us  [scatter_stages(): jnp.stack([part(3, low), part(2, low)])]
  transfers between devices with their start and end apart: 97 -> 97, of which waited for: 37 -> 42; matrix products, arithmetic and copies ran while one was open for 20% -> 13% of each run, Pallas kernels for 19% -> 25%
where the time goes in v3:
time: 893 us; the launch traced here: 883 us
  waiting for transfers between devices  331 us (37%)
  Pallas kernels  289 us (32%)
  starting transfers between devices  114 us (13%)
  other arithmetic  78.6 us (9%)
  local copies, waits for them, and re-layouts  67.5 us (8%)
    pallas_call x12, Pallas kernels, call(): pl.pallas_call(run, out_shape=outs, in_specs=list(specs) + [pl.BlockSpec(...  289 us
    ppermute x24, waiting for transfers between devices, send(): lax.ppermute(value, 'col', [(i, (i + 2 * step) % self.col) for i in range...  124 us
    ppermute x20, waiting for transfers between devices, y(): return lax.ppermute(value, 'dp', [(i, i ^ 2) for i in range(self.dp)])  92.1 us
    ppermute x20, waiting for transfers between devices, x(): return lax.ppermute(value, 'dp', [(i, i ^ 1) for i in range(self.dp)])  86.3 us
    ppermute x24, starting transfers between devices, send(): lax.ppermute(value, 'col', [(i, (i + 2 * step) % self.col) for i in range...  51.8 us
    convert_element_type x17, other arithmetic, add(): return total.astype(jnp.bfloat16)  36.9 us
    ppermute x20, starting transfers between devices, y(): return lax.ppermute(value, 'dp', [(i, i ^ 2) for i in range(self.dp)])  19.8 us
    unnamed x101, local copies, waits for them, and re-layouts  18.8 us
  transfers between devices with their start and end apart: 97, of which 42 were waited for; matrix products, arithmetic and copies ran while one was open for 13% of the time, Pallas kernels for 25%

profile of v3, /device:TPU:0, one launch (start us, length us, event | category | flops | bytes accessed | tf_op | source)
XLA Modules:
  0.0 882.6 jit_solution(16753486755578665531)
XLA Ops:
  81.3 30.4 %collective-permute-done.13 = bf16[3,80,960]{2,1,0:T(8,128)(2,1)S(1)} collective-permute-done((bf16[3,80,960]{2,1,0:T(8,128)(2,1)S(1)}, bf16[3,80,960]{2,1,0:T(8,128)(2,1)S(1)}, u32[]{:S(2)}, u32[]{:S(2)}) %collective-permute-start.13) | collective-permute-done | bytes 460832 | tf_op jit(solution)/shard_map/ppermute | solution.py:412
  127.9 28.6 %shard_map.187 = (bf16[768,960]{1,0:T(8,128)(2,1)}, bf16[768,1600]{1,0:T(8,128)(2,1)}, bf16[768,960]{1,0:T(8,128)(2,1)}, f32[16,768]{1,0:T(8,128)}, f32[768,960]{1,0:T(8,128)}, /*index=5*/bf16[768,960]{1,0:T(8,128)(2,1)}) custom-call(f32[768,960]{1,0:T(8,128)} %bitcast_convert_fusion.refs_0_.refs_2_, f32[1,960]{1,0:T(1,128)} %get-tuple-element.384.refs_1_.refs_8_, ...), custom_call_target="tpu_custom_call" | custom-call | flops 20000000000 | bytes 20971520 | tf_op jit(solution)/shard_map/pallas_call | solution.py:54
  175.1 12.0 %collective-permute-done.24.refs_5_.refs_8_ = bf16[2,3,80,960]{3,2,1,0:T(8,128)(2,1)S(1)} collective-permute-done((bf16[2,3,80,960]{3,2,1,0:T(8,128)(2,1)S(1)}, bf16[2,3,80,960]{3,2,1,0:T(8,128)(2,1)S(1)}, u32[]{:S(2)}, u32[]{:S(2)}) %collective-permute-start.24) | collective-permute-done | bytes 921632 | tf_op jit(solution)/shard_map/ppermute | solution.py:403
  205.9 22.4 %shard_map.188 = (f32[768,960]{1,0:T(8,128)}, bf16[768,1280]{1,0:T(8,128)(2,1)}, bf16[768,1280]{1,0:T(8,128)(2,1)}, bf16[768,1280]{1,0:T(8,128)(2,1)}, bf16[768,1280]{1,0:T(8,128)(2,1)}) custom-call(f32[768,960]{1,0:T(8,128)} %get-tuple-element.153.refs_0_.refs_7_, bf16[768,960]{1,0:T(8,128)(2,1)} %get-tuple-element.163.refs_1_, ...), custom_call_target="tpu_custom_call" | custom-call | flops 11000000512 | bytes 31457280 | tf_op jit(solution)/shard_map/pallas_call | solution.py:54
  245.0 29.3 %collective-permute-done.37 = bf16[3,80,960]{2,1,0:T(8,128)(2,1)S(1)} collective-permute-done((bf16[3,80,960]{2,1,0:T(8,128)(2,1)S(1)}, bf16[3,80,960]{2,1,0:T(8,128)(2,1)S(1)}, u32[]{:S(2)}, u32[]{:S(2)}) %collective-permute-start.37) | collective-permute-done | bytes 460832 | tf_op jit(solution)/shard_map/ppermute | solution.py:412
  277.0 28.5 %shard_map.190 = (bf16[768,960]{1,0:T(8,128)(2,1)}, bf16[768,1600]{1,0:T(8,128)(2,1)}, bf16[768,960]{1,0:T(8,128)(2,1)}, f32[16,768]{1,0:T(8,128)}, f32[768,960]{1,0:T(8,128)}, /*index=5*/bf16[768,960]{1,0:T(8,128)(2,1)}) custom-call(f32[768,960]{1,0:T(8,128)} %get-tuple-element.170.refs_0_.refs_2_, f32[1,960]{1,0:T(1,128)} %get-tuple-element.383.refs_1_.refs_8_, ...), custom_call_target="tpu_custom_call" | custom-call | flops 20000000000 | bytes 20971520 | tf_op jit(solution)/shard_map/pallas_call | solution.py:54
  305.5 13.6 %collective-permute-done.39.refs_3_.refs_6_ = bf16[4,3,80,960]{3,2,1,0:T(8,128)(2,1)} collective-permute-done((bf16[4,3,80,960]{3,2,1,0:T(8,128)(2,1)S(1)}, bf16[4,3,80,960]{3,2,1,0:T(8,128)(2,1)}, u32[]{:S(2)}, u32[]{:S(2)}) %collective-permute-start.39) | collective-permute-done | bytes 1843232 | tf_op jit(solution)/shard_map/ppermute | solution.py:400
  325.9 17.8 %collective-permute-done.42.refs_5_.refs_8_ = bf16[2,3,80,960]{3,2,1,0:T(8,128)(2,1)} collective-permute-done((bf16[2,3,80,960]{3,2,1,0:T(8,128)(2,1)S(1)}, bf16[2,3,80,960]{3,2,1,0:T(8,128)(2,1)}, u32[]{:S(2)}, u32[]{:S(2)}) %collective-permute-start.42) | collective-permute-done | bytes 921632 | tf_op jit(solution)/shard_map/ppermute | solution.py:403
  350.6 21.8 %shard_map.191 = (f32[768,960]{1,0:T(8,128)}, bf16[768,1280]{1,0:T(8,128)(2,1)}, bf16[768,1280]{1,0:T(8,128)(2,1)}, bf16[768,1280]{1,0:T(8,128)(2,1)}, bf16[768,1280]{1,0:T(8,128)(2,1)}) custom-call(f32[768,960]{1,0:T(8,128)} %get-tuple-element.178.refs_0_.refs_7_, bf16[768,960]{1,0:T(8,128)(2,1)} %get-tuple-element.183.refs_1_, ...), custom_call_target="tpu_custom_call" | custom-call | flops 11000000512 | bytes 31457280 | tf_op jit(solution)/shard_map/pallas_call | solution.py:54
  372.4 22.0 %shard_map.192 = (bf16[16,3,80,960]{3,2,1,0:T(8,128)(2,1)}, f32[768,960]{1,0:T(8,128)}) custom-call(bf16[768,960]{1,0:T(8,128)(2,1)} %bitcast.370, bf16[768,960]{1,0:T(8,128)(2,1)} %get-tuple-element.183.refs_1_, bf16[768,1280]{1,0:T(8,128)(2,1)} %get-tuple-element.190.refs_2_, bf16[768,1280]{1,0:T(8,128)(2,1)} %get-tuple-element.191.refs_3_, ...), custom_call_target="tpu_custom_call" | custom-call | flops 11000000512 | bytes 31457280 | tf_op jit(solution)/shard_map/pallas_call | solution.py:54
  396.7 23.0 %shard_map.193 = (bf16[16,3,80,960]{3,2,1,0:T(8,128)(2,1)}, f32[768,960]{1,0:T(8,128)}) custom-call(bf16[768,960]{1,0:T(8,128)(2,1)} %bitcast.371, bf16[768,960]{1,0:T(8,128)(2,1)} %get-tuple-element.183.refs_1_, bf16[768,1280]{1,0:T(8,128)(2,1)} %get-tuple-element.188.refs_2_, bf16[768,1280]{1,0:T(8,128)(2,1)} %get-tuple-element.189.refs_3_, ...), custom_call_target="tpu_custom_call" | custom-call | flops 11000000512 | bytes 31457280 | tf_op jit(solution)/shard_map/pallas_call | solution.py:54
  429.8 41.8 %shard_map.194 = (bf16[1600,960]{1,0:T(8,128)(2,1)}, bf16[960,960]{1,0:T(8,128)(2,1)}, f32[768,960]{1,0:T(8,128)}, bf16[768,960]{1,0:T(8,128)(2,1)}, f32[1,960]{1,0:T(1,128)}, /*index=5*/f32[1,960]{1,0:T(1,128)}) custom-call(f32[768,960]{1,0:T(8,128)} %bitcast_convert_fusion.3.refs_0_, f32[768,960]{1,0:T(8,128)} %get-tuple-element.195.refs_1_, ...), custom_call_target="tpu_custom_call" | custom-call | flops 35000000512 | bytes 41943040 | tf_op jit(solution)/shard_map/pallas_call | solution.py:54
  482.8 22.0 %shard_map.195 = (bf16[16,3,80,960]{3,2,1,0:T(8,128)(2,1)}, f32[768,960]{1,0:T(8,128)}) custom-call(bf16[768,960]{1,0:T(8,128)(2,1)} %get-tuple-element.207.refs_0_, bf16[768,960]{1,0:T(8,128)(2,1)} %get-tuple-element.163.refs_1_, bf16[768,1280]{1,0:T(8,128)(2,1)} %get-tuple-element.210.refs_2_, bf16[768,1280]{1,0:T(8,128)(2,1)} %get-tuple-element.211.refs_3_, ...), custom_call_target="tpu_custom_call" | custom-call | flops 11000000512 | bytes 31457280 | tf_op jit(solution)/shard_map/pallas_call | solution.py:54
  523.0 12.3 %collective-permute-done.52 = bf16[2,3,80,960]{3,2,1,0:T(8,128)(2,1)} collective-permute-done((bf16[2,3,80,960]{3,2,1,0:T(8,128)(2,1)}, bf16[2,3,80,960]{3,2,1,0:T(8,128)(2,1)}, u32[]{:S(2)}, u32[]{:S(2)}) %collective-permute-start.52) | collective-permute-done | bytes 921632 | tf_op jit(solution)/shard_map/ppermute | solution.py:400
  536.1 13.2 %collective-permute-done.55 = bf16[2,2,80,960]{3,2,1,0:T(8,128)(2,1)} collective-permute-done((bf16[2,2,80,960]{3,2,1,0:T(8,128)(2,1)S(1)}, bf16[2,2,80,960]{3,2,1,0:T(8,128)(2,1)}, u32[]{:S(2)}, u32[]{:S(2)}) %collective-permute-start.55) | collective-permute-done | bytes 614432 | tf_op jit(solution)/shard_map/ppermute | solution.py:403
  565.2 23.1 %shard_map.196 = (bf16[16,3,80,960]{3,2,1,0:T(8,128)(2,1)}, f32[768,960]{1,0:T(8,128)}) custom-call(bf16[768,960]{1,0:T(8,128)(2,1)} %get-tuple-element.207.refs_0_, bf16[768,960]{1,0:T(8,128)(2,1)} %get-tuple-element.163.refs_1_, bf16[768,1280]{1,0:T(8,128)(2,1)} %get-tuple-element.208.refs_2_, bf16[768,1280]{1,0:T(8,128)(2,1)} %get-tuple-element.209.refs_3_, ...), custom_call_target="tpu_custom_call" | custom-call | flops 11000000512 | bytes 31457280 | tf_op jit(solution)/shard_map/pallas_call | solution.py:54
  603.6 41.8 %shard_map.197 = (bf16[1600,960]{1,0:T(8,128)(2,1)}, bf16[960,960]{1,0:T(8,128)(2,1)}, f32[768,960]{1,0:T(8,128)}, bf16[768,960]{1,0:T(8,128)(2,1)}, f32[1,960]{1,0:T(1,128)}, /*index=5*/f32[1,960]{1,0:T(1,128)}) custom-call(f32[768,960]{1,0:T(8,128)} %get-tuple-element.200.refs_0_, f32[768,960]{1,0:T(8,128)} %get-tuple-element.224.refs_1_, ...), custom_call_target="tpu_custom_call" | custom-call | flops 35000000512 | bytes 41943040 | tf_op jit(solution)/shard_map/pallas_call | solution.py:54
  669.8 11.1 %collective-permute-done.66 = f32[2,2,960]{2,1,0:T(2,128)S(1)} collective-permute-done((f32[2,2,960]{2,1,0:T(2,128)S(1)}, f32[2,2,960]{2,1,0:T(2,128)S(1)}, u32[]{:S(2)}, u32[]{:S(2)}) %collective-permute-start.66) | collective-permute-done | bytes 15392 | tf_op jit(solution)/shard_map/ppermute | solution.py:418
  695.2 9.9 %collective-permute-done.69 = bf16[3,80,960]{2,1,0:T(8,128)(2,1)} collective-permute-done((bf16[3,80,960]{2,1,0:T(8,128)(2,1)}, bf16[3,80,960]{2,1,0:T(8,128)(2,1)}, u32[]{:S(2)}, u32[]{:S(2)}) %collective-permute-start.69) | collective-permute-done | bytes 460832 | tf_op jit(solution)/shard_map/ppermute | solution.py:400
  727.8 17.7 %collective-permute-done.75 = bf16[2,3,80,960]{3,2,1,0:T(8,128)(2,1)S(1)} collective-permute-done((bf16[2,3,80,960]{3,2,1,0:T(8,128)(2,1)S(1)}, bf16[2,3,80,960]{3,2,1,0:T(8,128)(2,1)S(1)}, u32[]{:S(2)}, u32[]{:S(2)}) %collective-permute-start.75) | collective-permute-done | bytes 921632 | tf_op jit(solution)/shard_map/ppermute | solution.py:400
  771.6 11.4 %collective-permute-start.83 = (bf16[3,80,960]{2,1,0:T(8,128)(2,1)S(1)}, bf16[3,80,960]{2,1,0:T(8,128)(2,1)S(1)}, u32[]{:S(2)}, u32[]{:S(2)}) collective-permute-start(bf16[3,80,960]{2,1,0:T(8,128)(2,1)S(1)} %get-tuple-element.361), channel_id=1, source_target_pairs={{0,4},{1,5},{2,6},{3,7},{4,0},{5,1},{6,2},{7,3},{8,12},{9,13},{10,... | collective-permute-start | bytes 1382408 | tf_op jit(solution)/shard_map/ppermute | solution.py:412
  791.7 17.3 %collective-permute-done.83 = bf16[3,80,960]{2,1,0:T(8,128)(2,1)S(1)} collective-permute-done((bf16[3,80,960]{2,1,0:T(8,128)(2,1)S(1)}, bf16[3,80,960]{2,1,0:T(8,128)(2,1)S(1)}, u32[]{:S(2)}, u32[]{:S(2)}) %collective-permute-start.83) | collective-permute-done | bytes 460832 | tf_op jit(solution)/shard_map/ppermute | solution.py:412
  823.2 12.8 %collective-permute-done.86 = bf16[80,960]{1,0:T(8,128)(2,1)S(1)} collective-permute-done((bf16[80,960]{1,0:T(8,128)(2,1)S(1)}, bf16[80,960]{1,0:T(8,128)(2,1)S(1)}, u32[]{:S(2)}, u32[]{:S(2)}) %collective-permute-start.86) | collective-permute-done | bytes 153632 | tf_op jit(solution)/shard_map/ppermute | solution.py:412
  844.7 20.3 %collective-permute-done.89 = bf16[80,960]{1,0:T(8,128)(2,1)S(1)} collective-permute-done((bf16[80,960]{1,0:T(8,128)(2,1)S(1)}, bf16[80,960]{1,0:T(8,128)(2,1)S(1)}, u32[]{:S(2)}, u32[]{:S(2)}) %collective-permute-start.89) | collective-permute-done | bytes 153632 | tf_op jit(solution)/shard_map/ppermute | solution.py:403
  (418 shorter events, 376.3 us)
Async XLA Ops:
  66.2 45.5 %collective-permute-start.13 = (bf16[3,80,960]{2,1,0:T(8,128)(2,1)S(1)}, bf16[3,80,960]{2,1,0:T(8,128)(2,1)S(1)}, u32[]{:S(2)}, u32[]{:S(2)}) collective-permute-start(bf16[3,80,960]{2,1,0:T(8,128)(2,1)S(1)} %copy-done.20), channel_id=1, source_target_pairs={{0,4},{1,5},{2,6},{3,7},{4,0},{5,1},{6,2},{7,3},{8,12},{9,13},{10,... | collective-permute-start | bytes 1382408 | tf_op jit(solution)/shard_map/ppermute | solution.py:412
  68.7 43.1 %collective-permute-start.14 = (bf16[3,80,960]{2,1,0:T(8,128)(2,1)S(1)}, bf16[3,80,960]{2,1,0:T(8,128)(2,1)S(1)}, u32[]{:S(2)}, u32[]{:S(2)}) collective-permute-start(bf16[3,80,960]{2,1,0:T(8,128)(2,1)S(1)} %copy-done.20), channel_id=1, source_target_pairs={{0,2},{1,3},{2,4},{3,5},{4,6},{5,7},{6,0},{7,1},{8,10},{9,11},{10,... | collective-permute-start | bytes 1382408 | tf_op jit(solution)/shard_map/ppermute | solution.py:412
  114.7 45.9 %collective-permute-start.15 = (bf16[4,3,80,960]{3,2,1,0:T(8,128)(2,1)S(1)}, bf16[4,3,80,960]{3,2,1,0:T(8,128)(2,1)}, u32[]{:S(2)}, u32[]{:S(2)}) collective-permute-start(bf16[4,3,80,960]{3,2,1,0:T(8,128)(2,1)S(1)} %pad_maximum_fusion.4.refs_2_.refs_5_), channel_id=1, source_target_pairs={{0,8},{8,0},{16,24},{24,16},{1,9},{9,1},{17,25},{25,17},{2,10},{10... | collective-permute-start | bytes 5529608 | tf_op jit(solution)/shard_map/ppermute | solution.py:400
  115.3 45.3 %collective-permute-start.16 = (bf16[4,3,80,960]{3,2,1,0:T(8,128)(2,1)S(1)}, bf16[4,3,80,960]{3,2,1,0:T(8,128)(2,1)}, u32[]{:S(2)}, u32[]{:S(2)}) collective-permute-start(bf16[4,3,80,960]{3,2,1,0:T(8,128)(2,1)S(1)} %pad_maximum_fusion.4.refs_2_.refs_5_), channel_id=1, source_target_pairs={{0,16},{8,24},{16,0},{24,8},{1,17},{9,25},{17,1},{25,9},{2,18},{10... | collective-permute-start | bytes 5529608 | tf_op jit(solution)/shard_map/ppermute | solution.py:403
  118.4 42.2 %collective-permute-start.17 = (bf16[4,3,80,960]{3,2,1,0:T(8,128)(2,1)S(1)}, bf16[4,3,80,960]{3,2,1,0:T(8,128)(2,1)}, u32[]{:S(2)}, u32[]{:S(2)}) collective-permute-start(bf16[4,3,80,960]{3,2,1,0:T(8,128)(2,1)S(1)} %pad_maximum_fusion.4.refs_2_.refs_5_), channel_id=1, source_target_pairs={{0,1},{1,0},{2,3},{3,2},{4,5},{5,4},{6,7},{7,6},{8,9},{9,8},{10,11... | collective-permute-start | bytes 5529608 | tf_op jit(solution)/shard_map/ppermute | solution.py:406
  127.3 47.3 %collective-permute-start.21 = (bf16[4,80,960]{2,1,0:T(8,128)(2,1)S(1)}, bf16[4,80,960]{2,1,0:T(8,128)(2,1)S(1)}, u32[]{:S(2)}, u32[]{:S(2)}) collective-permute-start(bf16[4,80,960]{2,1,0:T(8,128)(2,1)S(1)} %pad_maximum_fusion.15.refs_0_), channel_id=1, source_target_pairs={{0,8},{8,0},{16,24},{24,16},{1,9},{9,1},{17,25},{25,17},{2,10},{10... | collective-permute-start | bytes 1843208 | tf_op jit(solution)/shard_map/ppermute | solution.py:400
  161.9 40.7 %collective-permute-start.26 = (bf16[4,3,80,960]{3,2,1,0:T(8,128)(2,1)}, bf16[4,3,80,960]{3,2,1,0:T(8,128)(2,1)S(1)}, u32[]{:S(2)}, u32[]{:S(2)}) collective-permute-start(bf16[4,3,80,960]{3,2,1,0:T(8,128)(2,1)} %collective-permute-done.15.refs_3_.refs_6_), channel_id=1, source_target_pairs={{0,1},{1,0},{2,3},{3,2},{4,5},{5,4},{6,7},{7,6},{8,9},{9,8},{10,11... | collective-permute-start | bytes 5529608 | tf_op jit(solution)/shard_map/ppermute | solution.py:406
  162.0 41.1 %collective-permute-start.27 = (bf16[4,3,80,960]{3,2,1,0:T(8,128)(2,1)}, bf16[4,3,80,960]{3,2,1,0:T(8,128)(2,1)S(1)}, u32[]{:S(2)}, u32[]{:S(2)}) collective-permute-start(bf16[4,3,80,960]{3,2,1,0:T(8,128)(2,1)} %collective-permute-done.16.refs_4_.refs_7_), channel_id=1, source_target_pairs={{0,1},{1,0},{2,3},{3,2},{4,5},{5,4},{6,7},{7,6},{8,9},{9,8},{10,11... | collective-permute-start | bytes 5529608 | tf_op jit(solution)/shard_map/ppermute | solution.py:406
  230.7 43.6 %collective-permute-start.37 = (bf16[3,80,960]{2,1,0:T(8,128)(2,1)S(1)}, bf16[3,80,960]{2,1,0:T(8,128)(2,1)S(1)}, u32[]{:S(2)}, u32[]{:S(2)}) collective-permute-start(bf16[3,80,960]{2,1,0:T(8,128)(2,1)S(1)} %copy-done.19), channel_id=1, source_target_pairs={{0,4},{1,5},{2,6},{3,7},{4,0},{5,1},{6,2},{7,3},{8,12},{9,13},{10,... | collective-permute-start | bytes 1382408 | tf_op jit(solution)/shard_map/ppermute | solution.py:412
  231.3 43.1 %collective-permute-start.38 = (bf16[3,80,960]{2,1,0:T(8,128)(2,1)S(1)}, bf16[3,80,960]{2,1,0:T(8,128)(2,1)S(1)}, u32[]{:S(2)}, u32[]{:S(2)}) collective-permute-start(bf16[3,80,960]{2,1,0:T(8,128)(2,1)S(1)} %copy-done.19), channel_id=1, source_target_pairs={{0,2},{1,3},{2,4},{3,5},{4,6},{5,7},{6,0},{7,1},{8,10},{9,11},{10,... | collective-permute-start | bytes 1382408 | tf_op jit(solution)/shard_map/ppermute | solution.py:412
  274.6 44.5 %collective-permute-start.39 = (bf16[4,3,80,960]{3,2,1,0:T(8,128)(2,1)S(1)}, bf16[4,3,80,960]{3,2,1,0:T(8,128)(2,1)}, u32[]{:S(2)}, u32[]{:S(2)}) collective-permute-start(bf16[4,3,80,960]{3,2,1,0:T(8,128)(2,1)S(1)} %pad_maximum_fusion.5.refs_2_.refs_5_), channel_id=1, source_target_pairs={{0,8},{8,0},{16,24},{24,16},{1,9},{9,1},{17,25},{25,17},{2,10},{10... | collective-permute-start | bytes 5529608 | tf_op jit(solution)/shard_map/ppermute | solution.py:400
  275.5 44.1 %collective-permute-start.40 = (bf16[4,3,80,960]{3,2,1,0:T(8,128)(2,1)S(1)}, bf16[4,3,80,960]{3,2,1,0:T(8,128)(2,1)}, u32[]{:S(2)}, u32[]{:S(2)}) collective-permute-start(bf16[4,3,80,960]{3,2,1,0:T(8,128)(2,1)S(1)} %pad_maximum_fusion.5.refs_2_.refs_5_), channel_id=1, source_target_pairs={{0,16},{8,24},{16,0},{24,8},{1,17},{9,25},{17,1},{25,9},{2,18},{10... | collective-permute-start | bytes 5529608 | tf_op jit(solution)/shard_map/ppermute | solution.py:403
  277.0 42.6 %collective-permute-start.41 = (bf16[4,3,80,960]{3,2,1,0:T(8,128)(2,1)S(1)}, bf16[4,3,80,960]{3,2,1,0:T(8,128)(2,1)S(1)}, u32[]{:S(2)}, u32[]{:S(2)}) collective-permute-start(bf16[4,3,80,960]{3,2,1,0:T(8,128)(2,1)S(1)} %pad_maximum_fusion.5.refs_2_.refs_5_), channel_id=1, source_target_pairs={{0,1},{1,0},{2,3},{3,2},{4,5},{5,4},{6,7},{7,6},{8,9},{9,8},{10,11... | collective-permute-start | bytes 5529608 | tf_op jit(solution)/shard_map/ppermute | solution.py:406
  426.5 51.2 %collective-permute-start.50 = (bf16[2,2,3,80,960]{4,3,2,1,0:T(8,128)(2,1)}, bf16[2,2,3,80,960]{4,3,2,1,0:T(8,128)(2,1)}, u32[]{:S(2)}, u32[]{:S(2)}) collective-permute-start(bf16[2,2,3,80,960]{4,3,2,1,0:T(8,128)(2,1)} %pad_maximum_fusion.7), channel_id=1, source_target_pairs={{0,16},{8,24},{16,0},{24,8},{1,17},{9,25},{17,1},{25,9},{2,18},{10... | collective-permute-start | bytes 5529608 | tf_op jit(solution)/shard_map/ppermute | solution.py:403
  428.5 49.2 %collective-permute-start.49 = (bf16[2,2,3,80,960]{4,3,2,1,0:T(8,128)(2,1)}, bf16[2,2,3,80,960]{4,3,2,1,0:T(8,128)(2,1)}, u32[]{:S(2)}, u32[]{:S(2)}) collective-permute-start(bf16[2,2,3,80,960]{4,3,2,1,0:T(8,128)(2,1)} %pad_maximum_fusion.6), channel_id=1, source_target_pairs={{0,8},{8,0},{16,24},{24,16},{1,9},{9,1},{17,25},{25,17},{2,10},{10... | collective-permute-start | bytes 5529608 | tf_op jit(solution)/shard_map/ppermute | solution.py:400
  504.8 90.4 %collective-permute-start.56 = (bf16[4,4,3,80,960]{4,3,2,1,0:T(8,128)(2,1)}, bf16[4,4,3,80,960]{4,3,2,1,0:T(8,128)(2,1)}, u32[]{:S(2)}, u32[]{:S(2)}) collective-permute-start(bf16[4,4,3,80,960]{4,3,2,1,0:T(8,128)(2,1)} %bitcast.432), channel_id=1, source_target_pairs={{0,1},{1,0},{2,3},{3,2},{4,5},{5,4},{6,7},{7,6},{8,9},{9,8},{10,11... | collective-permute-start | bytes 22118408 | tf_op jit(solution)/shard_map/ppermute | solution.py:406
  553.4 34.9 %collective-permute-start.60 = (bf16[2,80,960]{2,1,0:T(8,128)(2,1)S(1)}, bf16[2,80,960]{2,1,0:T(8,128)(2,1)S(1)}, u32[]{:S(2)}, u32[]{:S(2)}) collective-permute-start(bf16[2,80,960]{2,1,0:T(8,128)(2,1)S(1)} %fusion.25), channel_id=1, source_target_pairs={{0,8},{8,0},{16,24},{24,16},{1,9},{9,1},{17,25},{25,17},{2,10},{10... | collective-permute-start | bytes 921608 | tf_op jit(solution)/shard_map/ppermute | solution.py:400
  602.8 109.6 %collective-permute-start.68 = (bf16[2,2,3,80,960]{4,3,2,1,0:T(8,128)(2,1)}, bf16[2,2,3,80,960]{4,3,2,1,0:T(8,128)(2,1)}, u32[]{:S(2)}, u32[]{:S(2)}) collective-permute-start(bf16[2,2,3,80,960]{4,3,2,1,0:T(8,128)(2,1)} %pad_maximum_fusion.9), channel_id=1, source_target_pairs={{0,16},{8,24},{16,0},{24,8},{1,17},{9,25},{17,1},{25,9},{2,18},{10... | collective-permute-start | bytes 5529608 | tf_op jit(solution)/shard_map/ppermute | solution.py:403
  648.5 64.0 %collective-permute-start.67 = (bf16[2,2,3,80,960]{4,3,2,1,0:T(8,128)(2,1)}, bf16[2,2,3,80,960]{4,3,2,1,0:T(8,128)(2,1)}, u32[]{:S(2)}, u32[]{:S(2)}) collective-permute-start(bf16[2,2,3,80,960]{4,3,2,1,0:T(8,128)(2,1)} %pad_maximum_fusion.8), channel_id=1, source_target_pairs={{0,8},{8,0},{16,24},{24,16},{1,9},{9,1},{17,25},{25,17},{2,10},{10... | collective-permute-start | bytes 5529608 | tf_op jit(solution)/shard_map/ppermute | solution.py:400
  771.6 37.4 %collective-permute-start.83 = (bf16[3,80,960]{2,1,0:T(8,128)(2,1)S(1)}, bf16[3,80,960]{2,1,0:T(8,128)(2,1)S(1)}, u32[]{:S(2)}, u32[]{:S(2)}) collective-permute-start(bf16[3,80,960]{2,1,0:T(8,128)(2,1)S(1)} %get-tuple-element.361), channel_id=1, source_target_pairs={{0,4},{1,5},{2,6},{3,7},{4,0},{5,1},{6,2},{7,3},{8,12},{9,13},{10,... | collective-permute-start | bytes 1382408 | tf_op jit(solution)/shard_map/ppermute | solution.py:412
  783.0 34.8 %collective-permute-start.84 = (bf16[3,80,960]{2,1,0:T(8,128)(2,1)S(1)}, bf16[3,80,960]{2,1,0:T(8,128)(2,1)S(1)}, u32[]{:S(2)}, u32[]{:S(2)}) collective-permute-start(bf16[3,80,960]{2,1,0:T(8,128)(2,1)S(1)} %get-tuple-element.360), channel_id=1, source_target_pairs={{0,6},{1,7},{2,0},{3,1},{4,2},{5,3},{6,4},{7,5},{8,14},{9,15},{10,... | collective-permute-start | bytes 1382408 | tf_op jit(solution)/shard_map/ppermute | solution.py:412
  787.3 35.9 %collective-permute-start.85 = (bf16[80,960]{1,0:T(8,128)(2,1)S(1)}, bf16[80,960]{1,0:T(8,128)(2,1)S(1)}, u32[]{:S(2)}, u32[]{:S(2)}) collective-permute-start(bf16[80,960]{1,0:T(8,128)(2,1)S(1)} %get-tuple-element.365), channel_id=1, source_target_pairs={{0,2},{1,3},{2,4},{3,5},{4,6},{5,7},{6,0},{7,1},{8,10},{9,11},{10,... | collective-permute-start | bytes 460808 | tf_op jit(solution)/shard_map/ppermute | solution.py:412
  791.1 44.9 %collective-permute-start.86 = (bf16[80,960]{1,0:T(8,128)(2,1)S(1)}, bf16[80,960]{1,0:T(8,128)(2,1)S(1)}, u32[]{:S(2)}, u32[]{:S(2)}) collective-permute-start(bf16[80,960]{1,0:T(8,128)(2,1)S(1)} %get-tuple-element.366), channel_id=1, source_target_pairs={{0,4},{1,5},{2,6},{3,7},{4,0},{5,1},{6,2},{7,3},{8,12},{9,13},{10,... | collective-permute-start | bytes 460808 | tf_op jit(solution)/shard_map/ppermute | solution.py:412
  840.2 34.7 %collective-permute-start.96 = (bf16[3,80,960]{2,1,0:T(8,128)(2,1)}, bf16[3,80,960]{2,1,0:T(8,128)(2,1)}, u32[]{:S(2)}, u32[]{:S(2)}) collective-permute-start(bf16[3,80,960]{2,1,0:T(8,128)(2,1)} %get-tuple-element.297), channel_id=1, source_target_pairs={{0,24},{8,16},{16,8},{24,0},{1,25},{9,17},{17,9},{25,1},{2,26},{10... | collective-permute-start | bytes 1382408 | tf_op jit(solution)/shard_map/ppermute | solution.py:409
  (120 other events, 1755.4 us)

commit v4 on v3

--- a/solution.py
+++ b/solution.py
@@ -518,7 +518,7 @@
 
 
 def attention_weights(links, blocks, rows):
-    part, width = blocks[0][0].shape[1:]
+    part, width = blocks[0][0].shape[2:]
     line = links.line
     places, starts = (0, 1, 2, 3, 3), (0, 0, 0, 0, line // 2)
     pieces = blocks[0] + blocks[1]
@@ -534,7 +534,7 @@
             side, j = divmod(i, len(places))
             for z in range(piece.shape[0]):
                 target = whole.at[(chip + starts[j] + z) % line, core ^ side, quarter ^ places[j]]
-                copies.append(pltpu.make_async_copy(piece.at[z], target, semaphores.at[len(copies)]))
+                copies.append(pltpu.make_async_copy(piece.at[z, 3], target, semaphores.at[len(copies)]))
         for copy in copies:
             copy.start()
         for copy in copies:
@@ -570,8 +570,8 @@
 def ffn_pieces(blocks):
     if blocks[0].shape[2] % 16 == 0:
         return blocks
-    line, kinds, _, width = blocks[0].shape
-    joined = [jnp.moveaxis(block, 1, 0).reshape(kinds, -1, width) for block in blocks]
+    width = blocks[0].shape[-1]
+    joined = [jnp.moveaxis(block[:, :3], 1, 0).reshape(3, -1, width) for block in blocks]
     return [jnp.concatenate(joined, axis=1)[None]]
 
 
@@ -604,46 +604,37 @@
     attn_gains = attn_gain.astype(jnp.float32)
     ffn_gains = ffn_gain.astype(jnp.float32)
 
-    weights = []
-    previous = None
+    parts = []
     for layer in range(layers):
         attn_part = jnp.concatenate([query_weight[layer].T, key_value_weight[layer].T, output_weight[layer]])
         ffn_part = jnp.stack([gate_weight[layer].T, upward_weight[layer].T, down_weight[layer]])
-        attn_part = own_quarter(links, attn_part, 0)
-        ffn_part = own_quarter(links, ffn_part, 1)
-        weights.append((attn_part, ffn_part))
+        parts.append(
+            jnp.concatenate([own_quarter(links, ffn_part, 1), own_quarter(links, attn_part, 0)[None]])
+        )
 
     hidden = inputs[0].astype(jnp.float32)
     gains = [(attn_gains[layer][None], ffn_gains[layer][None]) for layer in range(layers)]
     saved = []
-    attn_move = Transfer(gather_stages(links, weights[0][0]))
+    move = Transfer(gather_stages(links, parts[0]))
     for layer in range(layers):
-        if layer == 0:
-            ffn_part = advance(weights[0][1], attn_move)
-            ffn_move = Transfer(gather_stages(links, ffn_part))
-            hidden = advance(hidden, attn_move)
-            hidden = advance(hidden, attn_move)
-        qkv_w, output_w = attention_weights(links, attn_move.finish(), rows)
-        qkv_w = advance(qkv_w, ffn_move)
+        later = []
         if layer + 1 < layers:
-            attn_part, qkv_w = lax.optimization_barrier((weights[layer + 1][0], qkv_w))
-            attn_move = Transfer(gather_stages(links, attn_part))
+            part = advance(parts[layer + 1], move)
+            later = [Transfer(gather_stages(links, part))]
+        advance(None, move)
+        hidden = advance(hidden, move, *later)
+        blocks = move.finish()
+        qkv_w, output_w = attention_weights(links, blocks, rows)
+        ffn_w = [ffn_pieces(half) for half in blocks]
         normed, qkv, attended, logsum, middle, normed2 = attention_forward(
             hidden, *gains[layer], qkv_w, output_w, *where
         )
-        normed2 = advance(normed2, ffn_move)
-        if layer + 1 < layers:
-            ffn_part = advance(weights[layer + 1][1], attn_move)
-            next_move = Transfer(gather_stages(links, ffn_part))
-        ffn_w = [ffn_pieces(half) for half in ffn_move.finish()]
-        if layer + 1 < layers:
-            normed2 = advance(normed2, attn_move)
         result, *products = ffn_forward(middle, normed2, *ffn_w)
         saved.append(((hidden, normed, qkv, attended, logsum, middle), normed2, products, (qkv_w, output_w), ffn_w))
         hidden = result
-        if layer + 1 < layers:
-            hidden = advance(hidden, attn_move)
-            ffn_move = next_move
+        if later:
+            hidden = advance(hidden, *later)
+            move = later[0]
     final = hidden.astype(jnp.bfloat16)[None]
 
     grad_low = cotangent[0]
@@ -660,31 +651,31 @@
 
     for layer in reversed(range(layers)):
         kept, normed2, products, attn_w, ffn_w = saved[layer]
-        both = [] if attn_move is None else [ffn_move, attn_move]
+        last_ffn = [] if ffn_move is None else [ffn_move]
+        last_attn = [] if attn_move is None else [attn_move]
         there, grad_normed = ffn_backward(grad_low, normed2, *products[2:], ffn_w[1])
+        there, grad_normed = advance((there, grad_normed), *last_ffn, *last_attn)
         here = []
         new_move = Transfer(scatter_stages(links, here, ffn_share(links, there), ffn_pick, False))
-        grad_normed = advance(grad_normed, *both)
         own, grad_normed = ffn_backward(grad_low, normed2, *products[:2], ffn_w[0], grad_normed)
+        own, grad_normed, *new_move.flying = advance((own, grad_normed, *new_move.flying), *last_attn)
         here.append(ffn_share(links, own))
-        grad_normed = advance(grad_normed, new_move, *both)
-        qkv_w_grad, output_grad, grad, grad_low, *gain_grads = attention_backward(
-            grad, grad_normed, *kept, *gains[layer], *attn_w, *where
+        new_move.advance()
+        results = attention_backward(grad, grad_normed, *kept, *gains[layer], *attn_w, *where)
+        results = advance(results, new_move, *last_ffn, *last_attn)
+        qkv_w_grad, output_grad, grad, grad_low, *gain_grads = results
+        ours, others = attention_shares(links, qkv_w_grad, output_grad, rows)
+        moves[layer] = (attn_move, ffn_move) = (
+            Transfer(scatter_stages(links, [ours], others, attn_pick, True)),
+            new_move,
         )
-        ours, others = attention_shares(links, qkv_w_grad, output_grad, rows)
-        (ours, others) = advance((ours, others), new_move, *both)
-        ffn_move = new_move
-        attn_move = Transfer(scatter_stages(links, [ours], others, attn_pick, True))
-        if layer:
-            grad_low = advance(grad_low, attn_move)
-        moves[layer] = (attn_move, ffn_move)
         gain_terms[layer] = jnp.stack(gain_grads)
+    gain_terms = jnp.concatenate(gain_terms, axis=1)
+    gain_terms = advance(gain_terms, ffn_move, attn_move)
+    gain_terms = advance(gain_terms, attn_move, *last_ffn, *last_attn)
+    gain_terms = advance(gain_terms, attn_move)
+    gains = links.sum_all(gain_terms)
     advance(None, ffn_move, attn_move)
-    advance(None, attn_move)
-    advance(None, attn_move)
-    advance(None, ffn_move, attn_move)
-
-    gains = links.sum_all(jnp.concatenate(gain_terms, axis=1))
     sums = [[] for _ in range(6)]
     for attn_move, ffn_move in moves:
         total = in_order(links, attn_move.finish()).reshape(-1, width).astype(jnp.float32)

time: 893 us -> 801 us (0.90)
  waiting for transfers between devices: 331 us -> 261 us
  starting transfers between devices: 114 us -> 94.8 us
  local copies, waits for them, and re-layouts: 67.5 us -> 78.8 us
    ppermute x20 -> x16, waiting for transfers between devices: 92.1 us -> 57.4 us  [y(): return lax.ppermute(value, 'dp', [(i, i ^ 2) for i in range(self.dp)])]
    ppermute x24 -> x18, waiting for transfers between devices: 124 us -> 110 us  [send(): lax.ppermute(value, 'col', [(i, (i + 2 * step) % self.col) for i in range...]
    unnamed x101 -> x123, local copies, waits for them, and re-layouts: 18.8 us -> 31.9 us
    ppermute x24 -> x18, starting transfers between devices: 51.8 us -> 40.9 us  [send(): lax.ppermute(value, 'col', [(i, (i + 2 * step) % self.col) for i in range...]
    ppermute x20 -> x16, waiting for transfers between devices: 86.3 us -> 82 us  [x(): return lax.ppermute(value, 'dp', [(i, i ^ 1) for i in range(self.dp)])]
    ppermute x20 -> x16, starting transfers between devices: 19.8 us -> 16.9 us  [y(): return lax.ppermute(value, 'dp', [(i, i ^ 2) for i in range(self.dp)])]
    ppermute x20 -> x16, starting transfers between devices: 18.2 us -> 17.1 us  [x(): return lax.ppermute(value, 'dp', [(i, i ^ 1) for i in range(self.dp)])]
    convert_element_type x17 -> x12, other arithmetic: 36.9 us -> 37.6 us  [add(): return total.astype(jnp.bfloat16)]
  transfers between devices with their start and end apart: 97 -> 73, of which waited for: 42 -> 30; matrix products, arithmetic and copies ran while one was open for 13% -> 12% of each run, Pallas kernels for 25% -> 26%
where the time goes in v4:
time: 801 us; the launch traced here: 794 us
  Pallas kernels  285 us (36%)
  waiting for transfers between devices  261 us (33%)
  starting transfers between devices  94.8 us (12%)
  local copies, waits for them, and re-layouts  78.8 us (10%)
  other arithmetic  72.2 us (9%)
    pallas_call x12, Pallas kernels, call(): pl.pallas_call(run, out_shape=outs, in_specs=list(specs) + [pl.BlockSpec(...  285 us
    ppermute x18, waiting for transfers between devices, send(): lax.ppermute(value, 'col', [(i, (i + 2 * step) % self.col) for i in range...  110 us
    ppermute x16, waiting for transfers between devices, x(): return lax.ppermute(value, 'dp', [(i, i ^ 1) for i in range(self.dp)])  82 us
    ppermute x16, waiting for transfers between devices, y(): return lax.ppermute(value, 'dp', [(i, i ^ 2) for i in range(self.dp)])  57.4 us
    ppermute x18, starting transfers between devices, send(): lax.ppermute(value, 'col', [(i, (i + 2 * step) % self.col) for i in range...  40.9 us
    convert_element_type x12, other arithmetic, add(): return total.astype(jnp.bfloat16)  37.6 us
    unnamed x123, local copies, waits for them, and re-layouts  31.9 us
    ppermute x16, starting transfers between devices, x(): return lax.ppermute(value, 'dp', [(i, i ^ 1) for i in range(self.dp)])  17.1 us
  transfers between devices with their start and end apart: 73, of which 30 were waited for; matrix products, arithmetic and copies ran while one was open for 12% of the time, Pallas kernels for 26%

profile of v4, /device:TPU:0, one launch (start us, length us, event | category | flops | bytes accessed | tf_op | source)
XLA Modules:
  0.0 793.9 jit_solution(7288510424911856623)
XLA Ops:
  14.8 14.0 %collective-permute-done = bf16[4,80,960]{2,1,0:T(8,128)(2,1)S(1)} collective-permute-done((bf16[4,80,960]{2,1,0:T(8,128)(2,1)S(1)}, bf16[4,80,960]{2,1,0:T(8,128)(2,1)S(1)}, u32[]{:S(2)}, u32[]{:S(2)}) %collective-permute-start) | collective-permute-done | bytes 614432 | tf_op jit(solution)/shard_map/ppermute | solution.py:412
  28.9 40.8 %collective-permute-done.1 = bf16[4,80,960]{2,1,0:T(8,128)(2,1)S(1)} collective-permute-done((bf16[4,80,960]{2,1,0:T(8,128)(2,1)S(1)}, bf16[4,80,960]{2,1,0:T(8,128)(2,1)S(1)}, u32[]{:S(2)}, u32[]{:S(2)}) %collective-permute-start.1) | collective-permute-done | bytes 614432 | tf_op jit(solution)/shard_map/ppermute | solution.py:412
  73.1 54.8 %collective-permute-done.3.refs_1_.refs_3_.refs_6_ = bf16[4,4,80,960]{3,2,1,0:T(8,128)(2,1)} collective-permute-done((bf16[4,4,80,960]{3,2,1,0:T(8,128)(2,1)S(1)}, bf16[4,4,80,960]{3,2,1,0:T(8,128)(2,1)}, u32[]{:S(2)}, u32[]{:S(2)}) %collective-permute-start.3) | collective-permute-done | bytes 2457632 | tf_op jit(solution)/shard_map/ppermute | solution.py:400
  140.7 7.1 collective-permute-done.10
  148.4 28.9 %collective-permute-done.11 = bf16[4,80,960]{2,1,0:T(8,128)(2,1)S(1)} collective-permute-done((bf16[4,80,960]{2,1,0:T(8,128)(2,1)S(1)}, bf16[4,80,960]{2,1,0:T(8,128)(2,1)S(1)}, u32[]{:S(2)}, u32[]{:S(2)}) %collective-permute-start.11) | collective-permute-done | bytes 614432 | tf_op jit(solution)/shard_map/ppermute | solution.py:412
  184.1 12.0 %collective-permute-done.12 = bf16[4,80,960]{2,1,0:T(8,128)(2,1)} collective-permute-done((bf16[4,80,960]{2,1,0:T(8,128)(2,1)S(1)}, bf16[4,80,960]{2,1,0:T(8,128)(2,1)}, u32[]{:S(2)}, u32[]{:S(2)}) %collective-permute-start.12) | collective-permute-done | bytes 614432 | tf_op jit(solution)/shard_map/ppermute | solution.py:412
  216.8 28.8 %shard_map.187 = (bf16[768,960]{1,0:T(8,128)(2,1)}, bf16[768,1600]{1,0:T(8,128)(2,1)}, bf16[768,960]{1,0:T(8,128)(2,1)}, f32[16,768]{1,0:T(8,128)}, f32[768,960]{1,0:T(8,128)}, /*index=5*/bf16[768,960]{1,0:T(8,128)(2,1)}) custom-call(f32[768,960]{1,0:T(8,128)} %bitcast_convert_fusion.refs_0_.refs_2_, f32[1,960]{1,0:T(1,128)} %get-tuple-element.381.refs_1_.refs_8_, ...), custom_call_target="tpu_custom_call" | custom-call | flops 20000000000 | bytes 20971520 | tf_op jit(solution)/shard_map/pallas_call | solution.py:54
  245.6 22.1 %shard_map.188 = (f32[768,960]{1,0:T(8,128)}, bf16[768,1280]{1,0:T(8,128)(2,1)}, bf16[768,1280]{1,0:T(8,128)(2,1)}, bf16[768,1280]{1,0:T(8,128)(2,1)}, bf16[768,1280]{1,0:T(8,128)(2,1)}) custom-call(f32[768,960]{1,0:T(8,128)} %get-tuple-element.144.refs_0_.refs_7_, bf16[768,960]{1,0:T(8,128)(2,1)} %get-tuple-element.145.refs_1_, ...), custom_call_target="tpu_custom_call" | custom-call | flops 11000000512 | bytes 31457280 | tf_op jit(solution)/shard_map/pallas_call | solution.py:54
  273.3 29.2 %collective-permute-done.18.refs_3_.refs_5_.refs_8_ = bf16[2,4,80,960]{3,2,1,0:T(8,128)(2,1)} collective-permute-done((bf16[2,4,80,960]{3,2,1,0:T(8,128)(2,1)S(1)}, bf16[2,4,80,960]{3,2,1,0:T(8,128)(2,1)}, u32[]{:S(2)}, u32[]{:S(2)}) %collective-permute-start.18) | collective-permute-done | bytes 1228832 | tf_op jit(solution)/shard_map/ppermute | solution.py:403
  323.2 28.8 %shard_map.190 = (bf16[768,960]{1,0:T(8,128)(2,1)}, bf16[768,1600]{1,0:T(8,128)(2,1)}, bf16[768,960]{1,0:T(8,128)(2,1)}, f32[16,768]{1,0:T(8,128)}, f32[768,960]{1,0:T(8,128)}, /*index=5*/bf16[768,960]{1,0:T(8,128)(2,1)}) custom-call(f32[768,960]{1,0:T(8,128)} %get-tuple-element.155.refs_0_.refs_2_, f32[1,960]{1,0:T(1,128)} %get-tuple-element.382.refs_1_.refs_8_, ...), custom_call_target="tpu_custom_call" | custom-call | flops 20000000000 | bytes 20971520 | tf_op jit(solution)/shard_map/pallas_call | solution.py:54
  352.0 22.2 %shard_map.191 = (f32[768,960]{1,0:T(8,128)}, bf16[768,1280]{1,0:T(8,128)(2,1)}, bf16[768,1280]{1,0:T(8,128)(2,1)}, bf16[768,1280]{1,0:T(8,128)(2,1)}, bf16[768,1280]{1,0:T(8,128)(2,1)}) custom-call(f32[768,960]{1,0:T(8,128)} %get-tuple-element.161.refs_0_.refs_7_, bf16[768,960]{1,0:T(8,128)(2,1)} %get-tuple-element.162.refs_1_, ...), custom_call_target="tpu_custom_call" | custom-call | flops 11000000512 | bytes 31457280 | tf_op jit(solution)/shard_map/pallas_call | solution.py:54
  374.2 22.1 %shard_map.192 = (bf16[16,3,80,960]{3,2,1,0:T(8,128)(2,1)}, f32[768,960]{1,0:T(8,128)}) custom-call(bf16[768,960]{1,0:T(8,128)(2,1)} %bitcast.486, bf16[768,960]{1,0:T(8,128)(2,1)} %get-tuple-element.162.refs_1_, bf16[768,1280]{1,0:T(8,128)(2,1)} %get-tuple-element.166.refs_2_, bf16[768,1280]{1,0:T(8,128)(2,1)} %get-tuple-element.167.refs_3_, ...), custom_call_target="tpu_custom_call" | custom-call | flops 11000000512 | bytes 31457280 | tf_op jit(solution)/shard_map/pallas_call | solution.py:54
  398.6 23.0 %shard_map.193 = (bf16[16,3,80,960]{3,2,1,0:T(8,128)(2,1)}, f32[768,960]{1,0:T(8,128)}) custom-call(bf16[768,960]{1,0:T(8,128)(2,1)} %bitcast.487, bf16[768,960]{1,0:T(8,128)(2,1)} %get-tuple-element.162.refs_1_, bf16[768,1280]{1,0:T(8,128)(2,1)} %get-tuple-element.164.refs_2_, bf16[768,1280]{1,0:T(8,128)(2,1)} %get-tuple-element.165.refs_3_, ...), custom_call_target="tpu_custom_call" | custom-call | flops 11000000512 | bytes 31457280 | tf_op jit(solution)/shard_map/pallas_call | solution.py:54
  421.7 5.5 add_convert_fusion.9
  430.7 42.0 %shard_map.194 = (bf16[1600,960]{1,0:T(8,128)(2,1)}, bf16[960,960]{1,0:T(8,128)(2,1)}, f32[768,960]{1,0:T(8,128)}, bf16[768,960]{1,0:T(8,128)(2,1)}, f32[1,960]{1,0:T(1,128)}, /*index=5*/f32[1,960]{1,0:T(1,128)}) custom-call(f32[768,960]{1,0:T(8,128)} %bitcast_convert_fusion.3.refs_0_, f32[768,960]{1,0:T(8,128)} %get-tuple-element.172.refs_1_, ...), custom_call_target="tpu_custom_call" | custom-call | flops 35000000512 | bytes 41943040 | tf_op jit(solution)/shard_map/pallas_call | solution.py:54
  488.5 22.1 %shard_map.195 = (bf16[16,3,80,960]{3,2,1,0:T(8,128)(2,1)}, f32[768,960]{1,0:T(8,128)}) custom-call(bf16[768,960]{1,0:T(8,128)(2,1)} %get-tuple-element.186.refs_0_, bf16[768,960]{1,0:T(8,128)(2,1)} %get-tuple-element.145.refs_1_, bf16[768,1280]{1,0:T(8,128)(2,1)} %get-tuple-element.189.refs_2_, bf16[768,1280]{1,0:T(8,128)(2,1)} %get-tuple-element.190.refs_3_, ...), custom_call_target="tpu_custom_call" | custom-call | flops 11000000512 | bytes 31457280 | tf_op jit(solution)/shard_map/pallas_call | solution.py:54
  526.4 23.0 %shard_map.196 = (bf16[16,3,80,960]{3,2,1,0:T(8,128)(2,1)}, f32[768,960]{1,0:T(8,128)}) custom-call(bf16[768,960]{1,0:T(8,128)(2,1)} %get-tuple-element.186.refs_0_, bf16[768,960]{1,0:T(8,128)(2,1)} %get-tuple-element.145.refs_1_, bf16[768,1280]{1,0:T(8,128)(2,1)} %get-tuple-element.187.refs_2_, bf16[768,1280]{1,0:T(8,128)(2,1)} %get-tuple-element.188.refs_3_, ...), custom_call_target="tpu_custom_call" | custom-call | flops 11000000512 | bytes 31457280 | tf_op jit(solution)/shard_map/pallas_call | solution.py:54
  565.1 42.0 %shard_map.197 = (bf16[1600,960]{1,0:T(8,128)(2,1)}, bf16[960,960]{1,0:T(8,128)(2,1)}, f32[768,960]{1,0:T(8,128)}, bf16[768,960]{1,0:T(8,128)(2,1)}, f32[1,960]{1,0:T(1,128)}, /*index=5*/f32[1,960]{1,0:T(1,128)}) custom-call(f32[768,960]{1,0:T(8,128)} %get-tuple-element.185.refs_0_, f32[768,960]{1,0:T(8,128)} %get-tuple-element.202.refs_1_, ...), custom_call_target="tpu_custom_call" | custom-call | flops 35000000512 | bytes 41943040 | tf_op jit(solution)/shard_map/pallas_call | solution.py:54
  617.2 5.5 fusion.7
  629.6 7.3 collective-permute-start.48
  663.1 18.6 %collective-permute-done.45 = bf16[3,80,960]{2,1,0:T(8,128)(2,1)S(1)} collective-permute-done((bf16[3,80,960]{2,1,0:T(8,128)(2,1)S(1)}, bf16[3,80,960]{2,1,0:T(8,128)(2,1)S(1)}, u32[]{:S(2)}, u32[]{:S(2)}) %collective-permute-start.45) | collective-permute-done | bytes 460832 | tf_op jit(solution)/shard_map/ppermute | solution.py:400
  681.8 5.8 collective-permute-start.59
  736.7 5.8 collective-permute-done.62
  751.1 25.3 %collective-permute-done.65 = bf16[80,960]{1,0:T(8,128)(2,1)S(1)} collective-permute-done((bf16[80,960]{1,0:T(8,128)(2,1)S(1)}, bf16[80,960]{1,0:T(8,128)(2,1)S(1)}, u32[]{:S(2)}, u32[]{:S(2)}) %collective-permute-start.65) | collective-permute-done | bytes 153632 | tf_op jit(solution)/shard_map/ppermute | solution.py:403
  (375 shorter events, 254.8 us)
Async XLA Ops:
  13.7 56.0 %collective-permute-start.1 = (bf16[4,80,960]{2,1,0:T(8,128)(2,1)S(1)}, bf16[4,80,960]{2,1,0:T(8,128)(2,1)S(1)}, u32[]{:S(2)}, u32[]{:S(2)}) collective-permute-start(bf16[4,80,960]{2,1,0:T(8,128)(2,1)S(1)} %get-tuple-element.363), channel_id=1, source_target_pairs={{0,4},{1,5},{2,6},{3,7},{4,0},{5,1},{6,2},{7,3},{8,12},{9,13},{10,... | collective-permute-start | bytes 1843208 | tf_op jit(solution)/shard_map/ppermute | solution.py:412
  13.7 56.0 %collective-permute-start.2 = (bf16[4,80,960]{2,1,0:T(8,128)(2,1)S(1)}, bf16[4,80,960]{2,1,0:T(8,128)(2,1)S(1)}, u32[]{:S(2)}, u32[]{:S(2)}) collective-permute-start(bf16[4,80,960]{2,1,0:T(8,128)(2,1)S(1)} %get-tuple-element.363), channel_id=1, source_target_pairs={{0,2},{1,3},{2,4},{3,5},{4,6},{5,7},{6,0},{7,1},{8,10},{9,11},{10,... | collective-permute-start | bytes 1843208 | tf_op jit(solution)/shard_map/ppermute | solution.py:412
  70.1 57.9 %collective-permute-start.3 = (bf16[4,4,80,960]{3,2,1,0:T(8,128)(2,1)S(1)}, bf16[4,4,80,960]{3,2,1,0:T(8,128)(2,1)}, u32[]{:S(2)}, u32[]{:S(2)}) collective-permute-start(bf16[4,4,80,960]{3,2,1,0:T(8,128)(2,1)S(1)} %pad_maximum_fusion.4.refs_0_.refs_2_.refs_5_), channel_id=1, source_target_pairs={{0,8},{8,0},{16,24},{24,16},{1,9},{9,1},{17,25},{25,17},{2,10},{10... | collective-permute-start | bytes 7372808 | tf_op jit(solution)/shard_map/ppermute | solution.py:400
  71.6 57.6 %collective-permute-start.4 = (bf16[4,4,80,960]{3,2,1,0:T(8,128)(2,1)S(1)}, bf16[4,4,80,960]{3,2,1,0:T(8,128)(2,1)}, u32[]{:S(2)}, u32[]{:S(2)}) collective-permute-start(bf16[4,4,80,960]{3,2,1,0:T(8,128)(2,1)S(1)} %pad_maximum_fusion.4.refs_0_.refs_2_.refs_5_), channel_id=1, source_target_pairs={{0,16},{8,24},{16,0},{24,8},{1,17},{9,25},{17,1},{25,9},{2,18},{10... | collective-permute-start | bytes 7372808 | tf_op jit(solution)/shard_map/ppermute | solution.py:403
  73.1 56.0 %collective-permute-start.5 = (bf16[4,4,80,960]{3,2,1,0:T(8,128)(2,1)S(1)}, bf16[4,4,80,960]{3,2,1,0:T(8,128)(2,1)S(1)}, u32[]{:S(2)}, u32[]{:S(2)}) collective-permute-start(bf16[4,4,80,960]{3,2,1,0:T(8,128)(2,1)S(1)} %pad_maximum_fusion.4.refs_0_.refs_2_.refs_5_), channel_id=1, source_target_pairs={{0,1},{1,0},{2,3},{3,2},{4,5},{5,4},{6,7},{7,6},{8,9},{9,8},{10,11... | collective-permute-start | bytes 7372808 | tf_op jit(solution)/shard_map/ppermute | solution.py:406
  130.7 65.4 %collective-permute-start.8 = (bf16[4,4,80,960]{3,2,1,0:T(8,128)(2,1)}, bf16[4,4,80,960]{3,2,1,0:T(8,128)(2,1)}, u32[]{:S(2)}, u32[]{:S(2)}) collective-permute-start(bf16[4,4,80,960]{3,2,1,0:T(8,128)(2,1)} %collective-permute-done.3.refs_1_.refs_3_.refs_6_), channel_id=1, source_target_pairs={{0,1},{1,0},{2,3},{3,2},{4,5},{5,4},{6,7},{7,6},{8,9},{9,8},{10,11... | collective-permute-start | bytes 7372808 | tf_op jit(solution)/shard_map/ppermute | solution.py:406
  130.7 65.4 %collective-permute-start.9 = (bf16[4,4,80,960]{3,2,1,0:T(8,128)(2,1)}, bf16[4,4,80,960]{3,2,1,0:T(8,128)(2,1)}, u32[]{:S(2)}, u32[]{:S(2)}) collective-permute-start(bf16[4,4,80,960]{3,2,1,0:T(8,128)(2,1)} %collective-permute-done.4.refs_2_.refs_4_.refs_7_), channel_id=1, source_target_pairs={{0,1},{1,0},{2,3},{3,2},{4,5},{5,4},{6,7},{7,6},{8,9},{9,8},{10,11... | collective-permute-start | bytes 7372808 | tf_op jit(solution)/shard_map/ppermute | solution.py:406
  131.2 46.0 %collective-permute-start.11 = (bf16[4,80,960]{2,1,0:T(8,128)(2,1)S(1)}, bf16[4,80,960]{2,1,0:T(8,128)(2,1)S(1)}, u32[]{:S(2)}, u32[]{:S(2)}) collective-permute-start(bf16[4,80,960]{2,1,0:T(8,128)(2,1)S(1)} %pad_maximum_fusion.15), channel_id=1, source_target_pairs={{0,4},{1,5},{2,6},{3,7},{4,0},{5,1},{6,2},{7,3},{8,12},{9,13},{10,... | collective-permute-start | bytes 1843208 | tf_op jit(solution)/shard_map/ppermute | solution.py:412
  139.2 56.9 %collective-permute-start.6 = (bf16[2,4,80,960]{3,2,1,0:T(8,128)(2,1)}, bf16[2,4,80,960]{3,2,1,0:T(8,128)(2,1)}, u32[]{:S(2)}, u32[]{:S(2)}) collective-permute-start(bf16[2,4,80,960]{3,2,1,0:T(8,128)(2,1)} %slice.364), channel_id=1, source_target_pairs={{0,16},{8,24},{16,0},{24,8},{1,17},{9,25},{17,1},{25,9},{2,18},{10... | collective-permute-start | bytes 3686408 | tf_op jit(solution)/shard_map/ppermute | solution.py:403
  147.8 48.3 %collective-permute-start.7 = (bf16[2,4,80,960]{3,2,1,0:T(8,128)(2,1)}, bf16[2,4,80,960]{3,2,1,0:T(8,128)(2,1)}, u32[]{:S(2)}, u32[]{:S(2)}) collective-permute-start(bf16[2,4,80,960]{3,2,1,0:T(8,128)(2,1)} %slice.365), channel_id=1, source_target_pairs={{0,8},{8,0},{16,24},{24,16},{1,9},{9,1},{17,25},{25,17},{2,10},{10... | collective-permute-start | bytes 3686408 | tf_op jit(solution)/shard_map/ppermute | solution.py:400
  206.5 61.2 %collective-permute-start.15 = (bf16[4,4,80,960]{3,2,1,0:T(8,128)(2,1)S(1)}, bf16[4,4,80,960]{3,2,1,0:T(8,128)(2,1)}, u32[]{:S(2)}, u32[]{:S(2)}) collective-permute-start(bf16[4,4,80,960]{3,2,1,0:T(8,128)(2,1)S(1)} %pad_maximum_fusion.5.refs_0_.refs_2_.refs_5_), channel_id=1, source_target_pairs={{0,8},{8,0},{16,24},{24,16},{1,9},{9,1},{17,25},{25,17},{2,10},{10... | collective-permute-start | bytes 7372808 | tf_op jit(solution)/shard_map/ppermute | solution.py:400
  207.1 60.6 %collective-permute-start.16 = (bf16[4,4,80,960]{3,2,1,0:T(8,128)(2,1)S(1)}, bf16[4,4,80,960]{3,2,1,0:T(8,128)(2,1)}, u32[]{:S(2)}, u32[]{:S(2)}) collective-permute-start(bf16[4,4,80,960]{3,2,1,0:T(8,128)(2,1)S(1)} %pad_maximum_fusion.5.refs_0_.refs_2_.refs_5_), channel_id=1, source_target_pairs={{0,16},{8,24},{16,0},{24,8},{1,17},{9,25},{17,1},{25,9},{2,18},{10... | collective-permute-start | bytes 7372808 | tf_op jit(solution)/shard_map/ppermute | solution.py:403
  208.6 59.1 %collective-permute-start.17 = (bf16[4,4,80,960]{3,2,1,0:T(8,128)(2,1)S(1)}, bf16[4,4,80,960]{3,2,1,0:T(8,128)(2,1)}, u32[]{:S(2)}, u32[]{:S(2)}) collective-permute-start(bf16[4,4,80,960]{3,2,1,0:T(8,128)(2,1)S(1)} %pad_maximum_fusion.5.refs_0_.refs_2_.refs_5_), channel_id=1, source_target_pairs={{0,1},{1,0},{2,3},{3,2},{4,5},{5,4},{6,7},{7,6},{8,9},{9,8},{10,11... | collective-permute-start | bytes 7372808 | tf_op jit(solution)/shard_map/ppermute | solution.py:406
  427.4 45.4 %collective-permute-start.26 = (bf16[2,2,3,80,960]{4,3,2,1,0:T(8,128)(2,1)S(1)}, bf16[2,2,3,80,960]{4,3,2,1,0:T(8,128)(2,1)S(1)}, u32[]{:S(2)}, u32[]{:S(2)}) collective-permute-start(bf16[2,2,3,80,960]{4,3,2,1,0:T(8,128)(2,1)S(1)} %pad_maximum_fusion.7), channel_id=1, source_target_pairs={{0,16},{8,24},{16,0},{24,8},{1,17},{9,25},{17,1},{25,9},{2,18},{10... | collective-permute-start | bytes 5529608 | tf_op jit(solution)/shard_map/ppermute | solution.py:403
  429.2 44.9 %collective-permute-start.25 = (bf16[2,2,3,80,960]{4,3,2,1,0:T(8,128)(2,1)S(1)}, bf16[2,2,3,80,960]{4,3,2,1,0:T(8,128)(2,1)S(1)}, u32[]{:S(2)}, u32[]{:S(2)}) collective-permute-start(bf16[2,2,3,80,960]{4,3,2,1,0:T(8,128)(2,1)S(1)} %pad_maximum_fusion.6), channel_id=1, source_target_pairs={{0,8},{8,0},{16,24},{24,16},{1,9},{9,1},{17,25},{25,17},{2,10},{10... | collective-permute-start | bytes 5529608 | tf_op jit(solution)/shard_map/ppermute | solution.py:400
  525.4 39.1 %collective-permute-start.37 = (bf16[3,80,960]{2,1,0:T(8,128)(2,1)S(1)}, bf16[3,80,960]{2,1,0:T(8,128)(2,1)}, u32[]{:S(2)}, u32[]{:S(2)}) collective-permute-start(bf16[3,80,960]{2,1,0:T(8,128)(2,1)S(1)} %get-tuple-element.354), channel_id=1, source_target_pairs={{0,6},{1,7},{2,0},{3,1},{4,2},{5,3},{6,4},{7,5},{8,14},{9,15},{10,... | collective-permute-start | bytes 1382408 | tf_op jit(solution)/shard_map/ppermute | solution.py:412
  550.2 56.8 %collective-permute-start.35 = (bf16[3,80,960]{2,1,0:T(8,128)(2,1)}, bf16[3,80,960]{2,1,0:T(8,128)(2,1)}, u32[]{:S(2)}, u32[]{:S(2)}) collective-permute-start(bf16[3,80,960]{2,1,0:T(8,128)(2,1)} %slice_bitcast_fusion.11), channel_id=1, source_target_pairs={{0,2},{1,3},{2,4},{3,5},{4,6},{5,7},{6,0},{7,1},{8,10},{9,11},{10,... | collective-permute-start | bytes 1382408 | tf_op jit(solution)/shard_map/ppermute | solution.py:412
  553.9 53.1 %collective-permute-start.38 = (bf16[2,80,960]{2,1,0:T(8,128)(2,1)}, bf16[2,80,960]{2,1,0:T(8,128)(2,1)S(1)}, u32[]{:S(2)}, u32[]{:S(2)}) collective-permute-start(bf16[2,80,960]{2,1,0:T(8,128)(2,1)} %get-tuple-element.325), channel_id=1, source_target_pairs={{0,8},{8,0},{16,24},{24,16},{1,9},{9,1},{17,25},{25,17},{2,10},{10... | collective-permute-start | bytes 921608 | tf_op jit(solution)/shard_map/ppermute | solution.py:400
  555.3 51.7 %collective-permute-start.39 = (bf16[2,80,960]{2,1,0:T(8,128)(2,1)}, bf16[2,80,960]{2,1,0:T(8,128)(2,1)}, u32[]{:S(2)}, u32[]{:S(2)}) collective-permute-start(bf16[2,80,960]{2,1,0:T(8,128)(2,1)} %get-tuple-element.324), channel_id=1, source_target_pairs={{0,16},{8,24},{16,0},{24,8},{1,17},{9,25},{17,1},{25,9},{2,18},{10... | collective-permute-start | bytes 921608 | tf_op jit(solution)/shard_map/ppermute | solution.py:403
  563.6 43.6 %collective-permute-start.34 = (bf16[2,2,3,80,960]{4,3,2,1,0:T(8,128)(2,1)S(1)}, bf16[2,2,3,80,960]{4,3,2,1,0:T(8,128)(2,1)S(1)}, u32[]{:S(2)}, u32[]{:S(2)}) collective-permute-start(bf16[2,2,3,80,960]{4,3,2,1,0:T(8,128)(2,1)S(1)} %pad_maximum_fusion.9), channel_id=1, source_target_pairs={{0,16},{8,24},{16,0},{24,8},{1,17},{9,25},{17,1},{25,9},{2,18},{10... | collective-permute-start | bytes 5529608 | tf_op jit(solution)/shard_map/ppermute | solution.py:403
  564.4 43.8 %collective-permute-start.33 = (bf16[2,2,3,80,960]{4,3,2,1,0:T(8,128)(2,1)}, bf16[2,2,3,80,960]{4,3,2,1,0:T(8,128)(2,1)S(1)}, u32[]{:S(2)}, u32[]{:S(2)}) collective-permute-start(bf16[2,2,3,80,960]{4,3,2,1,0:T(8,128)(2,1)} %pad_maximum_fusion.8), channel_id=1, source_target_pairs={{0,8},{8,0},{16,24},{24,16},{1,9},{9,1},{17,25},{25,17},{2,10},{10... | collective-permute-start | bytes 5529608 | tf_op jit(solution)/shard_map/ppermute | solution.py:400
  681.8 50.3 %collective-permute-start.59 = (bf16[3,80,960]{2,1,0:T(8,128)(2,1)S(1)}, bf16[3,80,960]{2,1,0:T(8,128)(2,1)S(1)}, u32[]{:S(2)}, u32[]{:S(2)}) collective-permute-start(bf16[3,80,960]{2,1,0:T(8,128)(2,1)S(1)} %get-tuple-element.353), channel_id=1, source_target_pairs={{0,4},{1,5},{2,6},{3,7},{4,0},{5,1},{6,2},{7,3},{8,12},{9,13},{10,... | collective-permute-start | bytes 1382408 | tf_op jit(solution)/shard_map/ppermute | solution.py:412
  687.6 47.2 %collective-permute-start.60 = (bf16[3,80,960]{2,1,0:T(8,128)(2,1)S(1)}, bf16[3,80,960]{2,1,0:T(8,128)(2,1)S(1)}, u32[]{:S(2)}, u32[]{:S(2)}) collective-permute-start(bf16[3,80,960]{2,1,0:T(8,128)(2,1)S(1)} %get-tuple-element.352), channel_id=1, source_target_pairs={{0,6},{1,7},{2,0},{3,1},{4,2},{5,3},{6,4},{7,5},{8,14},{9,15},{10,... | collective-permute-start | bytes 1382408 | tf_op jit(solution)/shard_map/ppermute | solution.py:412
  746.9 39.4 %collective-permute-start.72 = (bf16[3,80,960]{2,1,0:T(8,128)(2,1)}, bf16[3,80,960]{2,1,0:T(8,128)(2,1)}, u32[]{:S(2)}, u32[]{:S(2)}) collective-permute-start(bf16[3,80,960]{2,1,0:T(8,128)(2,1)} %get-tuple-element.285), channel_id=1, source_target_pairs={{0,24},{8,16},{16,8},{24,0},{1,25},{9,17},{17,9},{25,1},{2,26},{10... | collective-permute-start | bytes 1382408 | tf_op jit(solution)/shard_map/ppermute | solution.py:409
  (107 other events, 1564.2 us)

commit v5 on v4

--- a/solution.py
+++ b/solution.py
@@ -445,6 +445,10 @@
         return self.result
 
 
+def settle(value, *arrays):
+    return lax.optimization_barrier((value, arrays))[0]
+
+
 def advance(value, *transfers):
     flying = [transfer.flying for transfer in transfers]
     value, flying = lax.optimization_barrier((value, flying))
@@ -457,10 +461,11 @@
     far = yield [links.send(part, -step) for step in range(1, links.line)]
     own = jnp.stack([part, *far])
     half = links.line // 2
-    from_x, from_y, own_c = yield [links.x(own), links.y(own), links.other_core(own)]
-    low, high, x_c, y_c = yield [
+    from_x, from_y = yield [links.x(own), links.y(own)]
+    low, high, own_c, x_c, y_c = yield [
         links.y(from_x[:half]),
         links.x(from_y[half:]),
+        links.other_core(own),
         links.other_core(from_x),
         links.other_core(from_y),
     ]
@@ -501,6 +506,10 @@
     total = add(chip(0), *far)
     if links.dp > 4:
         total = lax.psum(total, "dp", axis_index_groups=links.rest)
+    return total
+
+
+def quarter_stages(links, total):
     others = yield [links.x(total), links.y(total), links.both(total)]
     return (total, *others)
 
@@ -621,7 +630,8 @@
         if layer + 1 < layers:
             part = advance(parts[layer + 1], move)
             later = [Transfer(gather_stages(links, part))]
-        advance(None, move)
+            move.flying = settle(move.flying, *later[0].flying)
+            advance(None, move)
         hidden = advance(hidden, move, *later)
         blocks = move.finish()
         qkv_w, output_w = attention_weights(links, blocks, rows)
@@ -629,11 +639,11 @@
         normed, qkv, attended, logsum, middle, normed2 = attention_forward(
             hidden, *gains[layer], qkv_w, output_w, *where
         )
+        normed2 = advance(normed2, *later)
         result, *products = ffn_forward(middle, normed2, *ffn_w)
         saved.append(((hidden, normed, qkv, attended, logsum, middle), normed2, products, (qkv_w, output_w), ffn_w))
         hidden = result
         if later:
-            hidden = advance(hidden, *later)
             move = later[0]
     final = hidden.astype(jnp.bfloat16)[None]
 
@@ -647,7 +657,7 @@
         return share[place, part]
 
     def attn_pick(share, place, part):
-        return lax.dynamic_index_in_dim(share[part], links.quarter ^ place, 1, False)
+        return lax.dynamic_slice_in_dim(share[part], links.quarter ^ place, 1, 1)
 
     for layer in reversed(range(layers)):
         kept, normed2, products, attn_w, ffn_w = saved[layer]
@@ -671,19 +681,29 @@
         )
         gain_terms[layer] = jnp.stack(gain_grads)
     gain_terms = jnp.concatenate(gain_terms, axis=1)
-    gain_terms = advance(gain_terms, ffn_move, attn_move)
-    gain_terms = advance(gain_terms, attn_move, *last_ffn, *last_attn)
-    gain_terms = advance(gain_terms, attn_move)
-    gains = links.sum_all(gain_terms)
-    advance(None, ffn_move, attn_move)
+    gain_terms = advance(gain_terms, ffn_move, attn_move, *last_attn)
+    rest = []
+    for layer in range(1, layers):
+        total = jnp.concatenate([moves[layer][1].finish(), moves[layer][0].finish()])
+        total = settle(total, ffn_move.flying[0], ffn_move.flying[-1])
+        rest.append(Transfer(quarter_stages(links, total)))
+    gains = advance(links.sum_all(gain_terms), ffn_move, attn_move)
+    last = Transfer(quarter_stages(links, ffn_move.finish()))
+    gains = advance(gains, attn_move, *rest)
+    tail = Transfer(quarter_stages(links, attn_move.finish()))
+    shares = [(last.finish(), tail.finish())]
+    for transfer in rest:
+        quarters = transfer.finish()
+        shares.append(([q[:3] for q in quarters], [q[3:] for q in quarters]))
+
     sums = [[] for _ in range(6)]
-    for attn_move, ffn_move in moves:
-        total = in_order(links, attn_move.finish()).reshape(-1, width).astype(jnp.float32)
+    for ffn_part, attn_part in shares:
+        total = in_order(links, attn_part).reshape(-1, width).astype(jnp.float32)
         a, b = rows[0], rows[0] + rows[1]
         sums[0].append(total[:a].T)
         sums[1].append(total[a:b].T)
         sums[2].append(total[b:])
-        quarters = in_order(links, ffn_move.finish())
+        quarters = in_order(links, ffn_part)
         for kind in range(3):
             total = quarters[:, kind].reshape(-1, width).astype(jnp.float32)
             sums[3 + kind].append(total if kind == 2 else total.T)

time: 801 us -> 773 us (0.965)
  starting transfers between devices: 94.8 us -> 69.9 us
  local copies, waits for them, and re-layouts: 78.8 us -> 61.2 us
  waiting for transfers between devices: 261 us -> 274 us
    ppermute x16 -> x15, waiting for transfers between devices: 82 us -> 35.8 us  [x(): return lax.ppermute(value, 'dp', [(i, i ^ 1) for i in range(self.dp)])]
    ppermute x18, waiting for transfers between devices: 110 us -> 140 us  [send(): lax.ppermute(value, 'col', [(i, (i + 2 * step) % self.col) for i in range...]
    ppermute x5, waiting for transfers between devices: 6.18 us -> 29.3 us  [sum_all(): lax.ppermute(value, axis, [(i, i ^ step) for i in range(size)])]
    ppermute x18, starting transfers between devices: 40.9 us -> 24.5 us  [send(): lax.ppermute(value, 'col', [(i, (i + 2 * step) % self.col) for i in range...]
    unnamed x123 -> x99, local copies, waits for them, and re-layouts: 31.9 us -> 20.7 us
    ppermute x16 -> x15, waiting for transfers between devices: 57.4 us -> 65.9 us  [y(): return lax.ppermute(value, 'dp', [(i, i ^ 2) for i in range(self.dp)])]
    convert_element_type x12 -> x16, other arithmetic: 37.6 us -> 42.6 us  [add(): return total.astype(jnp.bfloat16)]
    ppermute x16 -> x15, starting transfers between devices: 17.1 us -> 17 us  [x(): return lax.ppermute(value, 'dp', [(i, i ^ 1) for i in range(self.dp)])]
  transfers between devices with their start and end apart: 73 -> 70, of which waited for: 30 -> 33; matrix products, arithmetic and copies ran while one was open for 12% -> 12% of each run, Pallas kernels for 26% -> 27%
where the time goes in v5:
time: 773 us; the launch traced here: 767 us
  Pallas kernels  283 us (37%)
  waiting for transfers between devices  274 us (35%)
  other arithmetic  76.7 us (10%)
  starting transfers between devices  69.9 us (9%)
  local copies, waits for them, and re-layouts  61.2 us (8%)
    pallas_call x12, Pallas kernels, call(): pl.pallas_call(run, out_shape=outs, in_specs=list(specs) + [pl.BlockSpec(...  283 us
    ppermute x18, waiting for transfers between devices, send(): lax.ppermute(value, 'col', [(i, (i + 2 * step) % self.col) for i in range...  140 us
    ppermute x15, waiting for transfers between devices, y(): return lax.ppermute(value, 'dp', [(i, i ^ 2) for i in range(self.dp)])  65.9 us
    convert_element_type x16, other arithmetic, add(): return total.astype(jnp.bfloat16)  42.6 us
    ppermute x15, waiting for transfers between devices, x(): return lax.ppermute(value, 'dp', [(i, i ^ 1) for i in range(self.dp)])  35.8 us
    ppermute x5, waiting for transfers between devices, sum_all(): lax.ppermute(value, axis, [(i, i ^ step) for i in range(size)])  29.3 us
    ppermute x18, starting transfers between devices, send(): lax.ppermute(value, 'col', [(i, (i + 2 * step) % self.col) for i in range...  24.5 us
    unnamed x99, local copies, waits for them, and re-layouts  20.7 us
  transfers between devices with their start and end apart: 70, of which 33 were waited for; matrix products, arithmetic and copies ran while one was open for 12% of the time, Pallas kernels for 27%

profile of v5, /device:TPU:0, one launch (start us, length us, event | category | flops | bytes accessed | tf_op | source)
XLA Modules:
  0.0 767.2 jit_solution(4820325948269203118)
XLA Ops:
  14.8 14.0 %collective-permute-done = bf16[4,80,960]{2,1,0:T(8,128)(2,1)S(1)} collective-permute-done((bf16[4,80,960]{2,1,0:T(8,128)(2,1)S(1)}, bf16[4,80,960]{2,1,0:T(8,128)(2,1)S(1)}, u32[]{:S(2)}, u32[]{:S(2)}) %collective-permute-start) | collective-permute-done | bytes 614432 | tf_op jit(solution)/shard_map/ppermute | solution.py:412
  28.9 40.8 %collective-permute-done.1 = bf16[4,80,960]{2,1,0:T(8,128)(2,1)S(1)} collective-permute-done((bf16[4,80,960]{2,1,0:T(8,128)(2,1)S(1)}, bf16[4,80,960]{2,1,0:T(8,128)(2,1)S(1)}, u32[]{:S(2)}, u32[]{:S(2)}) %collective-permute-start.1) | collective-permute-done | bytes 614432 | tf_op jit(solution)/shard_map/ppermute | solution.py:412
  78.0 10.8 %collective-permute-done.5 = bf16[4,80,960]{2,1,0:T(8,128)(2,1)S(1)} collective-permute-done((bf16[4,80,960]{2,1,0:T(8,128)(2,1)S(1)}, bf16[4,80,960]{2,1,0:T(8,128)(2,1)S(1)}, u32[]{:S(2)}, u32[]{:S(2)}) %collective-permute-start.5) | collective-permute-done | bytes 614432 | tf_op jit(solution)/shard_map/ppermute | solution.py:412
  88.7 42.9 %collective-permute-done.6 = bf16[4,80,960]{2,1,0:T(8,128)(2,1)S(1)} collective-permute-done((bf16[4,80,960]{2,1,0:T(8,128)(2,1)S(1)}, bf16[4,80,960]{2,1,0:T(8,128)(2,1)S(1)}, u32[]{:S(2)}, u32[]{:S(2)}) %collective-permute-start.6) | collective-permute-done | bytes 614432 | tf_op jit(solution)/shard_map/ppermute | solution.py:412
  144.8 24.4 %collective-permute-done.8.refs_3_.refs_5_.refs_8_ = bf16[2,4,80,960]{3,2,1,0:T(8,128)(2,1)} collective-permute-done((bf16[2,4,80,960]{3,2,1,0:T(8,128)(2,1)}, bf16[2,4,80,960]{3,2,1,0:T(8,128)(2,1)}, u32[]{:S(2)}, u32[]{:S(2)}) %collective-permute-start.8) | collective-permute-done | bytes 1228832 | tf_op jit(solution)/shard_map/ppermute | solution.py:403
  189.5 29.0 %shard_map.187 = (bf16[768,960]{1,0:T(8,128)(2,1)}, bf16[768,1600]{1,0:T(8,128)(2,1)}, bf16[768,960]{1,0:T(8,128)(2,1)}, f32[16,768]{1,0:T(8,128)}, f32[768,960]{1,0:T(8,128)}, /*index=5*/bf16[768,960]{1,0:T(8,128)(2,1)}) custom-call(f32[768,960]{1,0:T(8,128)} %bitcast_convert_fusion.refs_0_.refs_2_, f32[1,960]{1,0:T(1,128)} %get-tuple-element.365.refs_1_.refs_8_, ...), custom_call_target="tpu_custom_call" | custom-call | flops 20000000000 | bytes 20971520 | tf_op jit(solution)/shard_map/pallas_call | solution.py:54
  218.5 20.1 %collective-permute-done.15.refs_1_.refs_3_.refs_6_ = bf16[4,4,80,960]{3,2,1,0:T(8,128)(2,1)} collective-permute-done((bf16[4,4,80,960]{3,2,1,0:T(8,128)(2,1)S(1)}, bf16[4,4,80,960]{3,2,1,0:T(8,128)(2,1)}, u32[]{:S(2)}, u32[]{:S(2)}) %collective-permute-start.15) | collective-permute-done | bytes 2457632 | tf_op jit(solution)/shard_map/ppermute | solution.py:400
  246.3 22.0 %shard_map.188 = (f32[768,960]{1,0:T(8,128)}, bf16[768,1280]{1,0:T(8,128)(2,1)}, bf16[768,1280]{1,0:T(8,128)(2,1)}, bf16[768,1280]{1,0:T(8,128)(2,1)}, bf16[768,1280]{1,0:T(8,128)(2,1)}) custom-call(f32[768,960]{1,0:T(8,128)} %get-tuple-element.144.refs_0_.refs_7_, bf16[768,960]{1,0:T(8,128)(2,1)} %get-tuple-element.149.refs_1_, ...), custom_call_target="tpu_custom_call" | custom-call | flops 11000000512 | bytes 31457280 | tf_op jit(solution)/shard_map/pallas_call | solution.py:54
  268.3 5.9 collective-permute-done.17.refs_3_.refs_5_.refs_8_
  288.4 28.8 %shard_map.190 = (bf16[768,960]{1,0:T(8,128)(2,1)}, bf16[768,1600]{1,0:T(8,128)(2,1)}, bf16[768,960]{1,0:T(8,128)(2,1)}, f32[16,768]{1,0:T(8,128)}, f32[768,960]{1,0:T(8,128)}, /*index=5*/bf16[768,960]{1,0:T(8,128)(2,1)}) custom-call(f32[768,960]{1,0:T(8,128)} %get-tuple-element.153.refs_0_.refs_2_, f32[1,960]{1,0:T(1,128)} %get-tuple-element.366.refs_1_.refs_8_, ...), custom_call_target="tpu_custom_call" | custom-call | flops 20000000000 | bytes 20971520 | tf_op jit(solution)/shard_map/pallas_call | solution.py:54
  317.2 22.0 %shard_map.191 = (f32[768,960]{1,0:T(8,128)}, bf16[768,1280]{1,0:T(8,128)(2,1)}, bf16[768,1280]{1,0:T(8,128)(2,1)}, bf16[768,1280]{1,0:T(8,128)(2,1)}, bf16[768,1280]{1,0:T(8,128)(2,1)}) custom-call(f32[768,960]{1,0:T(8,128)} %get-tuple-element.159.refs_0_.refs_7_, bf16[768,960]{1,0:T(8,128)(2,1)} %get-tuple-element.160.refs_1_, ...), custom_call_target="tpu_custom_call" | custom-call | flops 11000000512 | bytes 31457280 | tf_op jit(solution)/shard_map/pallas_call | solution.py:54
  339.2 22.0 %shard_map.192 = (bf16[16,3,80,960]{3,2,1,0:T(8,128)(2,1)}, f32[768,960]{1,0:T(8,128)}) custom-call(bf16[768,960]{1,0:T(8,128)(2,1)} %bitcast.492, bf16[768,960]{1,0:T(8,128)(2,1)} %get-tuple-element.160.refs_1_, bf16[768,1280]{1,0:T(8,128)(2,1)} %get-tuple-element.164.refs_2_, bf16[768,1280]{1,0:T(8,128)(2,1)} %get-tuple-element.165.refs_3_, ...), custom_call_target="tpu_custom_call" | custom-call | flops 11000000512 | bytes 31457280 | tf_op jit(solution)/shard_map/pallas_call | solution.py:54
  363.5 23.2 %shard_map.193 = (bf16[16,3,80,960]{3,2,1,0:T(8,128)(2,1)}, f32[768,960]{1,0:T(8,128)}) custom-call(bf16[768,960]{1,0:T(8,128)(2,1)} %bitcast.493, bf16[768,960]{1,0:T(8,128)(2,1)} %get-tuple-element.160.refs_1_, bf16[768,1280]{1,0:T(8,128)(2,1)} %get-tuple-element.162.refs_2_, bf16[768,1280]{1,0:T(8,128)(2,1)} %get-tuple-element.163.refs_3_, ...), custom_call_target="tpu_custom_call" | custom-call | flops 11000000512 | bytes 31457280 | tf_op jit(solution)/shard_map/pallas_call | solution.py:54
  394.8 42.1 %shard_map.194 = (bf16[1600,960]{1,0:T(8,128)(2,1)}, bf16[960,960]{1,0:T(8,128)(2,1)}, f32[768,960]{1,0:T(8,128)}, bf16[768,960]{1,0:T(8,128)(2,1)}, f32[1,960]{1,0:T(1,128)}, /*index=5*/f32[1,960]{1,0:T(1,128)}) custom-call(f32[768,960]{1,0:T(8,128)} %bitcast_convert_fusion.3.refs_0_, f32[768,960]{1,0:T(8,128)} %get-tuple-element.170.refs_1_, ...), custom_call_target="tpu_custom_call" | custom-call | flops 35000000512 | bytes 41943040 | tf_op jit(solution)/shard_map/pallas_call | solution.py:54
  453.3 22.1 %shard_map.195 = (bf16[16,3,80,960]{3,2,1,0:T(8,128)(2,1)}, f32[768,960]{1,0:T(8,128)}) custom-call(bf16[768,960]{1,0:T(8,128)(2,1)} %get-tuple-element.184.refs_0_, bf16[768,960]{1,0:T(8,128)(2,1)} %get-tuple-element.149.refs_1_, bf16[768,1280]{1,0:T(8,128)(2,1)} %get-tuple-element.187.refs_2_, bf16[768,1280]{1,0:T(8,128)(2,1)} %get-tuple-element.188.refs_3_, ...), custom_call_target="tpu_custom_call" | custom-call | flops 11000000512 | bytes 31457280 | tf_op jit(solution)/shard_map/pallas_call | solution.py:54
  488.6 23.1 %shard_map.196 = (bf16[16,3,80,960]{3,2,1,0:T(8,128)(2,1)}, f32[768,960]{1,0:T(8,128)}) custom-call(bf16[768,960]{1,0:T(8,128)(2,1)} %get-tuple-element.184.refs_0_, bf16[768,960]{1,0:T(8,128)(2,1)} %get-tuple-element.149.refs_1_, bf16[768,1280]{1,0:T(8,128)(2,1)} %get-tuple-element.185.refs_2_, bf16[768,1280]{1,0:T(8,128)(2,1)} %get-tuple-element.186.refs_3_, ...), custom_call_target="tpu_custom_call" | custom-call | flops 11000000512 | bytes 31457280 | tf_op jit(solution)/shard_map/pallas_call | solution.py:54
  530.7 41.8 %shard_map.197 = (bf16[1600,960]{1,0:T(8,128)(2,1)}, bf16[960,960]{1,0:T(8,128)(2,1)}, f32[768,960]{1,0:T(8,128)}, bf16[768,960]{1,0:T(8,128)(2,1)}, f32[1,960]{1,0:T(1,128)}, /*index=5*/f32[1,960]{1,0:T(1,128)}) custom-call(f32[768,960]{1,0:T(8,128)} %get-tuple-element.183.refs_0_, f32[768,960]{1,0:T(8,128)} %get-tuple-element.200.refs_1_, ...), custom_call_target="tpu_custom_call" | custom-call | flops 35000000512 | bytes 41943040 | tf_op jit(solution)/shard_map/pallas_call | solution.py:54
  625.0 9.5 %collective-permute-done.47 = f32[2,2,960]{2,1,0:T(2,128)S(1)} collective-permute-done((f32[2,2,960]{2,1,0:T(2,128)S(1)}, f32[2,2,960]{2,1,0:T(2,128)S(1)}, u32[]{:S(2)}, u32[]{:S(2)}) %collective-permute-start.47) | collective-permute-done | bytes 15392 | tf_op jit(solution)/shard_map/ppermute | solution.py:418
  639.2 10.9 %collective-permute-done.49 = f32[2,2,960]{2,1,0:T(2,128)S(1)} collective-permute-done((f32[2,2,960]{2,1,0:T(2,128)S(1)}, f32[2,2,960]{2,1,0:T(2,128)S(1)}, u32[]{:S(2)}, u32[]{:S(2)}) %collective-permute-start.49) | collective-permute-done | bytes 15392 | tf_op jit(solution)/shard_map/ppermute | solution.py:418
  653.2 8.9 %collective-permute-done.50 = f32[2,2,960]{2,1,0:T(2,128)S(1)} collective-permute-done((f32[2,2,960]{2,1,0:T(2,128)S(1)}, f32[2,2,960]{2,1,0:T(2,128)S(1)}, u32[]{:S(2)}, u32[]{:S(2)}) %collective-permute-start.50) | collective-permute-done | bytes 15392 | tf_op jit(solution)/shard_map/ppermute | solution.py:418
  665.6 20.1 %collective-permute-done.52 = bf16[3,80,960]{2,1,0:T(8,128)(2,1)S(1)} collective-permute-done((bf16[3,80,960]{2,1,0:T(8,128)(2,1)S(1)}, bf16[3,80,960]{2,1,0:T(8,128)(2,1)S(1)}, u32[]{:S(2)}, u32[]{:S(2)}) %collective-permute-start.52) | collective-permute-done | bytes 460832 | tf_op jit(solution)/shard_map/ppermute | solution.py:412
  692.2 18.0 %collective-permute-done.57 = bf16[2,1,80,960]{3,2,1,0:T(8,128)(2,1)S(1)} collective-permute-done((bf16[2,1,80,960]{3,2,1,0:T(8,128)(2,1)S(1)}, bf16[2,1,80,960]{3,2,1,0:T(8,128)(2,1)S(1)}, u32[]{:S(2)}, u32[]{:S(2)}) %collective-permute-start.57) | collective-permute-done | bytes 307232 | tf_op jit(solution)/shard_map/ppermute | solution.py:403
  713.7 10.5 %collective-permute-done.67 = bf16[3,80,960]{2,1,0:T(8,128)(2,1)S(1)} collective-permute-done((bf16[3,80,960]{2,1,0:T(8,128)(2,1)S(1)}, bf16[3,80,960]{2,1,0:T(8,128)(2,1)S(1)}, u32[]{:S(2)}, u32[]{:S(2)}) %collective-permute-start.67) | collective-permute-done | bytes 460832 | tf_op jit(solution)/shard_map/ppermute | solution.py:400
  724.5 10.4 %collective-permute-done.68 = bf16[3,80,960]{2,1,0:T(8,128)(2,1)S(1)} collective-permute-done((bf16[3,80,960]{2,1,0:T(8,128)(2,1)S(1)}, bf16[3,80,960]{2,1,0:T(8,128)(2,1)S(1)}, u32[]{:S(2)}, u32[]{:S(2)}) %collective-permute-start.68) | collective-permute-done | bytes 460832 | tf_op jit(solution)/shard_map/ppermute | solution.py:403
  (351 shorter events, 241.7 us)
Async XLA Ops:
  13.7 56.0 %collective-permute-start.1 = (bf16[4,80,960]{2,1,0:T(8,128)(2,1)S(1)}, bf16[4,80,960]{2,1,0:T(8,128)(2,1)S(1)}, u32[]{:S(2)}, u32[]{:S(2)}) collective-permute-start(bf16[4,80,960]{2,1,0:T(8,128)(2,1)S(1)} %get-tuple-element.347), channel_id=1, source_target_pairs={{0,4},{1,5},{2,6},{3,7},{4,0},{5,1},{6,2},{7,3},{8,12},{9,13},{10,... | collective-permute-start | bytes 1843208 | tf_op jit(solution)/shard_map/ppermute | solution.py:412
  13.7 56.0 %collective-permute-start.2 = (bf16[4,80,960]{2,1,0:T(8,128)(2,1)S(1)}, bf16[4,80,960]{2,1,0:T(8,128)(2,1)S(1)}, u32[]{:S(2)}, u32[]{:S(2)}) collective-permute-start(bf16[4,80,960]{2,1,0:T(8,128)(2,1)S(1)} %get-tuple-element.347), channel_id=1, source_target_pairs={{0,2},{1,3},{2,4},{3,5},{4,6},{5,7},{6,0},{7,1},{8,10},{9,11},{10,... | collective-permute-start | bytes 1843208 | tf_op jit(solution)/shard_map/ppermute | solution.py:412
  70.1 61.6 %collective-permute-start.3 = (bf16[4,4,80,960]{3,2,1,0:T(8,128)(2,1)S(1)}, bf16[4,4,80,960]{3,2,1,0:T(8,128)(2,1)}, u32[]{:S(2)}, u32[]{:S(2)}) collective-permute-start(bf16[4,4,80,960]{3,2,1,0:T(8,128)(2,1)S(1)} %pad_maximum_fusion.4.refs_0_.refs_2_.refs_5_), channel_id=1, source_target_pairs={{0,8},{8,0},{16,24},{24,16},{1,9},{9,1},{17,25},{25,17},{2,10},{10... | collective-permute-start | bytes 7372808 | tf_op jit(solution)/shard_map/ppermute | solution.py:400
  71.6 60.0 %collective-permute-start.4 = (bf16[4,4,80,960]{3,2,1,0:T(8,128)(2,1)S(1)}, bf16[4,4,80,960]{3,2,1,0:T(8,128)(2,1)}, u32[]{:S(2)}, u32[]{:S(2)}) collective-permute-start(bf16[4,4,80,960]{3,2,1,0:T(8,128)(2,1)S(1)} %pad_maximum_fusion.4.refs_0_.refs_2_.refs_5_), channel_id=1, source_target_pairs={{0,16},{8,24},{16,0},{24,8},{1,17},{9,25},{17,1},{25,9},{2,18},{10... | collective-permute-start | bytes 7372808 | tf_op jit(solution)/shard_map/ppermute | solution.py:403
  73.1 58.5 %collective-permute-start.6 = (bf16[4,80,960]{2,1,0:T(8,128)(2,1)S(1)}, bf16[4,80,960]{2,1,0:T(8,128)(2,1)S(1)}, u32[]{:S(2)}, u32[]{:S(2)}) collective-permute-start(bf16[4,80,960]{2,1,0:T(8,128)(2,1)S(1)} %pad_maximum_fusion.15), channel_id=1, source_target_pairs={{0,4},{1,5},{2,6},{3,7},{4,0},{5,1},{6,2},{7,3},{8,12},{9,13},{10,... | collective-permute-start | bytes 1843208 | tf_op jit(solution)/shard_map/ppermute | solution.py:412
  75.9 55.7 %collective-permute-start.7 = (bf16[4,80,960]{2,1,0:T(8,128)(2,1)S(1)}, bf16[4,80,960]{2,1,0:T(8,128)(2,1)S(1)}, u32[]{:S(2)}, u32[]{:S(2)}) collective-permute-start(bf16[4,80,960]{2,1,0:T(8,128)(2,1)S(1)} %pad_maximum_fusion.15), channel_id=1, source_target_pairs={{0,2},{1,3},{2,4},{3,5},{4,6},{5,7},{6,0},{7,1},{8,10},{9,11},{10,... | collective-permute-start | bytes 1843208 | tf_op jit(solution)/shard_map/ppermute | solution.py:412
  88.7 56.0 %collective-permute-start.10 = (bf16[4,4,80,960]{3,2,1,0:T(8,128)(2,1)S(1)}, bf16[4,4,80,960]{3,2,1,0:T(8,128)(2,1)}, u32[]{:S(2)}, u32[]{:S(2)}) collective-permute-start(bf16[4,4,80,960]{3,2,1,0:T(8,128)(2,1)S(1)} %pad_maximum_fusion.4.refs_0_.refs_2_.refs_5_), channel_id=1, source_target_pairs={{0,1},{1,0},{2,3},{3,2},{4,5},{5,4},{6,7},{7,6},{8,9},{9,8},{10,11... | collective-permute-start | bytes 7372808 | tf_op jit(solution)/shard_map/ppermute | solution.py:406
  131.7 37.7 %collective-permute-start.11 = (bf16[4,4,80,960]{3,2,1,0:T(8,128)(2,1)}, bf16[4,4,80,960]{3,2,1,0:T(8,128)(2,1)}, u32[]{:S(2)}, u32[]{:S(2)}) collective-permute-start(bf16[4,4,80,960]{3,2,1,0:T(8,128)(2,1)} %collective-permute-done.3.refs_1_.refs_3_.refs_6_), channel_id=1, source_target_pairs={{0,1},{1,0},{2,3},{3,2},{4,5},{5,4},{6,7},{7,6},{8,9},{9,8},{10,11... | collective-permute-start | bytes 7372808 | tf_op jit(solution)/shard_map/ppermute | solution.py:406
  179.5 59.0 %collective-permute-start.15 = (bf16[4,4,80,960]{3,2,1,0:T(8,128)(2,1)S(1)}, bf16[4,4,80,960]{3,2,1,0:T(8,128)(2,1)}, u32[]{:S(2)}, u32[]{:S(2)}) collective-permute-start(bf16[4,4,80,960]{3,2,1,0:T(8,128)(2,1)S(1)} %pad_maximum_fusion.5.refs_0_.refs_2_.refs_5_), channel_id=1, source_target_pairs={{0,8},{8,0},{16,24},{24,16},{1,9},{9,1},{17,25},{25,17},{2,10},{10... | collective-permute-start | bytes 7372808 | tf_op jit(solution)/shard_map/ppermute | solution.py:400
  180.1 58.7 %collective-permute-start.16 = (bf16[4,4,80,960]{3,2,1,0:T(8,128)(2,1)S(1)}, bf16[4,4,80,960]{3,2,1,0:T(8,128)(2,1)}, u32[]{:S(2)}, u32[]{:S(2)}) collective-permute-start(bf16[4,4,80,960]{3,2,1,0:T(8,128)(2,1)S(1)} %pad_maximum_fusion.5.refs_0_.refs_2_.refs_5_), channel_id=1, source_target_pairs={{0,16},{8,24},{16,0},{24,8},{1,17},{9,25},{17,1},{25,9},{2,18},{10... | collective-permute-start | bytes 7372808 | tf_op jit(solution)/shard_map/ppermute | solution.py:403
  181.7 86.7 %collective-permute-start.19 = (bf16[4,4,80,960]{3,2,1,0:T(8,128)(2,1)S(1)}, bf16[4,4,80,960]{3,2,1,0:T(8,128)(2,1)}, u32[]{:S(2)}, u32[]{:S(2)}) collective-permute-start(bf16[4,4,80,960]{3,2,1,0:T(8,128)(2,1)S(1)} %pad_maximum_fusion.5.refs_0_.refs_2_.refs_5_), channel_id=1, source_target_pairs={{0,1},{1,0},{2,3},{3,2},{4,5},{5,4},{6,7},{7,6},{8,9},{9,8},{10,11... | collective-permute-start | bytes 7372808 | tf_op jit(solution)/shard_map/ppermute | solution.py:406
  392.4 45.2 %collective-permute-start.26 = (bf16[2,2,3,80,960]{4,3,2,1,0:T(8,128)(2,1)S(1)}, bf16[2,2,3,80,960]{4,3,2,1,0:T(8,128)(2,1)S(1)}, u32[]{:S(2)}, u32[]{:S(2)}) collective-permute-start(bf16[2,2,3,80,960]{4,3,2,1,0:T(8,128)(2,1)S(1)} %pad_maximum_fusion.7), channel_id=1, source_target_pairs={{0,16},{8,24},{16,0},{24,8},{1,17},{9,25},{17,1},{25,9},{2,18},{10... | collective-permute-start | bytes 5529608 | tf_op jit(solution)/shard_map/ppermute | solution.py:403
  393.2 44.9 %collective-permute-start.25 = (bf16[2,2,3,80,960]{4,3,2,1,0:T(8,128)(2,1)S(1)}, bf16[2,2,3,80,960]{4,3,2,1,0:T(8,128)(2,1)S(1)}, u32[]{:S(2)}, u32[]{:S(2)}) collective-permute-start(bf16[2,2,3,80,960]{4,3,2,1,0:T(8,128)(2,1)S(1)} %pad_maximum_fusion.6), channel_id=1, source_target_pairs={{0,8},{8,0},{16,24},{24,16},{1,9},{9,1},{17,25},{25,17},{2,10},{10... | collective-permute-start | bytes 5529608 | tf_op jit(solution)/shard_map/ppermute | solution.py:400
  477.0 37.4 %collective-permute-start.30 = (bf16[4,4,3,80,960]{4,3,2,1,0:T(8,128)(2,1)}, bf16[4,4,3,80,960]{4,3,2,1,0:T(8,128)(2,1)}, u32[]{:S(2)}, u32[]{:S(2)}) collective-permute-start(bf16[4,4,3,80,960]{4,3,2,1,0:T(8,128)(2,1)} %bitcast.535), channel_id=1, source_target_pairs={{0,1},{1,0},{2,3},{3,2},{4,5},{5,4},{6,7},{7,6},{8,9},{9,8},{10,11... | collective-permute-start | bytes 22118408 | tf_op jit(solution)/shard_map/ppermute | solution.py:406
  488.1 41.0 %collective-permute-start.36 = (bf16[3,80,960]{2,1,0:T(8,128)(2,1)S(1)}, bf16[3,80,960]{2,1,0:T(8,128)(2,1)}, u32[]{:S(2)}, u32[]{:S(2)}) collective-permute-start(bf16[3,80,960]{2,1,0:T(8,128)(2,1)S(1)} %get-tuple-element.339), channel_id=1, source_target_pairs={{0,4},{1,5},{2,6},{3,7},{4,0},{5,1},{6,2},{7,3},{8,12},{9,13},{10,... | collective-permute-start | bytes 1382408 | tf_op jit(solution)/shard_map/ppermute | solution.py:412
  488.2 41.9 %collective-permute-start.37 = (bf16[3,80,960]{2,1,0:T(8,128)(2,1)S(1)}, bf16[3,80,960]{2,1,0:T(8,128)(2,1)}, u32[]{:S(2)}, u32[]{:S(2)}) collective-permute-start(bf16[3,80,960]{2,1,0:T(8,128)(2,1)S(1)} %get-tuple-element.338), channel_id=1, source_target_pairs={{0,6},{1,7},{2,0},{3,1},{4,2},{5,3},{6,4},{7,5},{8,14},{9,15},{10,... | collective-permute-start | bytes 1382408 | tf_op jit(solution)/shard_map/ppermute | solution.py:412
  512.5 60.0 %collective-permute-start.35 = (bf16[3,80,960]{2,1,0:T(8,128)(2,1)}, bf16[3,80,960]{2,1,0:T(8,128)(2,1)S(1)}, u32[]{:S(2)}, u32[]{:S(2)}) collective-permute-start(bf16[3,80,960]{2,1,0:T(8,128)(2,1)} %slice_bitcast_fusion.11), channel_id=1, source_target_pairs={{0,2},{1,3},{2,4},{3,5},{4,6},{5,7},{6,0},{7,1},{8,10},{9,11},{10,... | collective-permute-start | bytes 1382408 | tf_op jit(solution)/shard_map/ppermute | solution.py:412
  516.5 56.1 %collective-permute-start.39 = (bf16[2,1,80,960]{3,2,1,0:T(8,128)(2,1)}, bf16[2,1,80,960]{3,2,1,0:T(8,128)(2,1)S(1)}, u32[]{:S(2)}, u32[]{:S(2)}) collective-permute-start(bf16[2,1,80,960]{3,2,1,0:T(8,128)(2,1)} %fusion.31), channel_id=1, source_target_pairs={{0,16},{8,24},{16,0},{24,8},{1,17},{9,25},{17,1},{25,9},{2,18},{10... | collective-permute-start | bytes 921608 | tf_op jit(solution)/shard_map/ppermute | solution.py:403
  519.5 53.1 %collective-permute-start.38 = (bf16[2,1,80,960]{3,2,0,1:T(8,128)(2,1)}, bf16[2,1,80,960]{3,2,0,1:T(8,128)(2,1)}, u32[]{:S(2)}, u32[]{:S(2)}) collective-permute-start(bf16[2,1,80,960]{3,2,0,1:T(8,128)(2,1)} %fusion.33), channel_id=1, source_target_pairs={{0,8},{8,0},{16,24},{24,16},{1,9},{9,1},{17,25},{25,17},{2,10},{10... | collective-permute-start | bytes 921608 | tf_op jit(solution)/shard_map/ppermute | solution.py:400
  529.2 43.5 %collective-permute-start.34 = (bf16[2,2,3,80,960]{4,3,2,1,0:T(8,128)(2,1)}, bf16[2,2,3,80,960]{4,3,2,1,0:T(8,128)(2,1)S(1)}, u32[]{:S(2)}, u32[]{:S(2)}) collective-permute-start(bf16[2,2,3,80,960]{4,3,2,1,0:T(8,128)(2,1)} %pad_maximum_fusion.9), channel_id=1, source_target_pairs={{0,16},{8,24},{16,0},{24,8},{1,17},{9,25},{17,1},{25,9},{2,18},{10... | collective-permute-start | bytes 5529608 | tf_op jit(solution)/shard_map/ppermute | solution.py:403
  530.1 43.5 %collective-permute-start.33 = (bf16[2,2,3,80,960]{4,3,2,1,0:T(8,128)(2,1)}, bf16[2,2,3,80,960]{4,3,2,1,0:T(8,128)(2,1)S(1)}, u32[]{:S(2)}, u32[]{:S(2)}) collective-permute-start(bf16[2,2,3,80,960]{4,3,2,1,0:T(8,128)(2,1)} %pad_maximum_fusion.8), channel_id=1, source_target_pairs={{0,8},{8,0},{16,24},{24,16},{1,9},{9,1},{17,25},{25,17},{2,10},{10... | collective-permute-start | bytes 5529608 | tf_op jit(solution)/shard_map/ppermute | solution.py:400
  618.3 69.0 %collective-permute-start.55 = (bf16[2,2,1,80,960]{4,3,1,2,0:T(8,128)(2,1)S(1)}, bf16[2,2,1,80,960]{4,3,1,2,0:T(8,128)(2,1)S(1)}, u32[]{:S(2)}, u32[]{:S(2)}) collective-permute-start(bf16[2,2,1,80,960]{4,3,1,2,0:T(8,128)(2,1)S(1)} %pad_maximum_fusion.19), channel_id=1, source_target_pairs={{0,16},{8,24},{16,0},{24,8},{1,17},{9,25},{17,1},{25,9},{2,18},{10... | collective-permute-start | bytes 1843208 | tf_op jit(solution)/shard_map/ppermute | solution.py:403
  663.0 49.4 %collective-permute-start.58 = (bf16[4,80,960]{2,1,0:T(8,128)(2,1)S(1)}, bf16[4,80,960]{2,1,0:T(8,128)(2,1)S(1)}, u32[]{:S(2)}, u32[]{:S(2)}) collective-permute-start(bf16[4,80,960]{2,1,0:T(8,128)(2,1)S(1)} %pad_maximum_fusion.20), channel_id=1, source_target_pairs={{0,8},{8,0},{16,24},{24,16},{1,9},{9,1},{17,25},{25,17},{2,10},{10... | collective-permute-start | bytes 1843208 | tf_op jit(solution)/shard_map/ppermute | solution.py:400
  664.2 49.5 %collective-permute-start.59 = (bf16[4,80,960]{2,1,0:T(8,128)(2,1)S(1)}, bf16[4,80,960]{2,1,0:T(8,128)(2,1)S(1)}, u32[]{:S(2)}, u32[]{:S(2)}) collective-permute-start(bf16[4,80,960]{2,1,0:T(8,128)(2,1)S(1)} %pad_maximum_fusion.20), channel_id=1, source_target_pairs={{0,16},{8,24},{16,0},{24,8},{1,17},{9,25},{17,1},{25,9},{2,18},{10... | collective-permute-start | bytes 1843208 | tf_op jit(solution)/shard_map/ppermute | solution.py:403
  (92 other events, 1424.5 us)

commit v6 on v5

--- a/solution.py
+++ b/solution.py
@@ -411,14 +411,6 @@
     def send(self, value, step):
         return lax.ppermute(value, "col", [(i, (i + 2 * step) % self.col) for i in range(self.col)])
 
-    def sum_all(self, value):
-        for axis, size in (("dp", self.dp), ("col", self.col)):
-            step = 1
-            while step < size:
-                value = value + lax.ppermute(value, axis, [(i, i ^ step) for i in range(size)])
-                step *= 2
-        return value
-
 
 def add(*terms):
     total = terms[0].astype(jnp.float32)
@@ -568,11 +560,14 @@
     )
 
 
-def attention_shares(links, qkv_grad, output_grad, rows):
+def attention_shares(links, qkv_grad, output_grad, rows, everywhere=None):
     width = output_grad.shape[1]
     cut = rows[0] * links.col
     parts = [g.reshape(links.col, -1, width) for g in (qkv_grad[:cut], qkv_grad[cut:], output_grad)]
     whole = jnp.concatenate(parts, axis=1).reshape(links.line, 2, 4, -1, width)
+    if everywhere is not None:
+        more = jnp.broadcast_to(everywhere, (*whole.shape[:3], *everywhere.shape))
+        whole = jnp.concatenate([whole, more], axis=3)
     return [lax.dynamic_index_in_dim(whole, links.core ^ core, 1, False) for core in range(2)]
 
 
@@ -674,26 +669,33 @@
         results = attention_backward(grad, grad_normed, *kept, *gains[layer], *attn_w, *where)
         results = advance(results, new_move, *last_ffn, *last_attn)
         qkv_w_grad, output_grad, grad, grad_low, *gain_grads = results
-        ours, others = attention_shares(links, qkv_w_grad, output_grad, rows)
+        gain_terms[layer] = gain_grads
+        everywhere = None
+        if layer == 0:
+            terms = [gain_terms[i][kind] for kind in range(2) for i in range(layers)]
+            pad = jnp.zeros((-len(terms) % 16, width), jnp.float32)
+            everywhere = jnp.concatenate([*terms, pad]).astype(jnp.bfloat16)
+        ours, others = attention_shares(links, qkv_w_grad, output_grad, rows, everywhere)
         moves[layer] = (attn_move, ffn_move) = (
             Transfer(scatter_stages(links, [ours], others, attn_pick, True)),
             new_move,
         )
-        gain_terms[layer] = jnp.stack(gain_grads)
-    gain_terms = jnp.concatenate(gain_terms, axis=1)
-    gain_terms = advance(gain_terms, ffn_move, attn_move, *last_attn)
+    advance(None, ffn_move, attn_move, *last_attn)
     rest = []
     for layer in range(1, layers):
         total = jnp.concatenate([moves[layer][1].finish(), moves[layer][0].finish()])
-        total = settle(total, ffn_move.flying[0], ffn_move.flying[-1])
+        total = settle(total, ffn_move.flying[len(ffn_move.flying) // 2], *attn_move.flying)
         rest.append(Transfer(quarter_stages(links, total)))
-    gains = advance(links.sum_all(gain_terms), ffn_move, attn_move)
+    advance(None, ffn_move, attn_move, *rest)
     last = Transfer(quarter_stages(links, ffn_move.finish()))
-    gains = advance(gains, attn_move, *rest)
-    tail = Transfer(quarter_stages(links, attn_move.finish()))
-    shares = [(last.finish(), tail.finish())]
-    for transfer in rest:
-        quarters = transfer.finish()
+    advance(None, attn_move, last)
+    done = settle([transfer.finish() for transfer in (last, *rest)], attn_move.flying[0])
+    total = attn_move.finish()
+    part = rows[0] + rows[1] + rows[2]
+    gains = total[0, part // 4 :][: 2 * layers].astype(jnp.float32).reshape(2, layers, width)
+    tail = Transfer(quarter_stages(links, total[:, : part // 4]))
+    shares = [(done[0], tail.finish())]
+    for quarters in done[1:]:
         shares.append(([q[:3] for q in quarters], [q[3:] for q in quarters]))
 
     sums = [[] for _ in range(6)]

time: 773 us -> 769 us (level)
  waiting for transfers between devices: 274 us -> 238 us
  starting transfers between devices: 69.9 us -> 93.5 us
    ppermute x18, starting transfers between devices: 24.5 us -> 54.5 us  [send(): lax.ppermute(value, 'col', [(i, (i + 2 * step) % self.col) for i in range...]
    ppermute x5 -> x0, waiting for transfers between devices: 29.3 us -> none  [sum_all(): lax.ppermute(value, axis, [(i, i ^ step) for i in range(size)])]
    ppermute x18, waiting for transfers between devices: 140 us -> 157 us  [send(): lax.ppermute(value, 'col', [(i, (i + 2 * step) % self.col) for i in range...]
    ppermute x15, waiting for transfers between devices: 35.8 us -> 22.5 us  [x(): return lax.ppermute(value, 'dp', [(i, i ^ 1) for i in range(self.dp)])]
    ppermute x15, waiting for transfers between devices: 65.9 us -> 56.3 us  [y(): return lax.ppermute(value, 'dp', [(i, i ^ 2) for i in range(self.dp)])]
    unnamed x99 -> x129, local copies, waits for them, and re-layouts: 20.7 us -> 24.8 us
    convert_element_type x16 -> x18, other arithmetic: 42.6 us -> 41.8 us  [add(): return total.astype(jnp.bfloat16)]
  transfers between devices with their start and end apart: 70 -> 65, of which waited for: 33 -> 24; matrix products, arithmetic and copies ran while one was open for 12% -> 12% of each run, Pallas kernels for 27% -> 27%
where the time goes in v6:
time: 769 us; the launch traced here: 762 us
  Pallas kernels  284 us (37%)
  waiting for transfers between devices  238 us (31%)
  starting transfers between devices  93.5 us (12%)
  other arithmetic  78.1 us (10%)
  local copies, waits for them, and re-layouts  66.4 us (9%)
    pallas_call x12, Pallas kernels, call(): pl.pallas_call(run, out_shape=outs, in_specs=list(specs) + [pl.BlockSpec(...  284 us
    ppermute x18, waiting for transfers between devices, send(): lax.ppermute(value, 'col', [(i, (i + 2 * step) % self.col) for i in range...  157 us
    ppermute x15, waiting for transfers between devices, y(): return lax.ppermute(value, 'dp', [(i, i ^ 2) for i in range(self.dp)])  56.3 us
    ppermute x18, starting transfers between devices, send(): lax.ppermute(value, 'col', [(i, (i + 2 * step) % self.col) for i in range...  54.5 us
    convert_element_type x18, other arithmetic, add(): return total.astype(jnp.bfloat16)  41.8 us
    unnamed x129, local copies, waits for them, and re-layouts  24.8 us
    ppermute x15, waiting for transfers between devices, x(): return lax.ppermute(value, 'dp', [(i, i ^ 1) for i in range(self.dp)])  22.5 us
    ppermute x15, starting transfers between devices, x(): return lax.ppermute(value, 'dp', [(i, i ^ 1) for i in range(self.dp)])  17.1 us
  transfers between devices with their start and end apart: 65, of which 24 were waited for; matrix products, arithmetic and copies ran while one was open for 12% of the time, Pallas kernels for 27%

profile of v6, /device:TPU:0, one launch (start us, length us, event | category | flops | bytes accessed | tf_op | source)
XLA Modules:
  0.0 762.0 jit_solution(1147675952753958481)
XLA Ops:
  14.8 14.0 %collective-permute-done = bf16[4,80,960]{2,1,0:T(8,128)(2,1)S(1)} collective-permute-done((bf16[4,80,960]{2,1,0:T(8,128)(2,1)S(1)}, bf16[4,80,960]{2,1,0:T(8,128)(2,1)S(1)}, u32[]{:S(2)}, u32[]{:S(2)}) %collective-permute-start) | collective-permute-done | bytes 614432 | tf_op jit(solution)/shard_map/ppermute | solution.py:412
  28.9 40.8 %collective-permute-done.1 = bf16[4,80,960]{2,1,0:T(8,128)(2,1)S(1)} collective-permute-done((bf16[4,80,960]{2,1,0:T(8,128)(2,1)S(1)}, bf16[4,80,960]{2,1,0:T(8,128)(2,1)S(1)}, u32[]{:S(2)}, u32[]{:S(2)}) %collective-permute-start.1) | collective-permute-done | bytes 614432 | tf_op jit(solution)/shard_map/ppermute | solution.py:412
  78.0 10.8 %collective-permute-done.5 = bf16[4,80,960]{2,1,0:T(8,128)(2,1)S(1)} collective-permute-done((bf16[4,80,960]{2,1,0:T(8,128)(2,1)S(1)}, bf16[4,80,960]{2,1,0:T(8,128)(2,1)S(1)}, u32[]{:S(2)}, u32[]{:S(2)}) %collective-permute-start.5) | collective-permute-done | bytes 614432 | tf_op jit(solution)/shard_map/ppermute | solution.py:412
  88.7 42.9 %collective-permute-done.6 = bf16[4,80,960]{2,1,0:T(8,128)(2,1)S(1)} collective-permute-done((bf16[4,80,960]{2,1,0:T(8,128)(2,1)S(1)}, bf16[4,80,960]{2,1,0:T(8,128)(2,1)S(1)}, u32[]{:S(2)}, u32[]{:S(2)}) %collective-permute-start.6) | collective-permute-done | bytes 614432 | tf_op jit(solution)/shard_map/ppermute | solution.py:412
  144.8 24.4 %collective-permute-done.8.refs_3_.refs_5_.refs_8_ = bf16[2,4,80,960]{3,2,1,0:T(8,128)(2,1)} collective-permute-done((bf16[2,4,80,960]{3,2,1,0:T(8,128)(2,1)}, bf16[2,4,80,960]{3,2,1,0:T(8,128)(2,1)}, u32[]{:S(2)}, u32[]{:S(2)}) %collective-permute-start.8) | collective-permute-done | bytes 1228832 | tf_op jit(solution)/shard_map/ppermute | solution.py:403
  189.6 28.8 %shard_map.187 = (bf16[768,960]{1,0:T(8,128)(2,1)}, bf16[768,1600]{1,0:T(8,128)(2,1)}, bf16[768,960]{1,0:T(8,128)(2,1)}, f32[16,768]{1,0:T(8,128)}, f32[768,960]{1,0:T(8,128)}, /*index=5*/bf16[768,960]{1,0:T(8,128)(2,1)}) custom-call(f32[768,960]{1,0:T(8,128)} %bitcast_convert_fusion.refs_0_.refs_2_, f32[1,960]{1,0:T(1,128)} %get-tuple-element.389.refs_1_.refs_8_, ...), custom_call_target="tpu_custom_call" | custom-call | flops 20000000000 | bytes 20971520 | tf_op jit(solution)/shard_map/pallas_call | solution.py:54
  218.4 20.2 %collective-permute-done.15.refs_1_.refs_3_.refs_6_ = bf16[4,4,80,960]{3,2,1,0:T(8,128)(2,1)} collective-permute-done((bf16[4,4,80,960]{3,2,1,0:T(8,128)(2,1)S(1)}, bf16[4,4,80,960]{3,2,1,0:T(8,128)(2,1)}, u32[]{:S(2)}, u32[]{:S(2)}) %collective-permute-start.15) | collective-permute-done | bytes 2457632 | tf_op jit(solution)/shard_map/ppermute | solution.py:400
  246.3 22.1 %shard_map.188 = (f32[768,960]{1,0:T(8,128)}, bf16[768,1280]{1,0:T(8,128)(2,1)}, bf16[768,1280]{1,0:T(8,128)(2,1)}, bf16[768,1280]{1,0:T(8,128)(2,1)}, bf16[768,1280]{1,0:T(8,128)(2,1)}) custom-call(f32[768,960]{1,0:T(8,128)} %get-tuple-element.152.refs_0_.refs_7_, bf16[768,960]{1,0:T(8,128)(2,1)} %get-tuple-element.157.refs_1_, ...), custom_call_target="tpu_custom_call" | custom-call | flops 11000000512 | bytes 31457280 | tf_op jit(solution)/shard_map/pallas_call | solution.py:54
  268.4 5.9 collective-permute-done.17.refs_3_.refs_5_.refs_8_
  288.5 28.8 %shard_map.190 = (bf16[768,960]{1,0:T(8,128)(2,1)}, bf16[768,1600]{1,0:T(8,128)(2,1)}, bf16[768,960]{1,0:T(8,128)(2,1)}, f32[16,768]{1,0:T(8,128)}, f32[768,960]{1,0:T(8,128)}, /*index=5*/bf16[768,960]{1,0:T(8,128)(2,1)}) custom-call(f32[768,960]{1,0:T(8,128)} %get-tuple-element.161.refs_0_.refs_2_, f32[1,960]{1,0:T(1,128)} %get-tuple-element.390.refs_1_.refs_8_, ...), custom_call_target="tpu_custom_call" | custom-call | flops 20000000000 | bytes 20971520 | tf_op jit(solution)/shard_map/pallas_call | solution.py:54
  317.3 22.1 %shard_map.191 = (f32[768,960]{1,0:T(8,128)}, bf16[768,1280]{1,0:T(8,128)(2,1)}, bf16[768,1280]{1,0:T(8,128)(2,1)}, bf16[768,1280]{1,0:T(8,128)(2,1)}, bf16[768,1280]{1,0:T(8,128)(2,1)}) custom-call(f32[768,960]{1,0:T(8,128)} %get-tuple-element.167.refs_0_.refs_7_, bf16[768,960]{1,0:T(8,128)(2,1)} %get-tuple-element.168.refs_1_, ...), custom_call_target="tpu_custom_call" | custom-call | flops 11000000512 | bytes 31457280 | tf_op jit(solution)/shard_map/pallas_call | solution.py:54
  339.4 22.0 %shard_map.192 = (bf16[16,3,80,960]{3,2,1,0:T(8,128)(2,1)}, f32[768,960]{1,0:T(8,128)}) custom-call(bf16[768,960]{1,0:T(8,128)(2,1)} %bitcast.440, bf16[768,960]{1,0:T(8,128)(2,1)} %get-tuple-element.168.refs_1_, bf16[768,1280]{1,0:T(8,128)(2,1)} %get-tuple-element.172.refs_2_, bf16[768,1280]{1,0:T(8,128)(2,1)} %get-tuple-element.173.refs_3_, ...), custom_call_target="tpu_custom_call" | custom-call | flops 11000000512 | bytes 31457280 | tf_op jit(solution)/shard_map/pallas_call | solution.py:54
  363.7 23.2 %shard_map.193 = (bf16[16,3,80,960]{3,2,1,0:T(8,128)(2,1)}, f32[768,960]{1,0:T(8,128)}) custom-call(bf16[768,960]{1,0:T(8,128)(2,1)} %bitcast.441, bf16[768,960]{1,0:T(8,128)(2,1)} %get-tuple-element.168.refs_1_, bf16[768,1280]{1,0:T(8,128)(2,1)} %get-tuple-element.170.refs_2_, bf16[768,1280]{1,0:T(8,128)(2,1)} %get-tuple-element.171.refs_3_, ...), custom_call_target="tpu_custom_call" | custom-call | flops 11000000512 | bytes 31457280 | tf_op jit(solution)/shard_map/pallas_call | solution.py:54
  386.9 5.5 add_convert_fusion.9
  395.0 42.3 %shard_map.194 = (bf16[1600,960]{1,0:T(8,128)(2,1)}, bf16[960,960]{1,0:T(8,128)(2,1)}, f32[768,960]{1,0:T(8,128)}, bf16[768,960]{1,0:T(8,128)(2,1)}, f32[1,960]{1,0:T(1,128)}, /*index=5*/f32[1,960]{1,0:T(1,128)}) custom-call(f32[768,960]{1,0:T(8,128)} %bitcast_convert_fusion.3.refs_0_, f32[768,960]{1,0:T(8,128)} %get-tuple-element.178.refs_1_, ...), custom_call_target="tpu_custom_call" | custom-call | flops 35000000512 | bytes 41943040 | tf_op jit(solution)/shard_map/pallas_call | solution.py:54
  455.8 22.1 %shard_map.195 = (bf16[16,3,80,960]{3,2,1,0:T(8,128)(2,1)}, f32[768,960]{1,0:T(8,128)}) custom-call(bf16[768,960]{1,0:T(8,128)(2,1)} %get-tuple-element.192.refs_0_, bf16[768,960]{1,0:T(8,128)(2,1)} %get-tuple-element.157.refs_1_, bf16[768,1280]{1,0:T(8,128)(2,1)} %get-tuple-element.195.refs_2_, bf16[768,1280]{1,0:T(8,128)(2,1)} %get-tuple-element.196.refs_3_, ...), custom_call_target="tpu_custom_call" | custom-call | flops 11000000512 | bytes 31457280 | tf_op jit(solution)/shard_map/pallas_call | solution.py:54
  490.2 23.0 %shard_map.196 = (bf16[16,3,80,960]{3,2,1,0:T(8,128)(2,1)}, f32[768,960]{1,0:T(8,128)}) custom-call(bf16[768,960]{1,0:T(8,128)(2,1)} %get-tuple-element.192.refs_0_, bf16[768,960]{1,0:T(8,128)(2,1)} %get-tuple-element.157.refs_1_, bf16[768,1280]{1,0:T(8,128)(2,1)} %get-tuple-element.193.refs_2_, bf16[768,1280]{1,0:T(8,128)(2,1)} %get-tuple-element.194.refs_3_, ...), custom_call_target="tpu_custom_call" | custom-call | flops 11000000512 | bytes 31457280 | tf_op jit(solution)/shard_map/pallas_call | solution.py:54
  529.6 41.8 %shard_map.197 = (bf16[1600,960]{1,0:T(8,128)(2,1)}, bf16[960,960]{1,0:T(8,128)(2,1)}, f32[768,960]{1,0:T(8,128)}, bf16[768,960]{1,0:T(8,128)(2,1)}, f32[1,960]{1,0:T(1,128)}, /*index=5*/f32[1,960]{1,0:T(1,128)}) custom-call(f32[768,960]{1,0:T(8,128)} %get-tuple-element.191.refs_0_, f32[768,960]{1,0:T(8,128)} %get-tuple-element.208.refs_1_, ...), custom_call_target="tpu_custom_call" | custom-call | flops 35000000512 | bytes 41943040 | tf_op jit(solution)/shard_map/pallas_call | solution.py:54
  597.7 6.2 collective-permute-start.43
  638.3 16.5 %collective-permute-done.47 = bf16[3,80,960]{2,1,0:T(8,128)(2,1)S(1)} collective-permute-done((bf16[3,80,960]{2,1,0:T(8,128)(2,1)S(1)}, bf16[3,80,960]{2,1,0:T(8,128)(2,1)S(1)}, u32[]{:S(2)}, u32[]{:S(2)}) %collective-permute-start.47) | collective-permute-done | bytes 460832 | tf_op jit(solution)/shard_map/ppermute | solution.py:412
  658.3 9.5 %collective-permute-start.46 = (bf16[3,80,960]{2,1,0:T(8,128)(2,1)S(1)}, bf16[3,80,960]{2,1,0:T(8,128)(2,1)S(1)}, u32[]{:S(2)}, u32[]{:S(2)}) collective-permute-start(bf16[3,80,960]{2,1,0:T(8,128)(2,1)S(1)} %slice_bitcast_fusion.8), channel_id=1, source_target_pairs={{0,2},{1,3},{2,4},{3,5},{4,6},{5,7},{6,0},{7,1},{8,10},{9,11},{10,... | collective-permute-start | bytes 1382408 | tf_op jit(solution)/shard_map/ppermute | solution.py:412
  667.8 13.2 %collective-permute-done.46 = bf16[3,80,960]{2,1,0:T(8,128)(2,1)S(1)} collective-permute-done((bf16[3,80,960]{2,1,0:T(8,128)(2,1)S(1)}, bf16[3,80,960]{2,1,0:T(8,128)(2,1)S(1)}, u32[]{:S(2)}, u32[]{:S(2)}) %collective-permute-start.46) | collective-permute-done | bytes 460832 | tf_op jit(solution)/shard_map/ppermute | solution.py:412
  689.9 23.0 %collective-permute-done.55 = bf16[2,1,96,960]{3,2,0,1:T(8,128)(2,1)S(1)} collective-permute-done((bf16[2,1,96,960]{3,2,0,1:T(8,128)(2,1)S(1)}, bf16[2,1,96,960]{3,2,0,1:T(8,128)(2,1)S(1)}, u32[]{:S(2)}, u32[]{:S(2)}) %collective-permute-start.55) | collective-permute-done | bytes 368672 | tf_op jit(solution)/shard_map/ppermute | solution.py:403
  715.0 14.5 %collective-permute-start.59 = (bf16[1,96,960]{2,1,0:T(8,128)(2,1)}, bf16[1,96,960]{2,1,0:T(8,128)(2,1)}, u32[]{:S(2)}, u32[]{:S(2)}) collective-permute-start(bf16[1,96,960]{2,1,0:T(8,128)(2,1)} %get-tuple-element.364), channel_id=1, source_target_pairs={{0,2},{1,3},{2,4},{3,5},{4,6},{5,7},{6,0},{7,1},{8,10},{9,11},{10,... | collective-permute-start | bytes 552968 | tf_op jit(solution)/shard_map/ppermute | solution.py:412
  (379 shorter events, 236.0 us)
Async XLA Ops:
  13.7 56.0 %collective-permute-start.1 = (bf16[4,80,960]{2,1,0:T(8,128)(2,1)S(1)}, bf16[4,80,960]{2,1,0:T(8,128)(2,1)S(1)}, u32[]{:S(2)}, u32[]{:S(2)}) collective-permute-start(bf16[4,80,960]{2,1,0:T(8,128)(2,1)S(1)} %get-tuple-element.371), channel_id=1, source_target_pairs={{0,4},{1,5},{2,6},{3,7},{4,0},{5,1},{6,2},{7,3},{8,12},{9,13},{10,... | collective-permute-start | bytes 1843208 | tf_op jit(solution)/shard_map/ppermute | solution.py:412
  13.7 56.0 %collective-permute-start.2 = (bf16[4,80,960]{2,1,0:T(8,128)(2,1)S(1)}, bf16[4,80,960]{2,1,0:T(8,128)(2,1)S(1)}, u32[]{:S(2)}, u32[]{:S(2)}) collective-permute-start(bf16[4,80,960]{2,1,0:T(8,128)(2,1)S(1)} %get-tuple-element.371), channel_id=1, source_target_pairs={{0,2},{1,3},{2,4},{3,5},{4,6},{5,7},{6,0},{7,1},{8,10},{9,11},{10,... | collective-permute-start | bytes 1843208 | tf_op jit(solution)/shard_map/ppermute | solution.py:412
  70.1 61.6 %collective-permute-start.3 = (bf16[4,4,80,960]{3,2,1,0:T(8,128)(2,1)S(1)}, bf16[4,4,80,960]{3,2,1,0:T(8,128)(2,1)}, u32[]{:S(2)}, u32[]{:S(2)}) collective-permute-start(bf16[4,4,80,960]{3,2,1,0:T(8,128)(2,1)S(1)} %pad_maximum_fusion.4.refs_0_.refs_2_.refs_5_), channel_id=1, source_target_pairs={{0,8},{8,0},{16,24},{24,16},{1,9},{9,1},{17,25},{25,17},{2,10},{10... | collective-permute-start | bytes 7372808 | tf_op jit(solution)/shard_map/ppermute | solution.py:400
  71.6 60.0 %collective-permute-start.4 = (bf16[4,4,80,960]{3,2,1,0:T(8,128)(2,1)S(1)}, bf16[4,4,80,960]{3,2,1,0:T(8,128)(2,1)}, u32[]{:S(2)}, u32[]{:S(2)}) collective-permute-start(bf16[4,4,80,960]{3,2,1,0:T(8,128)(2,1)S(1)} %pad_maximum_fusion.4.refs_0_.refs_2_.refs_5_), channel_id=1, source_target_pairs={{0,16},{8,24},{16,0},{24,8},{1,17},{9,25},{17,1},{25,9},{2,18},{10... | collective-permute-start | bytes 7372808 | tf_op jit(solution)/shard_map/ppermute | solution.py:403
  73.1 58.5 %collective-permute-start.6 = (bf16[4,80,960]{2,1,0:T(8,128)(2,1)S(1)}, bf16[4,80,960]{2,1,0:T(8,128)(2,1)S(1)}, u32[]{:S(2)}, u32[]{:S(2)}) collective-permute-start(bf16[4,80,960]{2,1,0:T(8,128)(2,1)S(1)} %pad_maximum_fusion.17), channel_id=1, source_target_pairs={{0,4},{1,5},{2,6},{3,7},{4,0},{5,1},{6,2},{7,3},{8,12},{9,13},{10,... | collective-permute-start | bytes 1843208 | tf_op jit(solution)/shard_map/ppermute | solution.py:412
  75.9 55.7 %collective-permute-start.7 = (bf16[4,80,960]{2,1,0:T(8,128)(2,1)S(1)}, bf16[4,80,960]{2,1,0:T(8,128)(2,1)S(1)}, u32[]{:S(2)}, u32[]{:S(2)}) collective-permute-start(bf16[4,80,960]{2,1,0:T(8,128)(2,1)S(1)} %pad_maximum_fusion.17), channel_id=1, source_target_pairs={{0,2},{1,3},{2,4},{3,5},{4,6},{5,7},{6,0},{7,1},{8,10},{9,11},{10,... | collective-permute-start | bytes 1843208 | tf_op jit(solution)/shard_map/ppermute | solution.py:412
  88.7 56.0 %collective-permute-start.10 = (bf16[4,4,80,960]{3,2,1,0:T(8,128)(2,1)S(1)}, bf16[4,4,80,960]{3,2,1,0:T(8,128)(2,1)}, u32[]{:S(2)}, u32[]{:S(2)}) collective-permute-start(bf16[4,4,80,960]{3,2,1,0:T(8,128)(2,1)S(1)} %pad_maximum_fusion.4.refs_0_.refs_2_.refs_5_), channel_id=1, source_target_pairs={{0,1},{1,0},{2,3},{3,2},{4,5},{5,4},{6,7},{7,6},{8,9},{9,8},{10,11... | collective-permute-start | bytes 7372808 | tf_op jit(solution)/shard_map/ppermute | solution.py:406
  131.7 37.7 %collective-permute-start.11 = (bf16[4,4,80,960]{3,2,1,0:T(8,128)(2,1)}, bf16[4,4,80,960]{3,2,1,0:T(8,128)(2,1)}, u32[]{:S(2)}, u32[]{:S(2)}) collective-permute-start(bf16[4,4,80,960]{3,2,1,0:T(8,128)(2,1)} %collective-permute-done.3.refs_1_.refs_3_.refs_6_), channel_id=1, source_target_pairs={{0,1},{1,0},{2,3},{3,2},{4,5},{5,4},{6,7},{7,6},{8,9},{9,8},{10,11... | collective-permute-start | bytes 7372808 | tf_op jit(solution)/shard_map/ppermute | solution.py:406
  132.7 36.7 %collective-permute-start.12 = (bf16[4,4,80,960]{3,2,1,0:T(8,128)(2,1)}, bf16[4,4,80,960]{3,2,1,0:T(8,128)(2,1)}, u32[]{:S(2)}, u32[]{:S(2)}) collective-permute-start(bf16[4,4,80,960]{3,2,1,0:T(8,128)(2,1)} %collective-permute-done.4.refs_2_.refs_4_.refs_7_), channel_id=1, source_target_pairs={{0,1},{1,0},{2,3},{3,2},{4,5},{5,4},{6,7},{7,6},{8,9},{9,8},{10,11... | collective-permute-start | bytes 7372808 | tf_op jit(solution)/shard_map/ppermute | solution.py:406
  179.6 59.0 %collective-permute-start.15 = (bf16[4,4,80,960]{3,2,1,0:T(8,128)(2,1)S(1)}, bf16[4,4,80,960]{3,2,1,0:T(8,128)(2,1)}, u32[]{:S(2)}, u32[]{:S(2)}) collective-permute-start(bf16[4,4,80,960]{3,2,1,0:T(8,128)(2,1)S(1)} %pad_maximum_fusion.5.refs_0_.refs_2_.refs_5_), channel_id=1, source_target_pairs={{0,8},{8,0},{16,24},{24,16},{1,9},{9,1},{17,25},{25,17},{2,10},{10... | collective-permute-start | bytes 7372808 | tf_op jit(solution)/shard_map/ppermute | solution.py:400
  180.2 58.7 %collective-permute-start.16 = (bf16[4,4,80,960]{3,2,1,0:T(8,128)(2,1)S(1)}, bf16[4,4,80,960]{3,2,1,0:T(8,128)(2,1)}, u32[]{:S(2)}, u32[]{:S(2)}) collective-permute-start(bf16[4,4,80,960]{3,2,1,0:T(8,128)(2,1)S(1)} %pad_maximum_fusion.5.refs_0_.refs_2_.refs_5_), channel_id=1, source_target_pairs={{0,16},{8,24},{16,0},{24,8},{1,17},{9,25},{17,1},{25,9},{2,18},{10... | collective-permute-start | bytes 7372808 | tf_op jit(solution)/shard_map/ppermute | solution.py:403
  181.7 86.7 %collective-permute-start.19 = (bf16[4,4,80,960]{3,2,1,0:T(8,128)(2,1)S(1)}, bf16[4,4,80,960]{3,2,1,0:T(8,128)(2,1)}, u32[]{:S(2)}, u32[]{:S(2)}) collective-permute-start(bf16[4,4,80,960]{3,2,1,0:T(8,128)(2,1)S(1)} %pad_maximum_fusion.5.refs_0_.refs_2_.refs_5_), channel_id=1, source_target_pairs={{0,1},{1,0},{2,3},{3,2},{4,5},{5,4},{6,7},{7,6},{8,9},{9,8},{10,11... | collective-permute-start | bytes 7372808 | tf_op jit(solution)/shard_map/ppermute | solution.py:406
  238.9 36.5 %collective-permute-start.20 = (bf16[4,4,80,960]{3,2,1,0:T(8,128)(2,1)}, bf16[4,4,80,960]{3,2,1,0:T(8,128)(2,1)}, u32[]{:S(2)}, u32[]{:S(2)}) collective-permute-start(bf16[4,4,80,960]{3,2,1,0:T(8,128)(2,1)} %collective-permute-done.15.refs_1_.refs_3_.refs_6_), channel_id=1, source_target_pairs={{0,1},{1,0},{2,3},{3,2},{4,5},{5,4},{6,7},{7,6},{8,9},{9,8},{10,11... | collective-permute-start | bytes 7372808 | tf_op jit(solution)/shard_map/ppermute | solution.py:406
  238.9 36.5 %collective-permute-start.21 = (bf16[4,4,80,960]{3,2,1,0:T(8,128)(2,1)}, bf16[4,4,80,960]{3,2,1,0:T(8,128)(2,1)}, u32[]{:S(2)}, u32[]{:S(2)}) collective-permute-start(bf16[4,4,80,960]{3,2,1,0:T(8,128)(2,1)} %collective-permute-done.16.refs_2_.refs_4_.refs_7_), channel_id=1, source_target_pairs={{0,1},{1,0},{2,3},{3,2},{4,5},{5,4},{6,7},{7,6},{8,9},{9,8},{10,11... | collective-permute-start | bytes 7372808 | tf_op jit(solution)/shard_map/ppermute | solution.py:406
  392.6 45.2 %collective-permute-start.26 = (bf16[2,2,3,80,960]{4,3,2,1,0:T(8,128)(2,1)S(1)}, bf16[2,2,3,80,960]{4,3,2,1,0:T(8,128)(2,1)S(1)}, u32[]{:S(2)}, u32[]{:S(2)}) collective-permute-start(bf16[2,2,3,80,960]{4,3,2,1,0:T(8,128)(2,1)S(1)} %pad_maximum_fusion.7), channel_id=1, source_target_pairs={{0,16},{8,24},{16,0},{24,8},{1,17},{9,25},{17,1},{25,9},{2,18},{10... | collective-permute-start | bytes 5529608 | tf_op jit(solution)/shard_map/ppermute | solution.py:403
  393.4 44.9 %collective-permute-start.25 = (bf16[2,2,3,80,960]{4,3,2,1,0:T(8,128)(2,1)S(1)}, bf16[2,2,3,80,960]{4,3,2,1,0:T(8,128)(2,1)S(1)}, u32[]{:S(2)}, u32[]{:S(2)}) collective-permute-start(bf16[2,2,3,80,960]{4,3,2,1,0:T(8,128)(2,1)S(1)} %pad_maximum_fusion.6), channel_id=1, source_target_pairs={{0,8},{8,0},{16,24},{24,16},{1,9},{9,1},{17,25},{25,17},{2,10},{10... | collective-permute-start | bytes 5529608 | tf_op jit(solution)/shard_map/ppermute | solution.py:400
  478.9 36.8 %collective-permute-start.30 = (bf16[4,4,3,80,960]{4,3,2,1,0:T(8,128)(2,1)}, bf16[4,4,3,80,960]{4,3,2,1,0:T(8,128)(2,1)}, u32[]{:S(2)}, u32[]{:S(2)}) collective-permute-start(bf16[4,4,3,80,960]{4,3,2,1,0:T(8,128)(2,1)} %bitcast.480), channel_id=1, source_target_pairs={{0,1},{1,0},{2,3},{3,2},{4,5},{5,4},{6,7},{7,6},{8,9},{9,8},{10,11... | collective-permute-start | bytes 22118408 | tf_op jit(solution)/shard_map/ppermute | solution.py:406
  489.3 38.5 %collective-permute-start.36 = (bf16[3,80,960]{2,1,0:T(8,128)(2,1)}, bf16[3,80,960]{2,1,0:T(8,128)(2,1)}, u32[]{:S(2)}, u32[]{:S(2)}) collective-permute-start(bf16[3,80,960]{2,1,0:T(8,128)(2,1)} %get-tuple-element.363), channel_id=1, source_target_pairs={{0,4},{1,5},{2,6},{3,7},{4,0},{5,1},{6,2},{7,3},{8,12},{9,13},{10,... | collective-permute-start | bytes 1382408 | tf_op jit(solution)/shard_map/ppermute | solution.py:412
  489.6 39.4 %collective-permute-start.37 = (bf16[3,80,960]{2,1,0:T(8,128)(2,1)}, bf16[3,80,960]{2,1,0:T(8,128)(2,1)}, u32[]{:S(2)}, u32[]{:S(2)}) collective-permute-start(bf16[3,80,960]{2,1,0:T(8,128)(2,1)} %get-tuple-element.362), channel_id=1, source_target_pairs={{0,6},{1,7},{2,0},{3,1},{4,2},{5,3},{6,4},{7,5},{8,14},{9,15},{10,... | collective-permute-start | bytes 1382408 | tf_op jit(solution)/shard_map/ppermute | solution.py:412
  514.1 57.3 %collective-permute-start.35 = (bf16[3,80,960]{2,1,0:T(8,128)(2,1)}, bf16[3,80,960]{2,1,0:T(8,128)(2,1)}, u32[]{:S(2)}, u32[]{:S(2)}) collective-permute-start(bf16[3,80,960]{2,1,0:T(8,128)(2,1)} %slice_bitcast_fusion.11), channel_id=1, source_target_pairs={{0,2},{1,3},{2,4},{3,5},{4,6},{5,7},{6,0},{7,1},{8,10},{9,11},{10,... | collective-permute-start | bytes 1382408 | tf_op jit(solution)/shard_map/ppermute | solution.py:412
  517.8 53.6 %collective-permute-start.39 = (bf16[2,1,80,960]{3,2,1,0:T(8,128)(2,1)}, bf16[2,1,80,960]{3,2,1,0:T(8,128)(2,1)}, u32[]{:S(2)}, u32[]{:S(2)}) collective-permute-start(bf16[2,1,80,960]{3,2,1,0:T(8,128)(2,1)} %fusion.32), channel_id=1, source_target_pairs={{0,16},{8,24},{16,0},{24,8},{1,17},{9,25},{17,1},{25,9},{2,18},{10... | collective-permute-start | bytes 921608 | tf_op jit(solution)/shard_map/ppermute | solution.py:403
  520.6 50.8 %collective-permute-start.38 = (bf16[2,1,80,960]{3,2,0,1:T(8,128)(2,1)}, bf16[2,1,80,960]{3,2,0,1:T(8,128)(2,1)S(1)}, u32[]{:S(2)}, u32[]{:S(2)}) collective-permute-start(bf16[2,1,80,960]{3,2,0,1:T(8,128)(2,1)} %fusion.34), channel_id=1, source_target_pairs={{0,8},{8,0},{16,24},{24,16},{1,9},{9,1},{17,25},{25,17},{2,10},{10... | collective-permute-start | bytes 921608 | tf_op jit(solution)/shard_map/ppermute | solution.py:400
  527.8 43.6 %collective-permute-start.34 = (bf16[2,2,3,80,960]{4,3,2,1,0:T(8,128)(2,1)S(1)}, bf16[2,2,3,80,960]{4,3,2,1,0:T(8,128)(2,1)S(1)}, u32[]{:S(2)}, u32[]{:S(2)}) collective-permute-start(bf16[2,2,3,80,960]{4,3,2,1,0:T(8,128)(2,1)S(1)} %pad_maximum_fusion.9), channel_id=1, source_target_pairs={{0,16},{8,24},{16,0},{24,8},{1,17},{9,25},{17,1},{25,9},{2,18},{10... | collective-permute-start | bytes 5529608 | tf_op jit(solution)/shard_map/ppermute | solution.py:403
  529.0 43.0 %collective-permute-start.33 = (bf16[2,2,3,80,960]{4,3,2,1,0:T(8,128)(2,1)S(1)}, bf16[2,2,3,80,960]{4,3,2,1,0:T(8,128)(2,1)S(1)}, u32[]{:S(2)}, u32[]{:S(2)}) collective-permute-start(bf16[2,2,3,80,960]{4,3,2,1,0:T(8,128)(2,1)S(1)} %pad_maximum_fusion.8), channel_id=1, source_target_pairs={{0,8},{8,0},{16,24},{24,16},{1,9},{9,1},{17,25},{25,17},{2,10},{10... | collective-permute-start | bytes 5529608 | tf_op jit(solution)/shard_map/ppermute | solution.py:400
  (102 other events, 1565.7 us)

commit v7 on v6

--- a/solution.py
+++ b/solution.py
@@ -681,22 +681,22 @@
             new_move,
         )
     advance(None, ffn_move, attn_move, *last_attn)
-    rest = []
-    for layer in range(1, layers):
-        total = jnp.concatenate([moves[layer][1].finish(), moves[layer][0].finish()])
-        total = settle(total, ffn_move.flying[len(ffn_move.flying) // 2], *attn_move.flying)
-        rest.append(Transfer(quarter_stages(links, total)))
-    advance(None, ffn_move, attn_move, *rest)
-    last = Transfer(quarter_stages(links, ffn_move.finish()))
+    attn_move.flying = settle(attn_move.flying, ffn_move.flying[len(ffn_move.flying) // 2])
+    attn_move.advance()
+    advance(None, ffn_move, attn_move)
+    total = [ffn_move.finish()]
+    for attn, ffn in moves[1:]:
+        total += [ffn.finish(), attn.finish()]
+    last = Transfer(quarter_stages(links, jnp.concatenate(total)))
     advance(None, attn_move, last)
-    done = settle([transfer.finish() for transfer in (last, *rest)], attn_move.flying[0])
+    done = last.finish()
     total = attn_move.finish()
     part = rows[0] + rows[1] + rows[2]
     gains = total[0, part // 4 :][: 2 * layers].astype(jnp.float32).reshape(2, layers, width)
     tail = Transfer(quarter_stages(links, total[:, : part // 4]))
-    shares = [(done[0], tail.finish())]
-    for quarters in done[1:]:
-        shares.append(([q[:3] for q in quarters], [q[3:] for q in quarters]))
+    shares = [([q[:3] for q in done], tail.finish())]
+    for at in range(3, 4 * layers - 1, 4):
+        shares.append(([q[at : at + 3] for q in done], [q[at + 3 : at + 4] for q in done]))
 
     sums = [[] for _ in range(6)]
     for ffn_part, attn_part in shares:

time: 769 us -> 761 us (0.990)
  starting transfers between devices: 93.5 us -> 62.1 us
  local copies, waits for them, and re-layouts: 66.4 us -> 76.4 us
    ppermute x18, starting transfers between devices: 54.5 us -> 27.4 us  [send(): lax.ppermute(value, 'col', [(i, (i + 2 * step) % self.col) for i in range...]
    ppermute x15 -> x14, waiting for transfers between devices: 56.3 us -> 39.8 us  [y(): return lax.ppermute(value, 'dp', [(i, i ^ 2) for i in range(self.dp)])]
    ppermute x3 -> x2, waiting for transfers between devices: 0.01 us -> 15.1 us  [both(): return lax.ppermute(value, 'dp', [(i, i ^ 3) for i in range(self.dp)])]
    ppermute x15 -> x14, waiting for transfers between devices: 22.5 us -> 27.5 us  [x(): return lax.ppermute(value, 'dp', [(i, i ^ 1) for i in range(self.dp)])]
    ppermute x15 -> x14, starting transfers between devices: 17.1 us -> 13.3 us  [x(): return lax.ppermute(value, 'dp', [(i, i ^ 1) for i in range(self.dp)])]
    unnamed x129 -> x145, local copies, waits for them, and re-layouts: 24.8 us -> 26.6 us
    ppermute x15 -> x14, starting transfers between devices: 15.8 us -> 16.4 us  [y(): return lax.ppermute(value, 'dp', [(i, i ^ 2) for i in range(self.dp)])]
    convert_element_type x18 -> x13, other arithmetic: 41.8 us -> 41.5 us  [add(): return total.astype(jnp.bfloat16)]
  transfers between devices with their start and end apart: 65 -> 62, of which waited for: 24 -> 26; matrix products, arithmetic and copies ran while one was open for 12% -> 13% of each run, Pallas kernels for 27% -> 28%
where the time goes in v7:
time: 761 us; the launch traced here: 752 us
  Pallas kernels  284 us (37%)
  waiting for transfers between devices  244 us (32%)
  other arithmetic  83.5 us (11%)
  local copies, waits for them, and re-layouts  76.4 us (10%)
  starting transfers between devices  62.1 us (8%)
    pallas_call x12, Pallas kernels, call(): pl.pallas_call(run, out_shape=outs, in_specs=list(specs) + [pl.BlockSpec(...  284 us
    ppermute x18, waiting for transfers between devices, send(): lax.ppermute(value, 'col', [(i, (i + 2 * step) % self.col) for i in range...  159 us
    convert_element_type x13, other arithmetic, add(): return total.astype(jnp.bfloat16)  41.5 us
    ppermute x14, waiting for transfers between devices, y(): return lax.ppermute(value, 'dp', [(i, i ^ 2) for i in range(self.dp)])  39.8 us
    ppermute x14, waiting for transfers between devices, x(): return lax.ppermute(value, 'dp', [(i, i ^ 1) for i in range(self.dp)])  27.5 us
    ppermute x18, starting transfers between devices, send(): lax.ppermute(value, 'col', [(i, (i + 2 * step) % self.col) for i in range...  27.4 us
    unnamed x145, local copies, waits for them, and re-layouts  26.6 us
    ppermute x14, starting transfers between devices, y(): return lax.ppermute(value, 'dp', [(i, i ^ 2) for i in range(self.dp)])  16.4 us
  transfers between devices with their start and end apart: 62, of which 26 were waited for; matrix products, arithmetic and copies ran while one was open for 13% of the time, Pallas kernels for 28%

profile of v7, /device:TPU:0, one launch (start us, length us, event | category | flops | bytes accessed | tf_op | source)
XLA Modules:
  0.0 752.2 jit_solution(14060417841884025829)
XLA Ops:
  14.8 14.0 %collective-permute-done = bf16[4,80,960]{2,1,0:T(8,128)(2,1)S(1)} collective-permute-done((bf16[4,80,960]{2,1,0:T(8,128)(2,1)S(1)}, bf16[4,80,960]{2,1,0:T(8,128)(2,1)S(1)}, u32[]{:S(2)}, u32[]{:S(2)}) %collective-permute-start) | collective-permute-done | bytes 614432 | tf_op jit(solution)/shard_map/ppermute | solution.py:412
  28.9 40.8 %collective-permute-done.1 = bf16[4,80,960]{2,1,0:T(8,128)(2,1)S(1)} collective-permute-done((bf16[4,80,960]{2,1,0:T(8,128)(2,1)S(1)}, bf16[4,80,960]{2,1,0:T(8,128)(2,1)S(1)}, u32[]{:S(2)}, u32[]{:S(2)}) %collective-permute-start.1) | collective-permute-done | bytes 614432 | tf_op jit(solution)/shard_map/ppermute | solution.py:412
  78.0 10.8 %collective-permute-done.5 = bf16[4,80,960]{2,1,0:T(8,128)(2,1)S(1)} collective-permute-done((bf16[4,80,960]{2,1,0:T(8,128)(2,1)S(1)}, bf16[4,80,960]{2,1,0:T(8,128)(2,1)S(1)}, u32[]{:S(2)}, u32[]{:S(2)}) %collective-permute-start.5) | collective-permute-done | bytes 614432 | tf_op jit(solution)/shard_map/ppermute | solution.py:412
  88.7 42.9 %collective-permute-done.6 = bf16[4,80,960]{2,1,0:T(8,128)(2,1)S(1)} collective-permute-done((bf16[4,80,960]{2,1,0:T(8,128)(2,1)S(1)}, bf16[4,80,960]{2,1,0:T(8,128)(2,1)S(1)}, u32[]{:S(2)}, u32[]{:S(2)}) %collective-permute-start.6) | collective-permute-done | bytes 614432 | tf_op jit(solution)/shard_map/ppermute | solution.py:412
  144.8 24.4 %collective-permute-done.8.refs_3_.refs_5_.refs_8_ = bf16[2,4,80,960]{3,2,1,0:T(8,128)(2,1)} collective-permute-done((bf16[2,4,80,960]{3,2,1,0:T(8,128)(2,1)}, bf16[2,4,80,960]{3,2,1,0:T(8,128)(2,1)}, u32[]{:S(2)}, u32[]{:S(2)}) %collective-permute-start.8) | collective-permute-done | bytes 1228832 | tf_op jit(solution)/shard_map/ppermute | solution.py:403
  189.6 28.8 %shard_map.187 = (bf16[768,960]{1,0:T(8,128)(2,1)}, bf16[768,1600]{1,0:T(8,128)(2,1)}, bf16[768,960]{1,0:T(8,128)(2,1)}, f32[16,768]{1,0:T(8,128)}, f32[768,960]{1,0:T(8,128)}, /*index=5*/bf16[768,960]{1,0:T(8,128)(2,1)}) custom-call(f32[768,960]{1,0:T(8,128)} %bitcast_convert_fusion.refs_0_.refs_2_, f32[1,960]{1,0:T(1,128)} %get-tuple-element.387.refs_1_.refs_8_, ...), custom_call_target="tpu_custom_call" | custom-call | flops 20000000000 | bytes 20971520 | tf_op jit(solution)/shard_map/pallas_call | solution.py:54
  218.4 20.1 %collective-permute-done.15.refs_1_.refs_3_.refs_6_ = bf16[4,4,80,960]{3,2,1,0:T(8,128)(2,1)} collective-permute-done((bf16[4,4,80,960]{3,2,1,0:T(8,128)(2,1)S(1)}, bf16[4,4,80,960]{3,2,1,0:T(8,128)(2,1)}, u32[]{:S(2)}, u32[]{:S(2)}) %collective-permute-start.15) | collective-permute-done | bytes 2457632 | tf_op jit(solution)/shard_map/ppermute | solution.py:400
  246.3 22.0 %shard_map.188 = (f32[768,960]{1,0:T(8,128)}, bf16[768,1280]{1,0:T(8,128)(2,1)}, bf16[768,1280]{1,0:T(8,128)(2,1)}, bf16[768,1280]{1,0:T(8,128)(2,1)}, bf16[768,1280]{1,0:T(8,128)(2,1)}) custom-call(f32[768,960]{1,0:T(8,128)} %get-tuple-element.143.refs_0_.refs_7_, bf16[768,960]{1,0:T(8,128)(2,1)} %get-tuple-element.148.refs_1_, ...), custom_call_target="tpu_custom_call" | custom-call | flops 11000000512 | bytes 31457280 | tf_op jit(solution)/shard_map/pallas_call | solution.py:54
  268.3 6.0 collective-permute-done.17.refs_3_.refs_5_.refs_8_
  288.4 28.8 %shard_map.190 = (bf16[768,960]{1,0:T(8,128)(2,1)}, bf16[768,1600]{1,0:T(8,128)(2,1)}, bf16[768,960]{1,0:T(8,128)(2,1)}, f32[16,768]{1,0:T(8,128)}, f32[768,960]{1,0:T(8,128)}, /*index=5*/bf16[768,960]{1,0:T(8,128)(2,1)}) custom-call(f32[768,960]{1,0:T(8,128)} %get-tuple-element.152.refs_0_.refs_2_, f32[1,960]{1,0:T(1,128)} %get-tuple-element.388.refs_1_.refs_8_, ...), custom_call_target="tpu_custom_call" | custom-call | flops 20000000000 | bytes 20971520 | tf_op jit(solution)/shard_map/pallas_call | solution.py:54
  317.2 22.2 %shard_map.191 = (f32[768,960]{1,0:T(8,128)}, bf16[768,1280]{1,0:T(8,128)(2,1)}, bf16[768,1280]{1,0:T(8,128)(2,1)}, bf16[768,1280]{1,0:T(8,128)(2,1)}, bf16[768,1280]{1,0:T(8,128)(2,1)}) custom-call(f32[768,960]{1,0:T(8,128)} %get-tuple-element.158.refs_0_.refs_7_, bf16[768,960]{1,0:T(8,128)(2,1)} %get-tuple-element.159.refs_1_, ...), custom_call_target="tpu_custom_call" | custom-call | flops 11000000512 | bytes 31457280 | tf_op jit(solution)/shard_map/pallas_call | solution.py:54
  339.5 22.0 %shard_map.192 = (bf16[16,3,80,960]{3,2,1,0:T(8,128)(2,1)}, f32[768,960]{1,0:T(8,128)}) custom-call(bf16[768,960]{1,0:T(8,128)(2,1)} %bitcast.440, bf16[768,960]{1,0:T(8,128)(2,1)} %get-tuple-element.159.refs_1_, bf16[768,1280]{1,0:T(8,128)(2,1)} %get-tuple-element.163.refs_2_, bf16[768,1280]{1,0:T(8,128)(2,1)} %get-tuple-element.164.refs_3_, ...), custom_call_target="tpu_custom_call" | custom-call | flops 11000000512 | bytes 31457280 | tf_op jit(solution)/shard_map/pallas_call | solution.py:54
  363.7 23.2 %shard_map.193 = (bf16[16,3,80,960]{3,2,1,0:T(8,128)(2,1)}, f32[768,960]{1,0:T(8,128)}) custom-call(bf16[768,960]{1,0:T(8,128)(2,1)} %bitcast.441, bf16[768,960]{1,0:T(8,128)(2,1)} %get-tuple-element.159.refs_1_, bf16[768,1280]{1,0:T(8,128)(2,1)} %get-tuple-element.161.refs_2_, bf16[768,1280]{1,0:T(8,128)(2,1)} %get-tuple-element.162.refs_3_, ...), custom_call_target="tpu_custom_call" | custom-call | flops 11000000512 | bytes 31457280 | tf_op jit(solution)/shard_map/pallas_call | solution.py:54
  386.9 5.5 add_convert_fusion.9
  395.0 42.2 %shard_map.194 = (bf16[1600,960]{1,0:T(8,128)(2,1)}, bf16[960,960]{1,0:T(8,128)(2,1)}, f32[768,960]{1,0:T(8,128)}, bf16[768,960]{1,0:T(8,128)(2,1)}, f32[1,960]{1,0:T(1,128)}, /*index=5*/f32[1,960]{1,0:T(1,128)}) custom-call(f32[768,960]{1,0:T(8,128)} %bitcast_convert_fusion.3.refs_0_, f32[768,960]{1,0:T(8,128)} %get-tuple-element.169.refs_1_, ...), custom_call_target="tpu_custom_call" | custom-call | flops 35000000512 | bytes 41943040 | tf_op jit(solution)/shard_map/pallas_call | solution.py:54
  455.8 22.1 %shard_map.195 = (bf16[16,3,80,960]{3,2,1,0:T(8,128)(2,1)}, f32[768,960]{1,0:T(8,128)}) custom-call(bf16[768,960]{1,0:T(8,128)(2,1)} %get-tuple-element.183.refs_0_, bf16[768,960]{1,0:T(8,128)(2,1)} %get-tuple-element.148.refs_1_, bf16[768,1280]{1,0:T(8,128)(2,1)} %get-tuple-element.186.refs_2_, bf16[768,1280]{1,0:T(8,128)(2,1)} %get-tuple-element.187.refs_3_, ...), custom_call_target="tpu_custom_call" | custom-call | flops 11000000512 | bytes 31457280 | tf_op jit(solution)/shard_map/pallas_call | solution.py:54
  490.2 23.0 %shard_map.196 = (bf16[16,3,80,960]{3,2,1,0:T(8,128)(2,1)}, f32[768,960]{1,0:T(8,128)}) custom-call(bf16[768,960]{1,0:T(8,128)(2,1)} %get-tuple-element.183.refs_0_, bf16[768,960]{1,0:T(8,128)(2,1)} %get-tuple-element.148.refs_1_, bf16[768,1280]{1,0:T(8,128)(2,1)} %get-tuple-element.184.refs_2_, bf16[768,1280]{1,0:T(8,128)(2,1)} %get-tuple-element.185.refs_3_, ...), custom_call_target="tpu_custom_call" | custom-call | flops 11000000512 | bytes 31457280 | tf_op jit(solution)/shard_map/pallas_call | solution.py:54
  528.1 41.8 %shard_map.197 = (bf16[1600,960]{1,0:T(8,128)(2,1)}, bf16[960,960]{1,0:T(8,128)(2,1)}, f32[768,960]{1,0:T(8,128)}, bf16[768,960]{1,0:T(8,128)(2,1)}, f32[1,960]{1,0:T(1,128)}, /*index=5*/f32[1,960]{1,0:T(1,128)}) custom-call(f32[768,960]{1,0:T(8,128)} %get-tuple-element.182.refs_0_, f32[768,960]{1,0:T(8,128)} %get-tuple-element.199.refs_1_, ...), custom_call_target="tpu_custom_call" | custom-call | flops 35000000512 | bytes 41943040 | tf_op jit(solution)/shard_map/pallas_call | solution.py:54
  594.5 7.8 %collective-permute-start.43 = (bf16[1,80,960]{2,1,0:T(8,128)(2,1)S(1)}, bf16[1,80,960]{2,1,0:T(8,128)(2,1)S(1)}, u32[]{:S(2)}, u32[]{:S(2)}) collective-permute-start(bf16[1,80,960]{2,1,0:T(8,128)(2,1)S(1)} %get-tuple-element.366), channel_id=1, source_target_pairs={{0,2},{1,3},{2,4},{3,5},{4,6},{5,7},{6,0},{7,1},{8,10},{9,11},{10,... | collective-permute-start | bytes 460808 | tf_op jit(solution)/shard_map/ppermute | solution.py:412
  625.4 5.5 fusion.4
  639.2 29.2 %collective-permute-done.48 = bf16[3,80,960]{2,1,0:T(8,128)(2,1)} collective-permute-done((bf16[3,80,960]{2,1,0:T(8,128)(2,1)}, bf16[3,80,960]{2,1,0:T(8,128)(2,1)}, u32[]{:S(2)}, u32[]{:S(2)}) %collective-permute-start.48) | collective-permute-done | bytes 460832 | tf_op jit(solution)/shard_map/ppermute | solution.py:412
  675.7 6.4 collective-permute-done.52
  695.2 7.6 %collective-permute-done.53 = bf16[1,96,960]{2,1,0:T(8,128)(2,1)S(1)} collective-permute-done((bf16[1,96,960]{2,1,0:T(8,128)(2,1)S(1)}, bf16[1,96,960]{2,1,0:T(8,128)(2,1)S(1)}, u32[]{:S(2)}, u32[]{:S(2)}) %collective-permute-start.53) | collective-permute-done | bytes 184352 | tf_op jit(solution)/shard_map/ppermute | solution.py:412
  713.8 15.1 %collective-permute-done.58 = bf16[7,80,960]{2,1,0:T(8,128)(2,1)} collective-permute-done((bf16[7,80,960]{2,1,0:T(8,128)(2,1)}, bf16[7,80,960]{2,1,0:T(8,128)(2,1)}, u32[]{:S(2)}, u32[]{:S(2)}) %collective-permute-start.58) | collective-permute-done | bytes 1075232 | tf_op jit(solution)/shard_map/ppermute | solution.py:409
  (381 shorter events, 237.4 us)
Async XLA Ops:
  13.7 56.0 %collective-permute-start.1 = (bf16[4,80,960]{2,1,0:T(8,128)(2,1)S(1)}, bf16[4,80,960]{2,1,0:T(8,128)(2,1)S(1)}, u32[]{:S(2)}, u32[]{:S(2)}) collective-permute-start(bf16[4,80,960]{2,1,0:T(8,128)(2,1)S(1)} %get-tuple-element.369), channel_id=1, source_target_pairs={{0,4},{1,5},{2,6},{3,7},{4,0},{5,1},{6,2},{7,3},{8,12},{9,13},{10,... | collective-permute-start | bytes 1843208 | tf_op jit(solution)/shard_map/ppermute | solution.py:412
  13.7 56.0 %collective-permute-start.2 = (bf16[4,80,960]{2,1,0:T(8,128)(2,1)S(1)}, bf16[4,80,960]{2,1,0:T(8,128)(2,1)S(1)}, u32[]{:S(2)}, u32[]{:S(2)}) collective-permute-start(bf16[4,80,960]{2,1,0:T(8,128)(2,1)S(1)} %get-tuple-element.369), channel_id=1, source_target_pairs={{0,2},{1,3},{2,4},{3,5},{4,6},{5,7},{6,0},{7,1},{8,10},{9,11},{10,... | collective-permute-start | bytes 1843208 | tf_op jit(solution)/shard_map/ppermute | solution.py:412
  70.1 61.6 %collective-permute-start.3 = (bf16[4,4,80,960]{3,2,1,0:T(8,128)(2,1)S(1)}, bf16[4,4,80,960]{3,2,1,0:T(8,128)(2,1)}, u32[]{:S(2)}, u32[]{:S(2)}) collective-permute-start(bf16[4,4,80,960]{3,2,1,0:T(8,128)(2,1)S(1)} %pad_maximum_fusion.4.refs_0_.refs_2_.refs_5_), channel_id=1, source_target_pairs={{0,8},{8,0},{16,24},{24,16},{1,9},{9,1},{17,25},{25,17},{2,10},{10... | collective-permute-start | bytes 7372808 | tf_op jit(solution)/shard_map/ppermute | solution.py:400
  71.6 60.0 %collective-permute-start.4 = (bf16[4,4,80,960]{3,2,1,0:T(8,128)(2,1)S(1)}, bf16[4,4,80,960]{3,2,1,0:T(8,128)(2,1)}, u32[]{:S(2)}, u32[]{:S(2)}) collective-permute-start(bf16[4,4,80,960]{3,2,1,0:T(8,128)(2,1)S(1)} %pad_maximum_fusion.4.refs_0_.refs_2_.refs_5_), channel_id=1, source_target_pairs={{0,16},{8,24},{16,0},{24,8},{1,17},{9,25},{17,1},{25,9},{2,18},{10... | collective-permute-start | bytes 7372808 | tf_op jit(solution)/shard_map/ppermute | solution.py:403
  73.1 58.5 %collective-permute-start.6 = (bf16[4,80,960]{2,1,0:T(8,128)(2,1)S(1)}, bf16[4,80,960]{2,1,0:T(8,128)(2,1)S(1)}, u32[]{:S(2)}, u32[]{:S(2)}) collective-permute-start(bf16[4,80,960]{2,1,0:T(8,128)(2,1)S(1)} %pad_maximum_fusion.18), channel_id=1, source_target_pairs={{0,4},{1,5},{2,6},{3,7},{4,0},{5,1},{6,2},{7,3},{8,12},{9,13},{10,... | collective-permute-start | bytes 1843208 | tf_op jit(solution)/shard_map/ppermute | solution.py:412
  75.9 55.7 %collective-permute-start.7 = (bf16[4,80,960]{2,1,0:T(8,128)(2,1)S(1)}, bf16[4,80,960]{2,1,0:T(8,128)(2,1)S(1)}, u32[]{:S(2)}, u32[]{:S(2)}) collective-permute-start(bf16[4,80,960]{2,1,0:T(8,128)(2,1)S(1)} %pad_maximum_fusion.18), channel_id=1, source_target_pairs={{0,2},{1,3},{2,4},{3,5},{4,6},{5,7},{6,0},{7,1},{8,10},{9,11},{10,... | collective-permute-start | bytes 1843208 | tf_op jit(solution)/shard_map/ppermute | solution.py:412
  88.7 56.0 %collective-permute-start.10 = (bf16[4,4,80,960]{3,2,1,0:T(8,128)(2,1)S(1)}, bf16[4,4,80,960]{3,2,1,0:T(8,128)(2,1)}, u32[]{:S(2)}, u32[]{:S(2)}) collective-permute-start(bf16[4,4,80,960]{3,2,1,0:T(8,128)(2,1)S(1)} %pad_maximum_fusion.4.refs_0_.refs_2_.refs_5_), channel_id=1, source_target_pairs={{0,1},{1,0},{2,3},{3,2},{4,5},{5,4},{6,7},{7,6},{8,9},{9,8},{10,11... | collective-permute-start | bytes 7372808 | tf_op jit(solution)/shard_map/ppermute | solution.py:406
  131.7 37.7 %collective-permute-start.11 = (bf16[4,4,80,960]{3,2,1,0:T(8,128)(2,1)}, bf16[4,4,80,960]{3,2,1,0:T(8,128)(2,1)}, u32[]{:S(2)}, u32[]{:S(2)}) collective-permute-start(bf16[4,4,80,960]{3,2,1,0:T(8,128)(2,1)} %collective-permute-done.3.refs_1_.refs_3_.refs_6_), channel_id=1, source_target_pairs={{0,1},{1,0},{2,3},{3,2},{4,5},{5,4},{6,7},{7,6},{8,9},{9,8},{10,11... | collective-permute-start | bytes 7372808 | tf_op jit(solution)/shard_map/ppermute | solution.py:406
  179.5 59.0 %collective-permute-start.15 = (bf16[4,4,80,960]{3,2,1,0:T(8,128)(2,1)S(1)}, bf16[4,4,80,960]{3,2,1,0:T(8,128)(2,1)}, u32[]{:S(2)}, u32[]{:S(2)}) collective-permute-start(bf16[4,4,80,960]{3,2,1,0:T(8,128)(2,1)S(1)} %pad_maximum_fusion.5.refs_0_.refs_2_.refs_5_), channel_id=1, source_target_pairs={{0,8},{8,0},{16,24},{24,16},{1,9},{9,1},{17,25},{25,17},{2,10},{10... | collective-permute-start | bytes 7372808 | tf_op jit(solution)/shard_map/ppermute | solution.py:400
  180.1 58.7 %collective-permute-start.16 = (bf16[4,4,80,960]{3,2,1,0:T(8,128)(2,1)S(1)}, bf16[4,4,80,960]{3,2,1,0:T(8,128)(2,1)}, u32[]{:S(2)}, u32[]{:S(2)}) collective-permute-start(bf16[4,4,80,960]{3,2,1,0:T(8,128)(2,1)S(1)} %pad_maximum_fusion.5.refs_0_.refs_2_.refs_5_), channel_id=1, source_target_pairs={{0,16},{8,24},{16,0},{24,8},{1,17},{9,25},{17,1},{25,9},{2,18},{10... | collective-permute-start | bytes 7372808 | tf_op jit(solution)/shard_map/ppermute | solution.py:403
  181.7 86.6 %collective-permute-start.19 = (bf16[4,4,80,960]{3,2,1,0:T(8,128)(2,1)S(1)}, bf16[4,4,80,960]{3,2,1,0:T(8,128)(2,1)}, u32[]{:S(2)}, u32[]{:S(2)}) collective-permute-start(bf16[4,4,80,960]{3,2,1,0:T(8,128)(2,1)S(1)} %pad_maximum_fusion.5.refs_0_.refs_2_.refs_5_), channel_id=1, source_target_pairs={{0,1},{1,0},{2,3},{3,2},{4,5},{5,4},{6,7},{7,6},{8,9},{9,8},{10,11... | collective-permute-start | bytes 7372808 | tf_op jit(solution)/shard_map/ppermute | solution.py:406
  392.6 45.2 %collective-permute-start.26 = (bf16[2,2,3,80,960]{4,3,2,1,0:T(8,128)(2,1)S(1)}, bf16[2,2,3,80,960]{4,3,2,1,0:T(8,128)(2,1)S(1)}, u32[]{:S(2)}, u32[]{:S(2)}) collective-permute-start(bf16[2,2,3,80,960]{4,3,2,1,0:T(8,128)(2,1)S(1)} %pad_maximum_fusion.7), channel_id=1, source_target_pairs={{0,16},{8,24},{16,0},{24,8},{1,17},{9,25},{17,1},{25,9},{2,18},{10... | collective-permute-start | bytes 5529608 | tf_op jit(solution)/shard_map/ppermute | solution.py:403
  393.4 44.9 %collective-permute-start.25 = (bf16[2,2,3,80,960]{4,3,2,1,0:T(8,128)(2,1)S(1)}, bf16[2,2,3,80,960]{4,3,2,1,0:T(8,128)(2,1)S(1)}, u32[]{:S(2)}, u32[]{:S(2)}) collective-permute-start(bf16[2,2,3,80,960]{4,3,2,1,0:T(8,128)(2,1)S(1)} %pad_maximum_fusion.6), channel_id=1, source_target_pairs={{0,8},{8,0},{16,24},{24,16},{1,9},{9,1},{17,25},{25,17},{2,10},{10... | collective-permute-start | bytes 5529608 | tf_op jit(solution)/shard_map/ppermute | solution.py:400
  489.3 37.0 %collective-permute-start.36 = (bf16[3,80,960]{2,1,0:T(8,128)(2,1)}, bf16[3,80,960]{2,1,0:T(8,128)(2,1)}, u32[]{:S(2)}, u32[]{:S(2)}) collective-permute-start(bf16[3,80,960]{2,1,0:T(8,128)(2,1)} %get-tuple-element.361), channel_id=1, source_target_pairs={{0,4},{1,5},{2,6},{3,7},{4,0},{5,1},{6,2},{7,3},{8,12},{9,13},{10,... | collective-permute-start | bytes 1382408 | tf_op jit(solution)/shard_map/ppermute | solution.py:412
  489.6 37.9 %collective-permute-start.37 = (bf16[3,80,960]{2,1,0:T(8,128)(2,1)}, bf16[3,80,960]{2,1,0:T(8,128)(2,1)}, u32[]{:S(2)}, u32[]{:S(2)}) collective-permute-start(bf16[3,80,960]{2,1,0:T(8,128)(2,1)} %get-tuple-element.360), channel_id=1, source_target_pairs={{0,6},{1,7},{2,0},{3,1},{4,2},{5,3},{6,4},{7,5},{8,14},{9,15},{10,... | collective-permute-start | bytes 1382408 | tf_op jit(solution)/shard_map/ppermute | solution.py:412
  514.1 55.8 %collective-permute-start.35 = (bf16[3,80,960]{2,1,0:T(8,128)(2,1)}, bf16[3,80,960]{2,1,0:T(8,128)(2,1)}, u32[]{:S(2)}, u32[]{:S(2)}) collective-permute-start(bf16[3,80,960]{2,1,0:T(8,128)(2,1)} %slice_bitcast_fusion.11), channel_id=1, source_target_pairs={{0,2},{1,3},{2,4},{3,5},{4,6},{5,7},{6,0},{7,1},{8,10},{9,11},{10,... | collective-permute-start | bytes 1382408 | tf_op jit(solution)/shard_map/ppermute | solution.py:412
  518.2 51.7 %collective-permute-start.38 = (bf16[2,1,80,960]{3,2,0,1:T(8,128)(2,1)}, bf16[2,1,80,960]{3,2,0,1:T(8,128)(2,1)S(1)}, u32[]{:S(2)}, u32[]{:S(2)}) collective-permute-start(bf16[2,1,80,960]{3,2,0,1:T(8,128)(2,1)} %get-tuple-element.319), channel_id=1, source_target_pairs={{0,8},{8,0},{16,24},{24,16},{1,9},{9,1},{17,25},{25,17},{2,10},{10... | collective-permute-start | bytes 921608 | tf_op jit(solution)/shard_map/ppermute | solution.py:400
  519.7 50.2 %collective-permute-start.39 = (bf16[2,1,80,960]{3,2,0,1:T(8,128)(2,1)}, bf16[2,1,80,960]{3,2,0,1:T(8,128)(2,1)}, u32[]{:S(2)}, u32[]{:S(2)}) collective-permute-start(bf16[2,1,80,960]{3,2,0,1:T(8,128)(2,1)} %get-tuple-element.318), channel_id=1, source_target_pairs={{0,16},{8,24},{16,0},{24,8},{1,17},{9,25},{17,1},{25,9},{2,18},{10... | collective-permute-start | bytes 921608 | tf_op jit(solution)/shard_map/ppermute | solution.py:403
  526.3 44.2 %collective-permute-start.34 = (bf16[2,2,3,80,960]{4,3,2,1,0:T(8,128)(2,1)S(1)}, bf16[2,2,3,80,960]{4,3,2,1,0:T(8,128)(2,1)S(1)}, u32[]{:S(2)}, u32[]{:S(2)}) collective-permute-start(bf16[2,2,3,80,960]{4,3,2,1,0:T(8,128)(2,1)S(1)} %pad_maximum_fusion.9), channel_id=1, source_target_pairs={{0,16},{8,24},{16,0},{24,8},{1,17},{9,25},{17,1},{25,9},{2,18},{10... | collective-permute-start | bytes 5529608 | tf_op jit(solution)/shard_map/ppermute | solution.py:403
  527.5 43.0 %collective-permute-start.33 = (bf16[2,2,3,80,960]{4,3,2,1,0:T(8,128)(2,1)S(1)}, bf16[2,2,3,80,960]{4,3,2,1,0:T(8,128)(2,1)S(1)}, u32[]{:S(2)}, u32[]{:S(2)}) collective-permute-start(bf16[2,2,3,80,960]{4,3,2,1,0:T(8,128)(2,1)S(1)} %pad_maximum_fusion.8), channel_id=1, source_target_pairs={{0,8},{8,0},{16,24},{24,16},{1,9},{9,1},{17,25},{25,17},{2,10},{10... | collective-permute-start | bytes 5529608 | tf_op jit(solution)/shard_map/ppermute | solution.py:400
  621.6 46.8 %collective-permute-start.47 = (bf16[2,2,1,96,960]{4,3,1,2,0:T(8,128)(2,1)}, bf16[2,2,1,96,960]{4,3,1,2,0:T(8,128)(2,1)}, u32[]{:S(2)}, u32[]{:S(2)}) collective-permute-start(bf16[2,2,1,96,960]{4,3,1,2,0:T(8,128)(2,1)} %pad_maximum_fusion.14), channel_id=1, source_target_pairs={{0,16},{8,24},{16,0},{24,8},{1,17},{9,25},{17,1},{25,9},{2,18},{10... | collective-permute-start | bytes 2211848 | tf_op jit(solution)/shard_map/ppermute | solution.py:403
  624.3 44.2 %collective-permute-start.46 = (bf16[2,2,1,96,960]{4,3,1,2,0:T(8,128)(2,1)}, bf16[2,2,1,96,960]{4,3,1,2,0:T(8,128)(2,1)}, u32[]{:S(2)}, u32[]{:S(2)}) collective-permute-start(bf16[2,2,1,96,960]{4,3,1,2,0:T(8,128)(2,1)} %pad_maximum_fusion.13), channel_id=1, source_target_pairs={{0,8},{8,0},{16,24},{24,16},{1,9},{9,1},{17,25},{25,17},{2,10},{10... | collective-permute-start | bytes 2211848 | tf_op jit(solution)/shard_map/ppermute | solution.py:400
  635.9 39.8 %collective-permute-start.50 = (bf16[3,80,960]{2,1,0:T(8,128)(2,1)}, bf16[3,80,960]{2,1,0:T(8,128)(2,1)S(1)}, u32[]{:S(2)}, u32[]{:S(2)}) collective-permute-start(bf16[3,80,960]{2,1,0:T(8,128)(2,1)} %get-tuple-element.358), channel_id=1, source_target_pairs={{0,6},{1,7},{2,0},{3,1},{4,2},{5,3},{6,4},{7,5},{8,14},{9,15},{10,... | collective-permute-start | bytes 1382408 | tf_op jit(solution)/shard_map/ppermute | solution.py:412
  689.5 39.4 %collective-permute-start.58 = (bf16[7,80,960]{2,1,0:T(8,128)(2,1)}, bf16[7,80,960]{2,1,0:T(8,128)(2,1)}, u32[]{:S(2)}, u32[]{:S(2)}) collective-permute-start(bf16[7,80,960]{2,1,0:T(8,128)(2,1)} %pad_maximum_fusion.10), channel_id=1, source_target_pairs={{0,24},{8,16},{16,8},{24,0},{1,25},{9,17},{17,9},{25,1},{2,26},{10... | collective-permute-start | bytes 3225608 | tf_op jit(solution)/shard_map/ppermute | solution.py:409
  (107 other events, 1666.9 us)
